TPU v7x, 256 devices: a whole 4x4x8 slice. The times are simulated.
256 devices in a mesh: shard: 64 (over x, z, core), rep: 4 (over y).
Axes of the slice: x: 4, y: 4, z: 8, core: 2. Of those that a mesh axis runs over, the one named last changes fastest.
Arguments:
- embeddings: float32 [196608, 1024], P('shard'), may hold values from -6 to 6
- labels: int32 [196608], replicated, may hold values from 0 to 191, never falling along the last dimension, each value on 1 to 4096 neighbouring positions
- holder: int32 [13056, 1], P('shard'), may hold values from 0 to 4; in each aligned block of 204 rows (0 to 203, 204 to 407, ...) at most 61 rows name the same one
Outputs:
- best: float32 [196608], P('shard')
Inputs may be any that keep to these rules, and one draw needn't show every extreme that they name: `labels`: labels never fall along the documents; every cluster has 1 to 4096 documents and one has exactly 4096. `holder`: among the 204 rows of one index of shard, at most 61 name any one value, a bound that some of them reach.
All inputs are finite; a program needn't handle non-finite values.
Results may differ from a plain program's by a relative error of at most 0.0012.
Values may be sent and summed in bfloat16 or wider, within the bound.
No kernel may reach another device: no remote copies, remote signals or barrier semaphores. Data moves between devices by JAX's collectives and lax.ppermute only.
A program may use at most 128 MiB of HBM per device.

v0:
```python
import jax
import jax.numpy as jnp
from jax import lax
from jax.sharding import PartitionSpec as P

BLOCK = 256
SPANS = 17
PCAP = 61


epsilon = 1e-06
group_width = 8


def passed_along(value, axis, steps):
    count = lax.axis_size(axis)
    leading, last = (max(0, -steps), min(count, count - steps))
    return lax.ppermute(value, axis, [(source, source + steps) for source in range(leading, last)])


def shards(embeddings, labels, holder):
    row_count = embeddings.shape[0]
    width = embeddings.shape[1]
    block_count = row_count // BLOCK
    neighbors = (SPANS - 1 + block_count - 1) // block_count
    reached = [
        min(block_count, SPANS - 1 - (distance - 1) * block_count)
        for distance in range(1, neighbors + 1)
    ]
    squares = jnp.sum(embeddings * embeddings, axis=1, keepdims=True)
    unit = (embeddings / jnp.sqrt(squares + epsilon)).astype(jnp.bfloat16)
    pieces = [unit]
    for distance in range(1, neighbors + 1):
        pieces.append(passed_along(unit, "shard", -distance))
    window = jnp.concatenate(pieces, axis=0)
    window = window.reshape(-1, BLOCK, width)
    total = window.shape[0]
    shard_pos = lax.axis_index("shard")
    tags_padded = jnp.concatenate(
        [labels + 1, jnp.zeros((neighbors * row_count,), jnp.int32)], axis=0
    )
    window_tags = lax.dynamic_slice_in_dim(tags_padded, shard_pos * row_count, total * BLOCK, 0)
    window_tags = window_tags.reshape(total, BLOCK)
    replica = lax.axis_index("rep")
    owners = holder[:, 0]
    pair_count = owners.shape[0]
    slot_total = (PCAP + group_width - 1) // group_width * group_width
    chosen = (owners == replica).astype(jnp.int32)
    slot_of = jnp.cumsum(chosen) - 1
    table = chosen[:, None] * (
        slot_of[:, None] == jnp.arange(slot_total, dtype=jnp.int32)[None, :]
    ).astype(jnp.int32)
    pair_ids = jnp.sum(table * jnp.arange(pair_count, dtype=jnp.int32)[:, None], axis=0)
    filled = jnp.sum(table, axis=0) > 0
    first_block = pair_ids // SPANS
    offsets = pair_ids % SPANS
    second_block = first_block + offsets
    group_count = slot_total // group_width
    first_groups = first_block.reshape(group_count, group_width)
    second_groups = second_block.reshape(group_count, group_width)
    offset_groups = offsets.reshape(group_count, group_width)
    filled_groups = filled.reshape(group_count, group_width)
    diagonal = jnp.eye(BLOCK, dtype=jnp.bool_)
    block_ids = jnp.arange(total, dtype=jnp.int32)

    def select_rows(hits):
        picker = hits.astype(jnp.bfloat16)
        chosen_rows = jnp.einsum("pt,tid->pid", picker, window, preferred_element_type=jnp.float32)
        return chosen_rows.astype(jnp.bfloat16)

    def select_tags(hits):
        return jnp.sum(jnp.where(hits[:, :, None], window_tags[None], 0), axis=1)

    def compare(running, operands):
        first_now, second_now, offset_now, filled_now = operands
        first_hits = first_now[:, None] == block_ids[None, :]
        second_hits = second_now[:, None] == block_ids[None, :]
        left_rows = select_rows(first_hits)
        right_rows = select_rows(second_hits)
        similarity = jnp.einsum(
            "pid,pjd->pij", left_rows, right_rows, preferred_element_type=jnp.float32
        )
        left_tags = select_tags(first_hits)
        right_tags = select_tags(second_hits)
        allowed = (left_tags[:, :, None] == right_tags[:, None, :]) & filled_now[:, None, None]
        allowed = allowed & jnp.logical_not((offset_now == 0)[:, None, None] & diagonal[None])
        scored = jnp.where(allowed, similarity, jnp.float32(-1.0))
        row_best = jnp.max(scored, axis=2)
        column_best = jnp.max(scored, axis=1)
        from_rows = jnp.max(
            jnp.where(first_hits[:, :, None], row_best[:, None, :], jnp.float32(-1.0)), axis=0
        )
        from_columns = jnp.max(
            jnp.where(second_hits[:, :, None], column_best[:, None, :], jnp.float32(-1.0)), axis=0
        )
        return (jnp.maximum(running, jnp.maximum(from_rows, from_columns)), None)

    initial = jnp.full((total, BLOCK), -1.0, jnp.float32)
    window_best, unused = lax.scan(
        compare, initial, (first_groups, second_groups, offset_groups, filled_groups)
    )
    result = window_best[:block_count]
    for distance in range(1, neighbors + 1):
        count_here = reached[distance - 1]
        part = window_best[distance * block_count : distance * block_count + count_here]
        returned = passed_along(part, "shard", distance)
        returned = jnp.where(shard_pos >= distance, returned, jnp.float32(-1.0))
        result = result.at[:count_here].max(returned)
    result = lax.pmax(result, "rep")
    return result.reshape(row_count)


def solution(mesh):
    return jax.shard_map(
        shards,
        mesh=mesh,
        in_specs=(P("shard", None), P(), P("shard", None)),
        out_specs=P("shard"),
        check_vma=False,
    )
```

profile of v0, /device:TPU:7, one launch (start us, length us, event | category | flops | bytes accessed | tf_op | source)
XLA Modules:
  0.0 531.2 jit_solution(1499336457453972669)
XLA Ops:
  0.0 5.6 %multiply_reduce_fusion = f32[3072]{0:T(1024)S(1)} fusion(f32[3072,1024]{1,0:T(8,128)} %param.11), kind=kLoop, calls=%fused_computation.27 | loop fusion | flops 6288384 | bytes 12595200 | tf_op jit(solution)/shard_map/reduce_sum | solution.py:30
  5.6 2.5 copy-done.1
  8.2 3.8 divide_convert_fusion
  11.9 2.6 collective-permute-start
  14.5 7.8 %collective-permute-start.1 = (bf16[3072,1024]{1,0:T(8,128)(2,1)}, bf16[3072,1024]{1,0:T(8,128)(2,1)}, u32[]{:S(2)}, u32[]{:S(2)}) collective-permute-start(bf16[3072,1024]{1,0:T(8,128)(2,1)} %divide_convert_fusion), channel_id=1, source_target_pairs={{8,0},{12,4},{16,8},{20,12},{24,16},{28,20},{32,24},{36,28},{40,32... | collective-permute-start | bytes 18874376 | tf_op jit(solution)/shard_map/ppermute | solution.py:18
  22.4 0.3 reduce-window.9
  23.6 127.0 %collective-permute-done = bf16[3072,1024]{1,0:T(8,128)(2,1)} collective-permute-done((bf16[3072,1024]{1,0:T(8,128)(2,1)}, bf16[3072,1024]{1,0:T(8,128)(2,1)}, u32[]{:S(2)}, u32[]{:S(2)}) %collective-permute-start) | collective-permute-done | bytes 6291488 | tf_op jit(solution)/shard_map/ppermute | solution.py:18
  150.6 7.4 %collective-permute-done.1 = bf16[3072,1024]{1,0:T(8,128)(2,1)} collective-permute-done((bf16[3072,1024]{1,0:T(8,128)(2,1)}, bf16[3072,1024]{1,0:T(8,128)(2,1)}, u32[]{:S(2)}, u32[]{:S(2)}) %collective-permute-start.1) | collective-permute-done | bytes 6291488 | tf_op jit(solution)/shard_map/ppermute | solution.py:18
  158.0 22.5 %pad_maximum_fusion = bf16[9216,1024]{1,0:T(8,128)(2,1)} fusion(bf16[3072,1024]{1,0:T(8,128)(2,1)} %collective-permute-done.1, bf16[3072,1024]{1,0:T(8,128)(2,1)} %collective-permute-done, bf16[3072,1024]{1,0:T(8,128)(2,1)} %divide_convert_fusion), kind=kLoop, calls=%fused_computation.25 | loop fusion | flops 56623104 | bytes 37748736 | tf_op jit(solution)/shard_map/concatenate | solution.py:35
  180.5 22.3 %copy.12 = bf16[36,256,1024]{2,0,1:T(8,128)(2,1)} copy(bf16[36,256,1024]{2,1,0:T(8,128)(2,1)} %bitcast.33) | data formatting | bytes 37748736
  202.8 240.4 %while.15 = (s32[]{:T(128)}, f32[36,256]{1,0:T(8,128)S(1)}, s32[8,8]{1,0:T(8,128)S(1)}, s32[9216]{0:T(1024)S(1)}, s32[8,8]{1,0:T(8,128)S(1)}, /*index=5*/pred[8,...) while((s32[]{:T(128)}, f32[36,256]{1,0:T(8,128)S(1)}, ...), condition=%wide.region_12.13_spmd.clone.clone, body=%wide.region_5.12_spmd.clone.clone.sunk | while | flops 1384777856 | bytes 130555152 | solution.py:99
  203.4 10.9 %convolution_convert_fusion.4 = bf16[8,256,1024]{2,0,1:T(8,128)(2,1)} fusion(bf16[36,256,1024]{2,0,1:T(8,128)(2,1)} %get-tuple-element.279, s32[8]{0:T(128)S(1)} %get-tuple-element.244), kind=kOutput, calls=%fused_computation.5.clone.1 | convolution fusion | flops 153092384 | bytes 23068704 | tf_op jit(solution)/shard_map/while/body/eval_jaxpr/pt,tid->pid/dot_general | solution.py:68
  214.3 3.5 copy-done
  217.8 6.0 %convolution_convert_fusion.5 = bf16[8,256,1024]{2,0,1:T(8,128)(2,1)} fusion(bf16[36,256,1024]{2,0,1:T(8,128)(2,1)S(1)} %copy-done, s32[8]{0:T(128)S(1)} %get-tuple-element.245), kind=kOutput, calls=%fused_computation.6.clone.1 | convolution fusion | flops 153092384 | bytes 23068704 | tf_op jit(solution)/shard_map/while/body/eval_jaxpr/pt,tid->pid/dot_general | solution.py:68
  223.8 8.6 %fusion.33 = (f32[8,256]{1,0:T(8,128)S(1)}, f32[8,256]{1,0:T(8,128)S(1)}) fusion(bf16[8,256,1024]{2,0,1:T(8,128)(2,1)} %convolution_convert_fusion.4, bf16[8,256,1024]{2,0,1:T(8,128)(2,1)} %convolution_convert_fusion.5, pred[256,256]{1,0:T(8,128)(4,1)S(1)} %iota_compare_fusion.9, pred[8]{0:T(512)(128)(4,1)S(1)} %get-tuple-element.246, ...), kind=kOutput, calls=%fused_computation.52.clone.1 | convolution fusion | flops 1077932032 | bytes 8486928 | tf_op jit(solution)/shard_map/while/body/eval_jaxpr/pid,pjd->pij/dot_general | solution.py:80
  233.4 10.9 %convolution_convert_fusion.4 = bf16[8,256,1024]{2,0,1:T(8,128)(2,1)} fusion(bf16[36,256,1024]{2,0,1:T(8,128)(2,1)} %get-tuple-element.279, s32[8]{0:T(128)S(1)} %get-tuple-element.244), kind=kOutput, calls=%fused_computation.5.clone.1 | convolution fusion | flops 153092384 | bytes 23068704 | tf_op jit(solution)/shard_map/while/body/eval_jaxpr/pt,tid->pid/dot_general | solution.py:68
  244.3 3.5 copy-done
  247.8 6.0 %convolution_convert_fusion.5 = bf16[8,256,1024]{2,0,1:T(8,128)(2,1)} fusion(bf16[36,256,1024]{2,0,1:T(8,128)(2,1)S(1)} %copy-done, s32[8]{0:T(128)S(1)} %get-tuple-element.245), kind=kOutput, calls=%fused_computation.6.clone.1 | convolution fusion | flops 153092384 | bytes 23068704 | tf_op jit(solution)/shard_map/while/body/eval_jaxpr/pt,tid->pid/dot_general | solution.py:68
  253.9 8.6 %fusion.33 = (f32[8,256]{1,0:T(8,128)S(1)}, f32[8,256]{1,0:T(8,128)S(1)}) fusion(bf16[8,256,1024]{2,0,1:T(8,128)(2,1)} %convolution_convert_fusion.4, bf16[8,256,1024]{2,0,1:T(8,128)(2,1)} %convolution_convert_fusion.5, pred[256,256]{1,0:T(8,128)(4,1)S(1)} %iota_compare_fusion.9, pred[8]{0:T(512)(128)(4,1)S(1)} %get-tuple-element.246, ...), kind=kOutput, calls=%fused_computation.52.clone.1 | convolution fusion | flops 1077932032 | bytes 8486928 | tf_op jit(solution)/shard_map/while/body/eval_jaxpr/pid,pjd->pij/dot_general | solution.py:80
  262.5 0.2 select_reduce_fusion.10
  263.5 10.9 %convolution_convert_fusion.4 = bf16[8,256,1024]{2,0,1:T(8,128)(2,1)} fusion(bf16[36,256,1024]{2,0,1:T(8,128)(2,1)} %get-tuple-element.279, s32[8]{0:T(128)S(1)} %get-tuple-element.244), kind=kOutput, calls=%fused_computation.5.clone.1 | convolution fusion | flops 153092384 | bytes 23068704 | tf_op jit(solution)/shard_map/while/body/eval_jaxpr/pt,tid->pid/dot_general | solution.py:68
  274.4 3.5 copy-done
  277.9 6.0 %convolution_convert_fusion.5 = bf16[8,256,1024]{2,0,1:T(8,128)(2,1)} fusion(bf16[36,256,1024]{2,0,1:T(8,128)(2,1)S(1)} %copy-done, s32[8]{0:T(128)S(1)} %get-tuple-element.245), kind=kOutput, calls=%fused_computation.6.clone.1 | convolution fusion | flops 153092384 | bytes 23068704 | tf_op jit(solution)/shard_map/while/body/eval_jaxpr/pt,tid->pid/dot_general | solution.py:68
  284.0 8.6 %fusion.33 = (f32[8,256]{1,0:T(8,128)S(1)}, f32[8,256]{1,0:T(8,128)S(1)}) fusion(bf16[8,256,1024]{2,0,1:T(8,128)(2,1)} %convolution_convert_fusion.4, bf16[8,256,1024]{2,0,1:T(8,128)(2,1)} %convolution_convert_fusion.5, pred[256,256]{1,0:T(8,128)(4,1)S(1)} %iota_compare_fusion.9, pred[8]{0:T(512)(128)(4,1)S(1)} %get-tuple-element.246, ...), kind=kOutput, calls=%fused_computation.52.clone.1 | convolution fusion | flops 1077932032 | bytes 8486928 | tf_op jit(solution)/shard_map/while/body/eval_jaxpr/pid,pjd->pij/dot_general | solution.py:80
  293.5 10.9 %convolution_convert_fusion.4 = bf16[8,256,1024]{2,0,1:T(8,128)(2,1)} fusion(bf16[36,256,1024]{2,0,1:T(8,128)(2,1)} %get-tuple-element.279, s32[8]{0:T(128)S(1)} %get-tuple-element.244), kind=kOutput, calls=%fused_computation.5.clone.1 | convolution fusion | flops 153092384 | bytes 23068704 | tf_op jit(solution)/shard_map/while/body/eval_jaxpr/pt,tid->pid/dot_general | solution.py:68
  304.5 3.5 copy-done
  308.0 6.0 %convolution_convert_fusion.5 = bf16[8,256,1024]{2,0,1:T(8,128)(2,1)} fusion(bf16[36,256,1024]{2,0,1:T(8,128)(2,1)S(1)} %copy-done, s32[8]{0:T(128)S(1)} %get-tuple-element.245), kind=kOutput, calls=%fused_computation.6.clone.1 | convolution fusion | flops 153092384 | bytes 23068704 | tf_op jit(solution)/shard_map/while/body/eval_jaxpr/pt,tid->pid/dot_general | solution.py:68
  314.0 8.6 %fusion.33 = (f32[8,256]{1,0:T(8,128)S(1)}, f32[8,256]{1,0:T(8,128)S(1)}) fusion(bf16[8,256,1024]{2,0,1:T(8,128)(2,1)} %convolution_convert_fusion.4, bf16[8,256,1024]{2,0,1:T(8,128)(2,1)} %convolution_convert_fusion.5, pred[256,256]{1,0:T(8,128)(4,1)S(1)} %iota_compare_fusion.9, pred[8]{0:T(512)(128)(4,1)S(1)} %get-tuple-element.246, ...), kind=kOutput, calls=%fused_computation.52.clone.1 | convolution fusion | flops 1077932032 | bytes 8486928 | tf_op jit(solution)/shard_map/while/body/eval_jaxpr/pid,pjd->pij/dot_general | solution.py:80
  323.6 10.9 %convolution_convert_fusion.4 = bf16[8,256,1024]{2,0,1:T(8,128)(2,1)} fusion(bf16[36,256,1024]{2,0,1:T(8,128)(2,1)} %get-tuple-element.279, s32[8]{0:T(128)S(1)} %get-tuple-element.244), kind=kOutput, calls=%fused_computation.5.clone.1 | convolution fusion | flops 153092384 | bytes 23068704 | tf_op jit(solution)/shard_map/while/body/eval_jaxpr/pt,tid->pid/dot_general | solution.py:68
  334.5 3.5 copy-done
  338.0 6.0 %convolution_convert_fusion.5 = bf16[8,256,1024]{2,0,1:T(8,128)(2,1)} fusion(bf16[36,256,1024]{2,0,1:T(8,128)(2,1)S(1)} %copy-done, s32[8]{0:T(128)S(1)} %get-tuple-element.245), kind=kOutput, calls=%fused_computation.6.clone.1 | convolution fusion | flops 153092384 | bytes 23068704 | tf_op jit(solution)/shard_map/while/body/eval_jaxpr/pt,tid->pid/dot_general | solution.py:68
  344.1 8.6 %fusion.33 = (f32[8,256]{1,0:T(8,128)S(1)}, f32[8,256]{1,0:T(8,128)S(1)}) fusion(bf16[8,256,1024]{2,0,1:T(8,128)(2,1)} %convolution_convert_fusion.4, bf16[8,256,1024]{2,0,1:T(8,128)(2,1)} %convolution_convert_fusion.5, pred[256,256]{1,0:T(8,128)(4,1)S(1)} %iota_compare_fusion.9, pred[8]{0:T(512)(128)(4,1)S(1)} %get-tuple-element.246, ...), kind=kOutput, calls=%fused_computation.52.clone.1 | convolution fusion | flops 1077932032 | bytes 8486928 | tf_op jit(solution)/shard_map/while/body/eval_jaxpr/pid,pjd->pij/dot_general | solution.py:80
  353.6 10.9 %convolution_convert_fusion.4 = bf16[8,256,1024]{2,0,1:T(8,128)(2,1)} fusion(bf16[36,256,1024]{2,0,1:T(8,128)(2,1)} %get-tuple-element.279, s32[8]{0:T(128)S(1)} %get-tuple-element.244), kind=kOutput, calls=%fused_computation.5.clone.1 | convolution fusion | flops 153092384 | bytes 23068704 | tf_op jit(solution)/shard_map/while/body/eval_jaxpr/pt,tid->pid/dot_general | solution.py:68
  364.6 3.5 copy-done
  368.1 6.0 %convolution_convert_fusion.5 = bf16[8,256,1024]{2,0,1:T(8,128)(2,1)} fusion(bf16[36,256,1024]{2,0,1:T(8,128)(2,1)S(1)} %copy-done, s32[8]{0:T(128)S(1)} %get-tuple-element.245), kind=kOutput, calls=%fused_computation.6.clone.1 | convolution fusion | flops 153092384 | bytes 23068704 | tf_op jit(solution)/shard_map/while/body/eval_jaxpr/pt,tid->pid/dot_general | solution.py:68
  374.1 8.6 %fusion.33 = (f32[8,256]{1,0:T(8,128)S(1)}, f32[8,256]{1,0:T(8,128)S(1)}) fusion(bf16[8,256,1024]{2,0,1:T(8,128)(2,1)} %convolution_convert_fusion.4, bf16[8,256,1024]{2,0,1:T(8,128)(2,1)} %convolution_convert_fusion.5, pred[256,256]{1,0:T(8,128)(4,1)S(1)} %iota_compare_fusion.9, pred[8]{0:T(512)(128)(4,1)S(1)} %get-tuple-element.246, ...), kind=kOutput, calls=%fused_computation.52.clone.1 | convolution fusion | flops 1077932032 | bytes 8486928 | tf_op jit(solution)/shard_map/while/body/eval_jaxpr/pid,pjd->pij/dot_general | solution.py:80
  383.7 10.9 %convolution_convert_fusion.4 = bf16[8,256,1024]{2,0,1:T(8,128)(2,1)} fusion(bf16[36,256,1024]{2,0,1:T(8,128)(2,1)} %get-tuple-element.279, s32[8]{0:T(128)S(1)} %get-tuple-element.244), kind=kOutput, calls=%fused_computation.5.clone.1 | convolution fusion | flops 153092384 | bytes 23068704 | tf_op jit(solution)/shard_map/while/body/eval_jaxpr/pt,tid->pid/dot_general | solution.py:68
  394.6 3.5 copy-done
  398.1 6.0 %convolution_convert_fusion.5 = bf16[8,256,1024]{2,0,1:T(8,128)(2,1)} fusion(bf16[36,256,1024]{2,0,1:T(8,128)(2,1)S(1)} %copy-done, s32[8]{0:T(128)S(1)} %get-tuple-element.245), kind=kOutput, calls=%fused_computation.6.clone.1 | convolution fusion | flops 153092384 | bytes 23068704 | tf_op jit(solution)/shard_map/while/body/eval_jaxpr/pt,tid->pid/dot_general | solution.py:68
  404.2 8.6 %fusion.33 = (f32[8,256]{1,0:T(8,128)S(1)}, f32[8,256]{1,0:T(8,128)S(1)}) fusion(bf16[8,256,1024]{2,0,1:T(8,128)(2,1)} %convolution_convert_fusion.4, bf16[8,256,1024]{2,0,1:T(8,128)(2,1)} %convolution_convert_fusion.5, pred[256,256]{1,0:T(8,128)(4,1)S(1)} %iota_compare_fusion.9, pred[8]{0:T(512)(128)(4,1)S(1)} %get-tuple-element.246, ...), kind=kOutput, calls=%fused_computation.52.clone.1 | convolution fusion | flops 1077932032 | bytes 8486928 | tf_op jit(solution)/shard_map/while/body/eval_jaxpr/pid,pjd->pij/dot_general | solution.py:80
  413.7 10.9 %convolution_convert_fusion.4 = bf16[8,256,1024]{2,0,1:T(8,128)(2,1)} fusion(bf16[36,256,1024]{2,0,1:T(8,128)(2,1)} %get-tuple-element.279, s32[8]{0:T(128)S(1)} %get-tuple-element.244), kind=kOutput, calls=%fused_computation.5.clone.1 | convolution fusion | flops 153092384 | bytes 23068704 | tf_op jit(solution)/shard_map/while/body/eval_jaxpr/pt,tid->pid/dot_general | solution.py:68
  424.7 3.5 copy-done
  428.2 6.0 %convolution_convert_fusion.5 = bf16[8,256,1024]{2,0,1:T(8,128)(2,1)} fusion(bf16[36,256,1024]{2,0,1:T(8,128)(2,1)S(1)} %copy-done, s32[8]{0:T(128)S(1)} %get-tuple-element.245), kind=kOutput, calls=%fused_computation.6.clone.1 | convolution fusion | flops 153092384 | bytes 23068704 | tf_op jit(solution)/shard_map/while/body/eval_jaxpr/pt,tid->pid/dot_general | solution.py:68
  434.2 8.6 %fusion.33 = (f32[8,256]{1,0:T(8,128)S(1)}, f32[8,256]{1,0:T(8,128)S(1)}) fusion(bf16[8,256,1024]{2,0,1:T(8,128)(2,1)} %convolution_convert_fusion.4, bf16[8,256,1024]{2,0,1:T(8,128)(2,1)} %convolution_convert_fusion.5, pred[256,256]{1,0:T(8,128)(4,1)S(1)} %iota_compare_fusion.9, pred[8]{0:T(512)(128)(4,1)S(1)} %get-tuple-element.246, ...), kind=kOutput, calls=%fused_computation.52.clone.1 | convolution fusion | flops 1077932032 | bytes 8486928 | tf_op jit(solution)/shard_map/while/body/eval_jaxpr/pid,pjd->pij/dot_general | solution.py:80
  443.2 66.0 %collective-permute-start.2 = (f32[12,256]{1,0:T(8,128)S(1)}, f32[12,256]{1,0:T(8,128)S(1)}, u32[]{:S(2)}, u32[]{:S(2)}) collective-permute-start(f32[12,256]{1,0:T(8,128)S(1)} %slice.56), channel_id=1, source_target_pairs={{0,4},{4,8},{8,12},{12,16},{16,20},{20,24},{24,28},{28,32},{32,36}... | collective-permute-start | bytes 36872 | tf_op jit(solution)/shard_map/ppermute | solution.py:18
  509.2 3.5 collective-permute-start.3
  512.8 4.4 collective-permute-done.3
  517.3 14.0 %pmax.7 = f32[3072]{0:T(1024)} all-reduce(f32[3072]{0:T(1024)S(1)} %reshape.178), channel_id=1, replica_groups=mesh['shard'=64,'rep'=4] {'rep'}, use_global_device_ids=true, to_apply=%region_13.14 | all-reduce | flops 3072 | bytes 24576 | tf_op jit(solution)/shard_map/pmax | solution.py:109
  (135 shorter events, 7.9 us)
Async XLA Ops:
  0.0 8.2 %copy-start.1 = (f32[3072,1024]{1,0:T(8,128)S(1)}, f32[3072,1024]{1,0:T(8,128)}, u32[]{:S(2)}) copy-start(f32[3072,1024]{1,0:T(8,128)} %param.11) | copy-start | bytes 37748740
  8.2 14.1 %copy-start.3 = (s32[204,1]{0,1:T(1,128)S(1)}, s32[204,1]{0,1:T(1,128)}, u32[]{:S(2)}) copy-start(s32[204,1]{0,1:T(1,128)} %param.13) | copy-start | bytes 2452
  8.2 15.3 %copy-start.2 = (s32[196608]{0:T(1024)S(1)}, s32[196608]{0:T(1024)}, u32[]{:S(2)}) copy-start(s32[196608]{0:T(1024)} %param.12) | copy-start | bytes 2359300
  11.9 138.7 %collective-permute-start = (bf16[3072,1024]{1,0:T(8,128)(2,1)}, bf16[3072,1024]{1,0:T(8,128)(2,1)}, u32[]{:S(2)}, u32[]{:S(2)}) collective-permute-start(bf16[3072,1024]{1,0:T(8,128)(2,1)} %divide_convert_fusion), channel_id=1, source_target_pairs={{4,0},{8,4},{12,8},{16,12},{20,16},{24,20},{28,24},{32,28},{36,32}... | collective-permute-start | bytes 18874376 | tf_op jit(solution)/shard_map/ppermute | solution.py:18
  14.5 143.4 %collective-permute-start.1 = (bf16[3072,1024]{1,0:T(8,128)(2,1)}, bf16[3072,1024]{1,0:T(8,128)(2,1)}, u32[]{:S(2)}, u32[]{:S(2)}) collective-permute-start(bf16[3072,1024]{1,0:T(8,128)(2,1)} %divide_convert_fusion), channel_id=1, source_target_pairs={{8,0},{12,4},{16,8},{20,12},{24,16},{28,20},{32,24},{36,28},{40,32... | collective-permute-start | bytes 18874376 | tf_op jit(solution)/shard_map/ppermute | solution.py:18
  203.4 14.4 %copy-start = (bf16[36,256,1024]{2,0,1:T(8,128)(2,1)S(1)}, bf16[36,256,1024]{2,0,1:T(8,128)(2,1)}, u32[]{:S(2)}) copy-start(bf16[36,256,1024]{2,0,1:T(8,128)(2,1)} %get-tuple-element.279) | copy-start | bytes 56623108 | tf_op jit(solution)/shard_map/while
  233.4 14.4 %copy-start = (bf16[36,256,1024]{2,0,1:T(8,128)(2,1)S(1)}, bf16[36,256,1024]{2,0,1:T(8,128)(2,1)}, u32[]{:S(2)}) copy-start(bf16[36,256,1024]{2,0,1:T(8,128)(2,1)} %get-tuple-element.279) | copy-start | bytes 56623108 | tf_op jit(solution)/shard_map/while
  263.5 14.4 %copy-start = (bf16[36,256,1024]{2,0,1:T(8,128)(2,1)S(1)}, bf16[36,256,1024]{2,0,1:T(8,128)(2,1)}, u32[]{:S(2)}) copy-start(bf16[36,256,1024]{2,0,1:T(8,128)(2,1)} %get-tuple-element.279) | copy-start | bytes 56623108 | tf_op jit(solution)/shard_map/while
  293.5 14.4 %copy-start = (bf16[36,256,1024]{2,0,1:T(8,128)(2,1)S(1)}, bf16[36,256,1024]{2,0,1:T(8,128)(2,1)}, u32[]{:S(2)}) copy-start(bf16[36,256,1024]{2,0,1:T(8,128)(2,1)} %get-tuple-element.279) | copy-start | bytes 56623108 | tf_op jit(solution)/shard_map/while
  323.6 14.4 %copy-start = (bf16[36,256,1024]{2,0,1:T(8,128)(2,1)S(1)}, bf16[36,256,1024]{2,0,1:T(8,128)(2,1)}, u32[]{:S(2)}) copy-start(bf16[36,256,1024]{2,0,1:T(8,128)(2,1)} %get-tuple-element.279) | copy-start | bytes 56623108 | tf_op jit(solution)/shard_map/while
  353.6 14.4 %copy-start = (bf16[36,256,1024]{2,0,1:T(8,128)(2,1)S(1)}, bf16[36,256,1024]{2,0,1:T(8,128)(2,1)}, u32[]{:S(2)}) copy-start(bf16[36,256,1024]{2,0,1:T(8,128)(2,1)} %get-tuple-element.279) | copy-start | bytes 56623108 | tf_op jit(solution)/shard_map/while
  383.7 14.4 %copy-start = (bf16[36,256,1024]{2,0,1:T(8,128)(2,1)S(1)}, bf16[36,256,1024]{2,0,1:T(8,128)(2,1)}, u32[]{:S(2)}) copy-start(bf16[36,256,1024]{2,0,1:T(8,128)(2,1)} %get-tuple-element.279) | copy-start | bytes 56623108 | tf_op jit(solution)/shard_map/while
  413.7 14.4 %copy-start = (bf16[36,256,1024]{2,0,1:T(8,128)(2,1)S(1)}, bf16[36,256,1024]{2,0,1:T(8,128)(2,1)}, u32[]{:S(2)}) copy-start(bf16[36,256,1024]{2,0,1:T(8,128)(2,1)} %get-tuple-element.279) | copy-start | bytes 56623108 | tf_op jit(solution)/shard_map/while
  443.2 69.6 %collective-permute-start.2 = (f32[12,256]{1,0:T(8,128)S(1)}, f32[12,256]{1,0:T(8,128)S(1)}, u32[]{:S(2)}, u32[]{:S(2)}) collective-permute-start(f32[12,256]{1,0:T(8,128)S(1)} %slice.56), channel_id=1, source_target_pairs={{0,4},{4,8},{8,12},{12,16},{16,20},{20,24},{24,28},{28,32},{32,36}... | collective-permute-start | bytes 36872 | tf_op jit(solution)/shard_map/ppermute | solution.py:18
  509.2 8.0 %collective-permute-start.3 = (f32[4,256]{1,0:T(4,128)S(1)}, f32[4,256]{1,0:T(4,128)S(1)}, u32[]{:S(2)}, u32[]{:S(2)}) collective-permute-start(f32[4,256]{1,0:T(4,128)S(1)} %slice.58), channel_id=1, source_target_pairs={{0,8},{4,12},{8,16},{12,20},{16,24},{20,28},{24,32},{28,36},{32,40... | collective-permute-start | bytes 12296 | tf_op jit(solution)/shard_map/ppermute | solution.py:18
where the time goes:
time: 537 us; the launch traced here: 531 us
  matrix products  205 us (38%)
  waiting for transfers between devices  139 us (26%)
  starting transfers between devices  79.9 us (15%)
  local copies, waits for them, and re-layouts  55.3 us (10%)
  other arithmetic  37.9 us (7%)
  blocking collectives  14 us (3%)
    ppermute x4, waiting for transfers between devices, passed_along(): lax.ppermute(value, axis, [(source, source + steps) for source in range(l...  139 us
    dot_general x16, matrix products, select_rows(): jnp.einsum('pt,tid->pid', picker, window, preferred_element_type=jnp.floa...  136 us
    ppermute x4, starting transfers between devices, passed_along(): lax.ppermute(value, axis, [(source, source + steps) for source in range(l...  79.9 us
    dot_general x8, matrix products, compare(): jnp.einsum('pid,pjd->pij', left_rows, right_rows, preferred_element_type=...  69.1 us
    while x16, local copies, waits for them, and re-layouts  28 us
    unnamed x7, local copies, waits for them, and re-layouts  24.8 us
    concatenate x1, other arithmetic, shards(): window = jnp.concatenate(pieces, axis=0)  22.5 us
    pmax x1, blocking collectives, shards(): result = lax.pmax(result, 'rep')  14 us
  transfers between devices with their start and end apart: 4, of which 3 were waited for; matrix products, arithmetic and copies ran while one was open for 0% of the time, Pallas kernels for 0%

commit v1 on v0

v1 whole, which is shorter than its diff:
```python
import functools

import jax
import jax.numpy as jnp
from jax import lax
from jax.experimental import pallas as pl
from jax.experimental.pallas import tpu as pltpu
from jax.sharding import PartitionSpec as P

BLOCK = 256
SPANS = 17
WIDTH = 1024
OWN = 12
REPS = 4
NEAR = 4
CHIP_SLOTS = NEAR + 1
FAR_SLOTS = 2
TAIL = 16
WINDOW = OWN + 2 * (SPANS - 1)
EPS = 1e-6
VMEM_LIMIT = 48 * 1024 * 1024

HBM = pl.BlockSpec(memory_space=pl.ANY)
SMEM = pl.BlockSpec(memory_space=pltpu.SMEM)
VMEM = pl.BlockSpec(memory_space=pltpu.VMEM)


def unit_rows(rows):
    squares = jnp.sum(rows * rows, axis=1, keepdims=True)
    return (rows * lax.rsqrt(squares + EPS)).astype(jnp.bfloat16)


def rows_of(slot, count=BLOCK):
    return pl.ds(pl.multiple_of(slot * BLOCK, BLOCK), count)


def far_local(core, m):
    return jnp.where(core == 0, m - 1, OWN - m)


def chip_local(core, m):
    return jnp.where(core == 0, OWN - m, m - 1)


def far_index(rep, slot):
    return jnp.where(slot == 0, rep + 1, 8 - rep)


def chip_index(rep, slot):
    return jnp.where(slot < NEAR, slot + 1, 8 - rep)


def send_kernel(place, holder, emb, far_out, chip_out, raw, out, tails, in_sems, out_sems, tail_sems):
    core, rep = place[0] % 2, place[1]
    total = FAR_SLOTS + CHIP_SLOTS

    def local(slot):
        return jnp.where(
            slot < FAR_SLOTS,
            far_local(core, far_index(rep, slot)),
            chip_local(core, chip_index(rep, slot - FAR_SLOTS)),
        )

    def fetch(slot):
        return pltpu.make_async_copy(
            emb.at[rows_of(local(slot))], raw.at[rows_of(slot)], in_sems.at[slot]
        )

    @pl.loop(0, total)
    def _(slot):
        fetch(slot).start()

    lane = lax.broadcasted_iota(jnp.int32, (TAIL, 128), 1)
    row = lax.broadcasted_iota(jnp.int32, (TAIL, 128), 0)
    for part, (first, count) in enumerate(((0, FAR_SLOTS), (FAR_SLOTS, CHIP_SLOTS))):
        flags = jnp.zeros((TAIL, 128), jnp.float32)
        for slot in range(count):
            base = local(jnp.int32(first + slot)) * SPANS
            for k in range(SPANS):
                listed = jnp.where(holder[base + k] != REPS, 1.0, 0.0)
                flags = jnp.where((row == slot) & (lane == k), listed, flags)
        tails[part] = jnp.zeros((TAIL, WIDTH), jnp.bfloat16)
        tails[part, :, 0:128] = flags.astype(jnp.bfloat16)
    far_tail = pltpu.make_async_copy(
        tails.at[0], far_out.at[pl.ds(FAR_SLOTS * BLOCK, TAIL)], tail_sems.at[0]
    )
    chip_tail = pltpu.make_async_copy(
        tails.at[1], chip_out.at[pl.ds(CHIP_SLOTS * BLOCK, TAIL)], tail_sems.at[1]
    )
    far_tail.start()
    chip_tail.start()

    def far_push(slot):
        return pltpu.make_async_copy(
            out.at[rows_of(slot)], far_out.at[rows_of(slot)], out_sems.at[slot]
        )

    def chip_push(slot):
        return pltpu.make_async_copy(
            out.at[rows_of(slot)], chip_out.at[rows_of(slot - FAR_SLOTS)], out_sems.at[slot]
        )

    @pl.loop(0, FAR_SLOTS)
    def _(slot):
        fetch(slot).wait()
        out[rows_of(slot), :] = unit_rows(raw[rows_of(slot), :])
        far_push(slot).start()

    @pl.loop(FAR_SLOTS, total)
    def _(slot):
        fetch(slot).wait()
        out[rows_of(slot), :] = unit_rows(raw[rows_of(slot), :])
        chip_push(slot).start()

    @pl.loop(0, FAR_SLOTS)
    def _(slot):
        far_push(slot).wait()

    @pl.loop(FAR_SLOTS, total)
    def _(slot):
        chip_push(slot).wait()

    far_tail.wait()
    chip_tail.wait()


def send_payloads(place, holder, emb):
    total = FAR_SLOTS + CHIP_SLOTS
    return pl.pallas_call(
        send_kernel,
        out_shape=(
            jax.ShapeDtypeStruct((FAR_SLOTS * BLOCK + TAIL, WIDTH), jnp.bfloat16),
            jax.ShapeDtypeStruct((CHIP_SLOTS * BLOCK + TAIL, WIDTH), jnp.bfloat16),
        ),
        in_specs=[SMEM, SMEM, HBM],
        out_specs=(HBM, HBM),
        scratch_shapes=[
            pltpu.VMEM((total * BLOCK, WIDTH), jnp.float32),
            pltpu.VMEM((total * BLOCK, WIDTH), jnp.bfloat16),
            pltpu.VMEM((2, TAIL, WIDTH), jnp.bfloat16),
            pltpu.SemaphoreType.DMA((total,)),
            pltpu.SemaphoreType.DMA((total,)),
            pltpu.SemaphoreType.DMA((2,)),
        ],
        compiler_params=pltpu.CompilerParams(vmem_limit_bytes=VMEM_LIMIT),
        name="send_rows",
    )(place, holder, emb)


def similarity(left, right):
    return lax.dot_general(
        left, right, (((1,), (1,)), ((), ())), preferred_element_type=jnp.float32
    )


def inside(scored, row_low, row_count, col_low, col_count):
    rows = lax.broadcasted_iota(jnp.int32, (BLOCK, BLOCK), 0)
    cols = lax.broadcasted_iota(jnp.int32, (BLOCK, BLOCK), 1)
    keep = (rows >= row_low) & (rows < row_low + row_count)
    keep = keep & (cols >= col_low) & (cols < col_low + col_count)
    return jnp.where(keep, scored, -1.0)


def fold_rows(scored):
    return jnp.maximum(scored[:, 0:128], scored[:, 128:256])


def fold_cols(scored):
    return jnp.max(scored.reshape(BLOCK // 8, 8, BLOCK), axis=0)


def as_lanes(column):
    rows = lax.broadcasted_iota(jnp.int32, (BLOCK, BLOCK), 0)
    cols = lax.broadcasted_iota(jnp.int32, (BLOCK, BLOCK), 1)
    return jnp.max(jnp.where(rows == cols, column, -1.0), axis=0, keepdims=True)


def label_stats(stats, block):
    slot = jnp.clip(block - stats[0], 0, WINDOW - 1)
    return [stats[1 + part * WINDOW + slot] for part in range(4)]


def local_kernel(place, holder, stats, tags, emb, units_out, best, raw, units, row_acc, col_acc, in_sems, out_sems):
    shard, rep = place[0], place[1]
    first_block = shard * OWN

    def fetch(block):
        return pltpu.make_async_copy(
            emb.at[rows_of(block)], raw.at[rows_of(block)], in_sems.at[block]
        )

    def push(block):
        return pltpu.make_async_copy(
            units.at[rows_of(block)], units_out.at[rows_of(block)], out_sems.at[block]
        )

    @pl.loop(0, OWN)
    def _(block):
        fetch(block).start()

    col_acc[...] = jnp.full(col_acc.shape, -1.0, jnp.float32)
    best[...] = jnp.full(best.shape, -1.0, jnp.float32)

    @pl.loop(0, OWN)
    def _(block):
        fetch(block).wait()
        units[rows_of(block), :] = unit_rows(raw[rows_of(block), :])
        push(block).start()

        turn = lax.rem(block, 4)
        mine = jnp.where(lax.rem(block // 4, 2) == 0, turn, 3 - turn) == rep

        @pl.when(mine)
        def _():
            b_first, _, b_count, _ = label_stats(stats, first_block + block)
            row_acc[...] = jnp.full(row_acc.shape, -1.0, jnp.float32)

            @pl.loop(0, block)
            def _(other):
                _, a_last, _, a_start = label_stats(stats, first_block + other)
                listed = holder[other * SPANS + (block - other)] != REPS

                @pl.when(listed & (a_last == b_first))
                def _():
                    scored = similarity(units[rows_of(block), :], units[rows_of(other), :])
                    scored = inside(scored, 0, b_count, a_start, BLOCK - a_start)
                    row_acc[...] = jnp.maximum(row_acc[...], fold_rows(scored))
                    col_acc[other] = jnp.maximum(col_acc[other], fold_cols(scored))

            found = as_lanes(jnp.max(row_acc[...], axis=1, keepdims=True))
            best[pl.ds(block, 1), :] = found

            @pl.when(holder[block * SPANS] != REPS)
            def _():
                tag_row = tags[pl.ds(first_block - stats[0] + block, 1), :].astype(jnp.float32)
                rows = lax.broadcasted_iota(jnp.int32, (BLOCK, BLOCK), 0)
                cols = lax.broadcasted_iota(jnp.int32, (BLOCK, BLOCK), 1)
                spread = jnp.broadcast_to(tag_row, (BLOCK, BLOCK))
                tag_col = jnp.max(
                    jnp.where(rows == cols, spread, -1.0), axis=1, keepdims=True
                )
                scored = similarity(units[rows_of(block), :], units[rows_of(block), :])
                scored = jnp.where((tag_col == tag_row) & (rows != cols), scored, -1.0)
                col_acc[block] = jnp.maximum(col_acc[block], fold_cols(scored))

    for block in range(OWN):
        found = jnp.max(col_acc[block], axis=0, keepdims=True)
        best[block : block + 1, :] = jnp.maximum(best[block : block + 1, :], found)

    @pl.loop(0, OWN)
    def _(block):
        push(block).wait()


def local_pairs(place, holder, stats, tags, emb):
    return pl.pallas_call(
        local_kernel,
        out_shape=(
            jax.ShapeDtypeStruct((OWN * BLOCK, WIDTH), jnp.bfloat16),
            jax.ShapeDtypeStruct((OWN, BLOCK), jnp.float32),
        ),
        in_specs=[SMEM, SMEM, SMEM, VMEM, HBM],
        out_specs=(HBM, VMEM),
        scratch_shapes=[
            pltpu.VMEM((OWN * BLOCK, WIDTH), jnp.float32),
            pltpu.VMEM((OWN * BLOCK, WIDTH), jnp.bfloat16),
            pltpu.VMEM((BLOCK, 128), jnp.float32),
            pltpu.VMEM((OWN, 8, BLOCK), jnp.float32),
            pltpu.SemaphoreType.DMA((OWN,)),
            pltpu.SemaphoreType.DMA((OWN,)),
        ],
        compiler_params=pltpu.CompilerParams(vmem_limit_bytes=VMEM_LIMIT),
        cost_estimate=pl.CostEstimate(
            flops=20 * 2 * BLOCK * BLOCK * WIDTH, bytes_accessed=18 << 20, transcendentals=0
        ),
        name="local_pairs",
    )(place, holder, stats, tags, emb)


def flag_bits(tail, slot):
    lane = lax.broadcasted_iota(jnp.int32, (TAIL, 128), 1)
    row = lax.broadcasted_iota(jnp.int32, (TAIL, 128), 0)
    weight = lax.shift_left(jnp.int32(1), jnp.minimum(lane, SPANS)).astype(jnp.float32)
    weight = jnp.where((row == slot) & (lane < SPANS), weight, 0.0)
    return jnp.sum(tail[:, 0:128].astype(jnp.float32) * weight).astype(jnp.int32)


def cross_kernel(
    far, block_count, place, holder, stats, best_in, units_hbm, chip_hbm, *rest
):
    if far:
        far_hbm, best, returned, units, chip, moved, bits, row_acc, col_acc, unit_sems, in_sems = rest
    else:
        best, units, chip, bits, row_acc, col_acc, unit_sems, in_sems = rest
        moved = chip
    shard, rep = place[0], place[1]
    core = lax.rem(shard, 2)
    side = core if far else 1 - core
    columns = OWN + NEAR if far else OWN
    first_block = shard * OWN
    chip_rows = CHIP_SLOTS * BLOCK + TAIL

    def local(m):
        return far_local(core, m) if far else chip_local(core, m)

    def fetch(m):
        block = rows_of(local(m))
        return pltpu.make_async_copy(units_hbm.at[block], units.at[block], unit_sems.at[m - 1])

    fetch_chip = pltpu.make_async_copy(chip_hbm, chip, in_sems.at[0])
    fetch_chip.start()
    if far:
        fetch_far = pltpu.make_async_copy(far_hbm, moved, in_sems.at[1])
        fetch_far.start()

    @pl.loop(1, OWN + 1)
    def _(m):
        fetch(m).start()

    col_acc[...] = jnp.full(col_acc.shape, -1.0, jnp.float32)
    row_acc[...] = jnp.full(row_acc.shape, -1.0, jnp.float32)
    fetch_chip.wait()
    chip_tail = chip[pl.ds(CHIP_SLOTS * BLOCK, TAIL), :]
    for slot in range(CHIP_SLOTS):
        bits[slot] = flag_bits(chip_tail, slot)
    if far:
        fetch_far.wait()
        far_tail = moved[pl.ds(FAR_SLOTS * BLOCK, TAIL), :]
        for slot in range(FAR_SLOTS):
            bits[CHIP_SLOTS + slot] = flag_bits(far_tail, slot)

    def moved_slot(which):
        if far:
            return which
        return jnp.where(which == 0, rep, NEAR)

    def compare(which, m, column):
        near = far_index(rep, which)
        moved_block = jnp.where(side == 0, first_block - near, first_block + OWN - 1 + near)
        column_block = jnp.where(side == 0, first_block + m - 1, first_block + OWN - m)
        offset = near + m - 1
        tie = lax.rem(near, 2) == 1 - side
        wanted = (m > near) | ((m == near) & tie)
        wanted = wanted & (offset < SPANS)
        wanted = wanted & (moved_block >= 0) & (moved_block < block_count)
        offset = jnp.minimum(offset, SPANS - 1)
        bit_slot = moved_slot(which) + (CHIP_SLOTS if far else 0)
        own_flag = holder[jnp.minimum(local(jnp.minimum(m, OWN)), OWN - 1) * SPANS + offset] != REPS
        bit_source = jnp.where(side == 0, bit_slot, jnp.clip(m - OWN - 1, 0, NEAR - 1))
        bit_flag = lax.rem(lax.shift_right_logical(bits[bit_source], offset), 2) == 1
        listed = jnp.where((side == 0) | (m > OWN), bit_flag, own_flag)
        m_first, m_last, m_count, m_start = label_stats(stats, moved_block)
        c_first, c_last, c_count, c_start = label_stats(stats, column_block)
        shared = jnp.where(side == 0, m_last == c_first, c_last == m_first)

        @pl.when(wanted & listed & shared)
        def _():
            scored = similarity(moved[rows_of(moved_slot(which)), :], column)
            scored = inside(
                scored,
                jnp.where(side == 0, m_start, 0),
                jnp.where(side == 0, BLOCK - m_start, m_count),
                jnp.where(side == 0, 0, c_start),
                jnp.where(side == 0, c_count, BLOCK - c_start),
            )
            row_acc[which] = jnp.maximum(row_acc[which], fold_rows(scored))
            col_acc[m - 1] = jnp.maximum(col_acc[m - 1], fold_cols(scored))

    @pl.loop(1, OWN + 1)
    def _(m):
        fetch(m).wait()

        @pl.loop(0, 2)
        def _(which):
            compare(which, m, units[rows_of(local(m)), :])

    if far:
        @pl.loop(OWN + 1, OWN + NEAR + 1)
        def _(m):
            compare(jnp.int32(0), m, chip[rows_of(m - OWN - 1), :])

    best[...] = best_in[...]

    def improve(place_core, block, found):
        here = (place_core, pl.ds(block, 1), slice(None))
        best[here] = jnp.maximum(best[here], found)

    for m in range(1, OWN + 1):
        improve(core, local(m), jnp.max(col_acc[m - 1], axis=0, keepdims=True))
    if far:
        for m in range(OWN + 1, OWN + NEAR + 1):
            found = jnp.max(col_acc[m - 1], axis=0, keepdims=True)
            improve(1 - core, chip_local(1 - core, m - OWN), found)
    for which in range(2):
        found = as_lanes(jnp.max(row_acc[which], axis=1, keepdims=True))
        if far:
            returned[which : which + 1, :] = found
        else:
            improve(1 - core, chip_local(1 - core, far_index(rep, which)), found)


def cross_pairs(far, block_count, place, holder, stats, best, units, chip, *more):
    columns = OWN + NEAR if far else OWN
    best_shape = jax.ShapeDtypeStruct((2, OWN, BLOCK), jnp.float32)
    chip_rows = CHIP_SLOTS * BLOCK + TAIL
    far_rows = FAR_SLOTS * BLOCK + TAIL
    return pl.pallas_call(
        functools.partial(cross_kernel, far, block_count),
        out_shape=(best_shape, jax.ShapeDtypeStruct((2, BLOCK), jnp.float32)) if far else best_shape,
        in_specs=[SMEM, SMEM, SMEM, VMEM] + [HBM] * (3 if far else 2),
        out_specs=(VMEM, VMEM) if far else VMEM,
        scratch_shapes=[
            pltpu.VMEM((OWN * BLOCK, WIDTH), jnp.bfloat16),
            pltpu.VMEM((chip_rows, WIDTH), jnp.bfloat16),
        ]
        + ([pltpu.VMEM((far_rows, WIDTH), jnp.bfloat16)] if far else [])
        + [
            pltpu.SMEM((CHIP_SLOTS + FAR_SLOTS,), jnp.int32),
            pltpu.VMEM((2, BLOCK, 128), jnp.float32),
            pltpu.VMEM((columns, 8, BLOCK), jnp.float32),
            pltpu.SemaphoreType.DMA((OWN,)),
            pltpu.SemaphoreType.DMA((2,)),
        ],
        compiler_params=pltpu.CompilerParams(vmem_limit_bytes=VMEM_LIMIT),
        cost_estimate=pl.CostEstimate(
            flops=14 * 2 * BLOCK * BLOCK * WIDTH, bytes_accessed=9 << 20, transcendentals=0
        ),
        name="far_pairs" if far else "chip_pairs",
    )(place, holder, stats, best, units, chip, *more)


def shards(embeddings, labels, holder):
    count = lax.axis_size("shard")
    block_count = count * OWN
    shard = lax.axis_index("shard")
    rep = lax.axis_index("rep")
    core = shard % 2
    place = jnp.stack([shard, rep]).astype(jnp.int32)
    listing = holder.reshape(-1)

    far_out, chip_out = send_payloads(place, listing, embeddings)
    across = [(s, s + 1) for s in range(1, count - 1, 2)]
    across = across + [(b, a) for a, b in across]
    within = [(s, s ^ 1) for s in range(count)]
    far_in = lax.ppermute(far_out, "shard", across)
    chip_in = lax.ppermute(chip_out, "shard", within)

    start = jnp.clip(shard * OWN - (SPANS - 1), 0, block_count - WINDOW)
    tags = lax.dynamic_slice_in_dim(labels, start * BLOCK, WINDOW * BLOCK, 0)
    tags = tags.reshape(WINDOW, BLOCK)
    first, last = tags[:, 0], tags[:, BLOCK - 1]
    of_first = jnp.sum((tags == first[:, None]).astype(jnp.int32), axis=1)
    before_last = jnp.sum((tags < last[:, None]).astype(jnp.int32), axis=1)
    stats = jnp.concatenate([start[None].astype(jnp.int32), first, last, of_first, before_last])

    units, own_best = local_pairs(place, listing, stats, tags, embeddings)
    mine = (jnp.arange(2) == core)[:, None, None]
    best = jnp.where(mine, own_best[None], -1.0)
    best = cross_pairs(False, block_count, place, listing, stats, best, units, chip_in)
    best, returned = cross_pairs(
        True, block_count, place, listing, stats, best, units, chip_in, far_in
    )

    back = lax.ppermute(returned, "shard", across)
    has_far = (shard > 0) & (shard < count - 1)
    back = jnp.where(has_far, back, -1.0)
    blocks = jnp.arange(OWN)[None, :, None]
    for which in range(2):
        target = far_local(core, far_index(rep, which))
        best = jnp.maximum(best, jnp.where(mine & (blocks == target), back[which], -1.0))
    outgoing = jnp.broadcast_to(best[:, None], (2, REPS, OWN, BLOCK)).reshape(-1, OWN, BLOCK)
    groups = [list(range(c * 2 * REPS, (c + 1) * 2 * REPS)) for c in range(count // 2)]
    parts = lax.all_to_all(outgoing, ("shard", "rep"), 0, 0, axis_index_groups=groups)
    return jnp.max(parts, axis=0).reshape(OWN * BLOCK)


def solution(mesh):
    return jax.shard_map(
        shards,
        mesh=mesh,
        in_specs=(P("shard", None), P(), P("shard", None)),
        out_specs=P("shard"),
        check_vma=False,
    )
```

time: 537 us -> 54.3 us (0.10)
  the two profiles are of different devices: /device:TPU:7 before, /device:TPU:3 now
where the time goes in v1:
time: 54.3 us
  Pallas kernels  23.2 us (43%)
  blocking collectives  19 us (35%)
  starting transfers between devices  7.27 us (13%)
  local copies, waits for them, and re-layouts  2.46 us (5%)
  waiting for transfers between devices  1.76 us (3%)
    all_to_all x1, blocking collectives, shards(): lax.all_to_all(outgoing, ('shard', 'rep'), 0, 0, axis_index_groups=groups)  19 us
    pallas_call x1, Pallas kernels, local_pairs(): pl.pallas_call(local_kernel, out_shape=(jax.ShapeDtypeStruct((OWN * BLOCK...  8.91 us
    pallas_call x2, Pallas kernels, cross_pairs(): pl.pallas_call(functools.partial(cross_kernel, far, block_count), out_sha...  8.7 us
    pallas_call x1, Pallas kernels, send_payloads(): pl.pallas_call(send_kernel, out_shape=(jax.ShapeDtypeStruct((FAR_SLOTS *...  5.61 us
    ppermute x1, starting transfers between devices, shards(): far_in = lax.ppermute(far_out, 'shard', across)  3.44 us
    ppermute x1, starting transfers between devices, shards(): back = lax.ppermute(returned, 'shard', across)  3.06 us
    ppermute x1, waiting for transfers between devices, shards(): back = lax.ppermute(returned, 'shard', across)  1.76 us
  transfers between devices with their start and end apart: 3, of which 1 were waited for; matrix products, arithmetic and copies ran while one was open for 3% of the time, Pallas kernels for 24%

profile of v1, /device:TPU:3, one launch (start us, length us, event | category | flops | bytes accessed | tf_op | source)
XLA Modules:
  0.0 54.3 jit_solution(11711319119120753170)
XLA Ops:
  0.0 0.1 pad_add_fusion.place
  0.1 0.0 copy-start
  0.1 0.7 %copy-done = s32[204,1]{0,1:T(1,128)S(1)} copy-done((s32[204,1]{0,1:T(1,128)S(1)}, s32[204,1]{0,1:T(1,128)}, u32[]{:S(2)}) %copy-start) | copy-done | bytes 840
  0.8 0.0 copy-start.1
  0.8 5.6 %send_rows.1 = (bf16[528,1024]{1,0:T(8,128)(2,1)}, bf16[1296,1024]{1,0:T(8,128)(2,1)}) custom-call(s32[2]{0:T(128)S(1)} %pad_add_fusion.place, s32[204]{0:T(256)S(1)} %bitcast.7, f32[3072,1024]{1,0:T(8,128)} %emb.3), custom_call_target="tpu_custom_call" | custom-call | tf_op jit(solution)/shard_map/send_rows/pallas_call | solution.py:129
  6.4 0.8 %collective-permute-start = (bf16[1296,1024]{1,0:T(8,128)(2,1)}, bf16[1296,1024]{1,0:T(8,128)(2,1)S(1)}, u32[]{:S(2)}, u32[]{:S(2)}) collective-permute-start(bf16[1296,1024]{1,0:T(8,128)(2,1)} %get-tuple-element.13), channel_id=1, source_target_pairs={{0,4},{4,0},{8,12},{12,8},{16,20},{20,16},{24,28},{28,24},{32,36},... | collective-permute-start | bytes 7962632 | tf_op jit(solution)/shard_map/ppermute | solution.py:446
  7.1 3.4 %collective-permute-start.1 = (bf16[528,1024]{1,0:T(8,128)(2,1)}, bf16[528,1024]{1,0:T(8,128)(2,1)}, u32[]{:S(2)}, u32[]{:S(2)}) collective-permute-start(bf16[528,1024]{1,0:T(8,128)(2,1)} %get-tuple-element.14), channel_id=1, source_target_pairs={{4,8},{12,16},{20,24},{28,32},{36,40},{44,48},{52,56},{60,64},{68,... | collective-permute-start | bytes 3244040 | tf_op jit(solution)/shard_map/ppermute | solution.py:445
  10.6 0.9 %dynamic_slice.3 = s32[11264]{0:T(1024)S(1)} dynamic-slice(s32[196608]{0:T(1024)} %param.4, s32[]{:T(128)S(6)} %select_n.38), dynamic_slice_sizes={11264} | dynamic-slice | bytes 90116 | tf_op jit(solution)/shard_map/dynamic_slice | solution.py:449
  11.5 0.2 slice_reduce_fusion
  11.7 0.2 convert_reduce_fusion
  11.9 0.1 concatenate.3.stats
  12.0 0.0 copy-done.1
  12.0 8.9 %local_pairs.1 = (bf16[3072,1024]{1,0:T(8,128)(2,1)}, f32[12,256]{1,0:T(8,128)S(1)}) custom-call(s32[2]{0:T(128)S(1)} %pad_add_fusion.place, s32[204]{0:T(256)S(1)} %bitcast.8, s32[177]{0:T(256)S(1)} %concatenate.3.stats, s32[44,256]{1,0:T(8,128)S(1)} %reshape.85.tags, f32[3072,1024]{1,0:T(8,128)} %emb.3), custom_call_target="tpu_custom_call" | custom-call | flops 2684354560 | bytes 18874368 | tf_op jit(solution)/shard_map/local_pairs/pallas_call | solution.py:256
  20.9 0.1 broadcast_select_fusion.best_in
  21.0 0.0 collective-permute-done.chip_hbm
  21.0 4.3 %chip_pairs.1.best_in = f32[2,12,256]{2,1,0:T(8,128)S(1)} custom-call(s32[2]{0:T(128)S(1)} %pad_add_fusion.place, s32[204]{0:T(256)S(1)} %bitcast.9, s32[177]{0:T(256)S(1)} %concatenate.3.stats, f32[2,12,256]{2,1,0:T(8,128)S(1)} %broadcast_select_fusion.best_in, bf16[3072,1024]{1,0:T(8,128)(2,1)} %get-tuple-element.12.units_hbm, ...), custom_call_target="tpu_custom_call" | custom-call | flops 1879048192 | bytes 9437184 | tf_op jit(solution)/shard_map/chip_pairs/pallas_call | solution.py:407
  25.3 0.0 collective-permute-done.1.rest_0_
  25.3 4.4 %far_pairs.1 = (f32[2,12,256]{2,1,0:T(8,128)S(1)}, f32[2,256]{1,0:T(2,128)S(1)}) custom-call(s32[2]{0:T(128)S(1)} %pad_add_fusion.place, s32[204]{0:T(256)S(1)} %bitcast.10, s32[177]{0:T(256)S(1)} %concatenate.3.stats, f32[2,12,256]{2,1,0:T(8,128)S(1)} %chip_pairs.1.best_in, bf16[3072,1024]{1,0:T(8,128)(2,1)} %get-tuple-element.12.units_hbm, ...), custom_call_target="tpu_custom_call" | custom-call | flops 1879048192 | bytes 9437184 | tf_op jit(solution)/shard_map/far_pairs/pallas_call | solution.py:407
  29.7 3.1 %collective-permute-start.2 = (f32[2,256]{1,0:T(2,128)S(1)}, f32[2,256]{1,0:T(2,128)S(1)}, u32[]{:S(2)}, u32[]{:S(2)}) collective-permute-start(f32[2,256]{1,0:T(2,128)S(1)} %get-tuple-element.16), channel_id=1, source_target_pairs={{4,8},{12,16},{20,24},{28,32},{36,40},{44,48},{52,56},{60,64},{68,... | collective-permute-start | bytes 6152 | tf_op jit(solution)/shard_map/ppermute | solution.py:464
  32.8 0.1 broadcast_and_fusion.1
  32.9 1.8 %collective-permute-done.2 = f32[2,256]{1,0:T(2,128)S(1)} collective-permute-done((f32[2,256]{1,0:T(2,128)S(1)}, f32[2,256]{1,0:T(2,128)S(1)}, u32[]{:S(2)}, u32[]{:S(2)}) %collective-permute-start.2) | collective-permute-done | bytes 2080 | tf_op jit(solution)/shard_map/ppermute | solution.py:464
  34.7 0.1 select_maximum_fusion
  34.8 19.0 %all_to_all.5 = f32[8,12,256]{2,1,0:T(8,128)S(1)} all-to-all(f32[8,12,256]{2,1,0:T(8,128)S(1)} %bitcast.11), channel_id=1, replica_groups={{0,1,2,3,4,5,6,7},{8,9,10,11,12,13,14,15},{16,17,18,19,20,21,22,23},{24..., dimensions={0} | all-to-all | bytes 196608 | tf_op jit(solution)/shard_map/all_to_all | solution.py:473
  53.7 0.6 %reshape.87 = f32[3072]{0:T(1024)} reshape(f32[12,256]{1,0:T(8,128)S(1)} %reduce_max.9) | data formatting | bytes 24576 | tf_op jit(solution)/shard_map/reshape | solution.py:474
  (7 shorter events, 0.1 us)
Async XLA Ops:
  0.1 0.7 %copy-start = (s32[204,1]{0,1:T(1,128)S(1)}, s32[204,1]{0,1:T(1,128)}, u32[]{:S(2)}) copy-start(s32[204,1]{0,1:T(1,128)} %param.5) | copy-start | bytes 2452
  0.8 11.3 %copy-start.1 = (s32[204,1]{0,1:T(1,128)S(1)}, s32[204,1]{0,1:T(1,128)}, u32[]{:S(2)}) copy-start(s32[204,1]{0,1:T(1,128)} %param.5) | copy-start | bytes 2452
  6.4 14.6 %collective-permute-start = (bf16[1296,1024]{1,0:T(8,128)(2,1)}, bf16[1296,1024]{1,0:T(8,128)(2,1)S(1)}, u32[]{:S(2)}, u32[]{:S(2)}) collective-permute-start(bf16[1296,1024]{1,0:T(8,128)(2,1)} %get-tuple-element.13), channel_id=1, source_target_pairs={{0,4},{4,0},{8,12},{12,8},{16,20},{20,16},{24,28},{28,24},{32,36},... | collective-permute-start | bytes 7962632 | tf_op jit(solution)/shard_map/ppermute | solution.py:446
  7.1 18.2 %collective-permute-start.1 = (bf16[528,1024]{1,0:T(8,128)(2,1)}, bf16[528,1024]{1,0:T(8,128)(2,1)}, u32[]{:S(2)}, u32[]{:S(2)}) collective-permute-start(bf16[528,1024]{1,0:T(8,128)(2,1)} %get-tuple-element.14), channel_id=1, source_target_pairs={{4,8},{12,16},{20,24},{28,32},{36,40},{44,48},{52,56},{60,64},{68,... | collective-permute-start | bytes 3244040 | tf_op jit(solution)/shard_map/ppermute | solution.py:445
  29.7 4.9 %collective-permute-start.2 = (f32[2,256]{1,0:T(2,128)S(1)}, f32[2,256]{1,0:T(2,128)S(1)}, u32[]{:S(2)}, u32[]{:S(2)}) collective-permute-start(f32[2,256]{1,0:T(2,128)S(1)} %get-tuple-element.16), channel_id=1, source_target_pairs={{4,8},{12,16},{20,24},{28,32},{36,40},{44,48},{52,56},{60,64},{68,... | collective-permute-start | bytes 6152 | tf_op jit(solution)/shard_map/ppermute | solution.py:464

commit v2 on v0

v2 whole, which is shorter than its diff:
```python
import functools

import jax
import jax.numpy as jnp
from jax import lax
from jax.experimental import pallas as pl
from jax.experimental.pallas import tpu as pltpu
from jax.sharding import PartitionSpec as P

BLOCK = 256
SPANS = 17
WIDTH = 1024
OWN = 12
REPS = 4
CHIP_SLOTS = 4
FAR_SLOTS = 2
TAIL = 16
FAR_ROWS = FAR_SLOTS * BLOCK + 2 * TAIL
CHIP_ROWS = 2 * BLOCK + TAIL
EXTRA_ROWS = 2 * BLOCK
WINDOW = OWN + 2 * (SPANS - 1)
GROUP = 8 * 128 // BLOCK
CHUNK = 64
BATCH = 4
FIELDS = 8
EPS = 1e-6
VMEM_LIMIT = 20 * 1024 * 1024

HBM = pl.BlockSpec(memory_space=pltpu.HBM)
ANY = pl.BlockSpec(memory_space=pl.ANY)
SMEM = pl.BlockSpec(memory_space=pltpu.SMEM)
VMEM = pl.BlockSpec(memory_space=pltpu.VMEM)


def cost(us):
    return pl.CostEstimate(flops=0, bytes_accessed=us * 3_000_000, transcendentals=0)


PARAMS = pltpu.CompilerParams(vmem_limit_bytes=VMEM_LIMIT)


def rows_of(slot, count=BLOCK):
    return pl.ds(pl.multiple_of(slot * BLOCK, BLOCK), count)


def unit_rows(rows):
    squares = jnp.sum(rows * rows, axis=1, keepdims=True)
    return (rows * lax.rsqrt(squares + EPS)).astype(jnp.bfloat16)


def normalise(raw, raw_slot, out, out_slot):
    for step in range(BLOCK // CHUNK):
        source = pl.ds(pl.multiple_of(raw_slot * BLOCK + step * CHUNK, CHUNK), CHUNK)
        target = pl.ds(pl.multiple_of(out_slot * BLOCK + step * CHUNK, CHUNK), CHUNK)
        out[target, :] = unit_rows(raw[source, :])


def far_local(core, m):
    return jnp.where(core == 0, m - 1, OWN - m)


def chip_local(core, m):
    return jnp.where(core == 0, OWN - m, m - 1)


def far_index(rep, slot):
    return jnp.where(slot == 0, rep + 1, 8 - rep)


CHIP_INDEX = ((3, 4, 1, 2), (2, 7, 1, 3), (5, 6, 1, 2), (1, 8, 2, 3))


def chip_index(rep, slot):
    picked = jnp.int32(CHIP_INDEX[REPS - 1][slot])
    for other in range(REPS - 1):
        picked = jnp.where(rep == other, CHIP_INDEX[other][slot], picked)
    return picked


def flag_rows(holder, locals_of_slots):
    lane = lax.broadcasted_iota(jnp.int32, (TAIL, 128), 1)
    row = lax.broadcasted_iota(jnp.int32, (TAIL, 128), 0)
    flags = jnp.zeros((TAIL, 128), jnp.float32)
    for slot, local in enumerate(locals_of_slots):
        for k in range(SPANS):
            listed = jnp.where(holder[local * SPANS + k] != REPS, 1.0, 0.0)
            flags = jnp.where((row == slot) & (lane == k), listed, flags)
    return flags.astype(jnp.bfloat16)


def far_rows_kernel(place, holder_hbm, emb, far_out, raw, holder, sems, holder_sem):
    core, rep = place[0] % 2, place[1]
    local = [far_local(core, far_index(rep, slot)) for slot in range(FAR_SLOTS)]
    listing = pltpu.make_async_copy(holder_hbm, holder, holder_sem)
    listing.start()
    fetches = [
        pltpu.make_async_copy(emb.at[rows_of(local[slot])], raw.at[rows_of(slot)], sems.at[slot])
        for slot in range(FAR_SLOTS)
    ]
    for fetch in fetches:
        fetch.start()
    far_out[FAR_SLOTS * BLOCK :, :] = jnp.zeros((2 * TAIL, WIDTH), jnp.bfloat16)
    listing.wait()
    far_out[pl.ds(FAR_SLOTS * BLOCK, TAIL), 0:128] = flag_rows(holder, local)
    for slot in range(FAR_SLOTS):
        fetches[slot].wait()
        normalise(raw, slot, far_out, slot)


def far_rows(place, holder, emb):
    return pl.pallas_call(
        far_rows_kernel,
        out_shape=pltpu.VMEM((FAR_ROWS, WIDTH), jnp.bfloat16),
        in_specs=[SMEM, HBM, HBM],
        out_specs=VMEM,
        scratch_shapes=[
            pltpu.VMEM((FAR_SLOTS * BLOCK, WIDTH), jnp.float32),
            pltpu.SMEM(holder.shape, jnp.int32),
            pltpu.SemaphoreType.DMA((FAR_SLOTS,)),
            pltpu.SemaphoreType.DMA,
        ],
        compiler_params=PARAMS,
        cost_estimate=cost(1),
        name="far_rows",
    )(place, pltpu.with_memory_space_constraint(holder, pltpu.HBM), emb)


def similarity(left, right):
    return lax.dot_general(
        left, right, (((1,), (1,)), ((), ())), preferred_element_type=jnp.float32
    )


def inside(scored, row_low, row_end, col_low, col_end):
    rows = lax.broadcasted_iota(jnp.int32, (BLOCK, BLOCK), 0)
    cols = lax.broadcasted_iota(jnp.int32, (BLOCK, BLOCK), 1)
    keep = (rows >= row_low) & (rows < row_end) & (cols >= col_low) & (cols < col_end)
    return jnp.where(keep, scored, -1.0)


def fold_rows(scored):
    return jnp.maximum(scored[:, 0:128], scored[:, 128:256])


def fold_cols(scored):
    return jnp.max(scored.reshape(BLOCK // 8, 8, BLOCK), axis=0)


def as_lanes(column):
    rows = lax.broadcasted_iota(jnp.int32, (BLOCK, BLOCK), 0)
    cols = lax.broadcasted_iota(jnp.int32, (BLOCK, BLOCK), 1)
    return jnp.max(jnp.where(rows == cols, column, -1.0), axis=0, keepdims=True)


def first_group(shard, block_count):
    own = OWN // GROUP
    return jnp.clip(
        shard * own - (SPANS - 1) // GROUP, 0, (block_count - WINDOW) // GROUP
    )


def label_stats(stats, block_count, shard, block):
    slot = jnp.clip(block - first_group(shard, block_count) * GROUP, 0, WINDOW - 1)
    return [stats[part, slot] for part in range(4)]


def write_stats(tags, table):
    halves = [tags[pl.ds(half, WINDOW, stride=2), :].astype(jnp.float32) for half in range(2)]
    first, last = halves[0][:, 0:1], halves[1][:, 127:128]
    of_first = sum(jnp.where(half == first, 1.0, 0.0) for half in halves)
    before_last = sum(jnp.where(half < last, 1.0, 0.0) for half in halves)
    columns = [
        first,
        last,
        jnp.sum(of_first, axis=1, keepdims=True),
        jnp.sum(before_last, axis=1, keepdims=True),
    ]
    lane = lax.broadcasted_iota(jnp.int32, (WINDOW, 128), 1)
    spread = jnp.zeros((WINDOW, 128), jnp.float32)
    for part, column in enumerate(columns):
        spread = jnp.where(lane == part, column, spread)
    spread = jnp.concatenate([spread, jnp.zeros((128 - WINDOW, 128), jnp.float32)], axis=0)
    table[...] = spread.T[0:8, :].astype(jnp.int32)


def put_task(tasks, count, active, *fields):
    for place, field in enumerate(fields):
        tasks[count * FIELDS + place] = field
    return count + active.astype(jnp.int32)


def run_tasks(tasks, count, left, right, row_acc, col_acc):
    for extra in range(BATCH - 1):
        for field in range(FIELDS):
            tasks[(count + extra) * FIELDS + field] = 0

    @pl.loop(0, (count + BATCH - 1) // BATCH)
    def _(step):
        found = []
        for lane in range(BATCH):
            base = (step * BATCH + lane) * FIELDS
            task = [tasks[base + field] for field in range(FIELDS)]
            scored = similarity(left[rows_of(task[0]), :], right[rows_of(task[1]), :])
            scored = inside(scored, *task[2:6])
            found.append((task[6], task[7], fold_rows(scored), fold_cols(scored)))
        for row_slot, col_slot, rows, cols in found:
            row_acc[row_slot] = jnp.maximum(row_acc[row_slot], rows)
            col_acc[col_slot] = jnp.maximum(col_acc[col_slot], cols)


def task_scratch(most):
    return pltpu.SMEM(((most + BATCH) * FIELDS,), jnp.int32)


def local_class(rep, turn):
    return (rep, 7 - rep, 8 + rep)[turn]


def own_kernel(
    block_count, place, holder, labels, far, emb,
    units, chip_out, extra_out, best, stats,
    raw, tags, table, row_acc, col_acc, tasks, sems, out_sems, tag_sem, table_sem,
):
    shard, rep = place[0], place[1]
    core = lax.rem(shard, 2)
    first_block = shard * OWN
    group = first_group(shard, block_count)

    def fetch(block):
        return pltpu.make_async_copy(
            emb.at[rows_of(block)], raw.at[rows_of(block)], sems.at[block]
        )

    rows = pl.ds(pl.multiple_of(group * 8, 8), WINDOW * 2)
    fetch_tags = pltpu.make_async_copy(labels.at[rows], tags, tag_sem)
    fetch_tags.start()

    @pl.loop(1, OWN + 1)
    def _(m):
        fetch(chip_local(core, m)).start()

    local = [chip_local(core, chip_index(rep, slot)) for slot in range(CHIP_SLOTS)]
    chip_out[2 * BLOCK :, :] = jnp.zeros((TAIL, WIDTH), jnp.bfloat16)
    chip_out[2 * BLOCK :, 0:128] = flag_rows(holder, local)
    col_acc[...] = jnp.full(col_acc.shape, -1.0, jnp.float32)
    row_acc[...] = jnp.full(row_acc.shape, -1.0, jnp.float32)
    fetch_tags.wait()
    write_stats(tags, table)
    to_scalars = pltpu.make_async_copy(table, stats, table_sem)
    to_scalars.start()
    to_scalars.wait()

    def label_facts(block):
        return label_stats(stats, block_count, shard, first_block + block)

    def diagonal(block):
        at = (first_block + block - group * GROUP) * 2
        tag_row = jnp.concatenate([tags[pl.ds(at, 1), :], tags[pl.ds(at + 1, 1), :]], axis=1)
        tag_row = tag_row.astype(jnp.float32)
        rows = lax.broadcasted_iota(jnp.int32, (BLOCK, BLOCK), 0)
        cols = lax.broadcasted_iota(jnp.int32, (BLOCK, BLOCK), 1)
        spread = jnp.broadcast_to(tag_row, (BLOCK, BLOCK))
        tag_col = jnp.max(jnp.where(rows == cols, spread, -1.0), axis=1, keepdims=True)
        scored = similarity(units[rows_of(block), :], units[rows_of(block), :])
        keep = (tag_col == tag_row) & (rows != cols)
        found = fold_cols(jnp.where(keep, scored, -1.0))
        found = jnp.where(holder[block * SPANS] != REPS, found, -1.0)
        col_acc[block] = jnp.maximum(col_acc[block], found)

    def push(slot):
        target = (chip_out, extra_out)[slot // 2]
        return pltpu.make_async_copy(
            units.at[rows_of(local[slot])], target.at[rows_of(slot % 2)], out_sems.at[slot]
        )

    for phase in range(3):

        @pl.loop(4 * phase + 1, 4 * phase + 5)
        def _(m):
            block = chip_local(core, m)
            fetch(block).wait()
            normalise(raw, block, units, block)
            mine = block == local_class(rep, 0)
            for turn in range(1, 3):
                mine = mine | (block == local_class(rep, turn))
            pl.when(mine)(functools.partial(diagonal, block))

        if phase == 1:
            for slot in range(CHIP_SLOTS):
                push(slot).start()
        low = OWN - 4 - 4 * phase
        count = jnp.int32(0)
        for turn in range(3):
            if turn != phase and turn < 2 - phase:
                continue
            block = local_class(rep, turn)
            b_first, _, b_count, _ = label_facts(block)

            def visit(other, count, block=block, turn=turn, b_first=b_first, b_count=b_count):
                _, a_last, _, a_start = label_facts(other)
                listed = holder[other * SPANS + (block - other)] != REPS
                return put_task(
                    tasks, count, listed & (a_last == b_first),
                    block, other, 0, b_count, a_start, BLOCK, turn, other,
                )

            begin_0 = low if turn >= 2 - phase else 0
            end_0 = jnp.minimum(block, low + 4) if turn >= 2 - phase else 0
            end_1 = block if turn == phase else 0
            begin = jnp.where(core == 0, begin_0, 0)
            end = jnp.where(core == 0, end_0, end_1)
            count = lax.fori_loop(begin, end, visit, count)
        run_tasks(tasks, count, units, units, row_acc, col_acc)

    best[...] = jnp.max(col_acc[...], axis=1)
    for turn in range(3):
        here = (pl.ds(local_class(rep, turn), 1), slice(None))
        found = as_lanes(jnp.max(row_acc[turn], axis=1, keepdims=True))
        best[here] = jnp.maximum(best[here], found)
    for slot in range(CHIP_SLOTS):
        push(slot).wait()


def own_pairs(block_count, place, holder, labels, far, emb):
    return pl.pallas_call(
        functools.partial(own_kernel, block_count),
        out_shape=(
            pltpu.VMEM((OWN * BLOCK, WIDTH), jnp.bfloat16),
            pltpu.VMEM((CHIP_ROWS, WIDTH), jnp.bfloat16),
            pltpu.VMEM((EXTRA_ROWS, WIDTH), jnp.bfloat16),
            pltpu.VMEM((OWN, BLOCK), jnp.float32),
            jax.ShapeDtypeStruct((8, 128), jnp.int32),
        ),
        in_specs=[SMEM, SMEM, HBM, ANY, HBM],
        out_specs=(VMEM, VMEM, VMEM, VMEM, SMEM),
        scratch_shapes=[
            pltpu.VMEM((OWN * BLOCK, WIDTH), jnp.float32),
            pltpu.VMEM((WINDOW * 2, 128), jnp.int32),
            pltpu.VMEM((8, 128), jnp.int32),
            pltpu.VMEM((3, BLOCK, 128), jnp.float32),
            pltpu.VMEM((OWN, 8, BLOCK), jnp.float32),
            task_scratch(3 * 4),
            pltpu.SemaphoreType.DMA((OWN,)),
            pltpu.SemaphoreType.DMA((CHIP_SLOTS,)),
            pltpu.SemaphoreType.DMA,
            pltpu.SemaphoreType.DMA,
        ],
        compiler_params=PARAMS,
        cost_estimate=cost(6),
        name="own_pairs",
    )(place, holder, labels, far, emb)


def flag_bits(tail, slot):
    lane = lax.broadcasted_iota(jnp.int32, (TAIL, 128), 1)
    row = lax.broadcasted_iota(jnp.int32, (TAIL, 128), 0)
    weight = lax.shift_left(jnp.int32(1), jnp.minimum(lane, SPANS)).astype(jnp.float32)
    weight = jnp.where((row == slot) & (lane < SPANS), weight, 0.0)
    return jnp.sum(tail[:, 0:128].astype(jnp.float32) * weight).astype(jnp.int32)


class Boundary:
    def __init__(self, far, block_count, place, stats):
        self.far, self.block_count, self.stats = far, block_count, stats
        self.shard, self.rep = place[0], place[1]
        self.core = lax.rem(self.shard, 2)
        self.side = self.core if far else 1 - self.core
        self.tie = 1 - self.side

    def local(self, m):
        return far_local(self.core, m) if self.far else chip_local(self.core, m)

    def near(self, which):
        return far_index(self.rep, which) if self.far else chip_index(self.rep, which)

    def pair(self, which, m, moved_bits, column_flag):
        near = self.near(which)
        first_block = self.shard * OWN
        before = self.side == 0
        moved_block = jnp.where(before, first_block - near, first_block + OWN - 1 + near)
        column_block = jnp.where(before, first_block + m - 1, first_block + OWN - m)
        offset = near + m - 1
        wanted = (m > near) | ((m == near) & (lax.rem(near, 2) == self.tie))
        wanted = wanted & (offset < SPANS)
        wanted = wanted & (moved_block >= 0) & (moved_block < self.block_count)
        offset = jnp.minimum(offset, SPANS - 1)
        moved_flag = lax.rem(lax.shift_right_logical(moved_bits, offset), 2) == 1
        listed = jnp.where(before, moved_flag, column_flag(offset))
        facts = functools.partial(label_stats, self.stats, self.block_count, self.shard)
        m_first, m_last, m_count, m_start = facts(moved_block)
        c_first, c_last, c_count, c_start = facts(column_block)
        shared = jnp.where(before, m_last == c_first, c_last == m_first)
        return wanted & listed & shared, (
            jnp.where(before, m_start, 0), jnp.where(before, BLOCK, m_count),
            jnp.where(before, 0, c_start), jnp.where(before, c_count, BLOCK),
        )

    def own_tasks(self, tasks, holder, moved_bits):
        count = jnp.int32(0)
        for which in range(2):

            def visit(m, count, which=which):
                column = self.local(m)

                def flag(offset):
                    return holder[column * SPANS + offset] != REPS

                active, area = self.pair(which, m, moved_bits[which], flag)
                return put_task(tasks, count, active, which, column, *area, which, column)

            count = lax.fori_loop(self.near(which), OWN + 1, visit, count)
        return count


def far_kernel(
    block_count, place, holder, stats, best, units, far, mine, returned, row_acc, col_acc, tasks
):
    edge = Boundary(True, block_count, place, stats)
    col_acc[...] = jnp.full(col_acc.shape, -1.0, jnp.float32)
    row_acc[...] = jnp.full(row_acc.shape, -1.0, jnp.float32)
    tail = far[pl.ds(FAR_SLOTS * BLOCK, TAIL), :]
    bits = [flag_bits(tail, slot) for slot in range(2)]
    count = edge.own_tasks(tasks, holder, bits)
    run_tasks(tasks, count, far, units, row_acc, col_acc)
    mine[...] = jnp.maximum(best[...], jnp.max(col_acc[...], axis=1))
    for which in range(2):
        returned[which : which + 1, :] = as_lanes(
            jnp.max(row_acc[which], axis=1, keepdims=True)
        )


def bridge_kernel(block_count, place, stats, found, far, chip, extra, returned, other):
    edge = Boundary(True, block_count, place, stats)
    returned[...] = found[...]
    other[...] = jnp.full(other.shape, -1.0, jnp.float32)
    far_bits = flag_bits(far[pl.ds(FAR_SLOTS * BLOCK, TAIL), :], 0)
    tail = chip[pl.ds(2 * BLOCK, TAIL), :]
    pairs = []
    for slot in range(CHIP_SLOTS):
        bits = flag_bits(tail, slot)

        def flag(offset, bits=bits):
            return lax.rem(lax.shift_right_logical(bits, offset), 2) == 1

        pairs.append(edge.pair(0, OWN + chip_index(edge.rep, slot), far_bits, flag))
    some = pairs[0][0]
    for active, _ in pairs[1:]:
        some = some | active

    @pl.when(some)
    def _():
        rows, cols = [], []
        for slot, (active, area) in enumerate(pairs):
            column = (chip, extra)[slot // 2][rows_of(slot % 2), :]
            scored = inside(similarity(far[0:BLOCK, :], column), *area)
            scored = jnp.where(active, scored, -1.0)
            rows.append(fold_rows(scored))
            cols.append(fold_cols(scored))
        for slot in range(CHIP_SLOTS):
            block = chip_local(1 - edge.core, chip_index(edge.rep, slot))
            other[pl.ds(block, 1), :] = jnp.max(cols[slot], axis=0, keepdims=True)
        best = functools.reduce(jnp.maximum, rows)
        best = as_lanes(jnp.max(best, axis=1, keepdims=True))
        returned[0:1, :] = jnp.maximum(returned[0:1, :], best)


def chip_kernel(
    block_count, place, holder, stats, mine_in, other_in, units, chip,
    mine, other, row_acc, col_acc, tasks,
):
    edge = Boundary(False, block_count, place, stats)
    col_acc[...] = jnp.full(col_acc.shape, -1.0, jnp.float32)
    row_acc[...] = jnp.full(row_acc.shape, -1.0, jnp.float32)
    tail = chip[pl.ds(2 * BLOCK, TAIL), :]
    bits = [flag_bits(tail, slot) for slot in range(2)]
    count = edge.own_tasks(tasks, holder, bits)
    run_tasks(tasks, count, chip, units, row_acc, col_acc)
    mine[...] = jnp.maximum(mine_in[...], jnp.max(col_acc[...], axis=1))
    other[...] = other_in[...]
    for which in range(2):
        here = (pl.ds(chip_local(1 - edge.core, edge.near(which)), 1), slice(None))
        found = as_lanes(jnp.max(row_acc[which], axis=1, keepdims=True))
        other[here] = jnp.maximum(other[here], found)


BEST = pltpu.VMEM((OWN, BLOCK), jnp.float32)
RETURNED = pltpu.VMEM((2, BLOCK), jnp.float32)


def pair_call(kernel, name, us, outs, scalars, scratch, args):
    return pl.pallas_call(
        kernel,
        out_shape=outs,
        in_specs=[SMEM] * scalars + [VMEM] * (len(args) - scalars),
        out_specs=(VMEM,) * len(outs),
        scratch_shapes=scratch,
        compiler_params=PARAMS,
        cost_estimate=cost(us),
        name=name,
    )(*args)


PAIR_SCRATCH = [
    pltpu.VMEM((2, BLOCK, 128), jnp.float32),
    pltpu.VMEM((OWN, 8, BLOCK), jnp.float32),
    task_scratch(2 * OWN),
]


def finish_kernel(block_count, place, mine, other, back, outgoing, merged):
    shard, rep = place[0], place[1]
    core = lax.rem(shard, 2)
    has_far = (shard > 0) & (shard < block_count // OWN - 1)
    merged[...] = mine[...]
    for which in range(2):
        here = (pl.ds(far_local(core, far_index(rep, which)), 1), slice(None))
        found = jnp.where(has_far, back[which : which + 1, :], -1.0)
        merged[here] = jnp.maximum(merged[here], found)
    for target in range(2):
        share = jnp.where(core == target, merged[...], other[...])
        for copy in range(REPS):
            outgoing[target * REPS + copy] = share


def finish(block_count, place, mine, other, back):
    return pl.pallas_call(
        functools.partial(finish_kernel, block_count),
        out_shape=jax.ShapeDtypeStruct((2 * REPS, OWN, BLOCK), jnp.float32),
        in_specs=[SMEM, VMEM, VMEM, VMEM],
        out_specs=VMEM,
        scratch_shapes=[pltpu.VMEM((OWN, BLOCK), jnp.float32)],
        compiler_params=PARAMS,
        cost_estimate=cost(1),
        name="finish",
    )(place, mine, other, back)


def shards(embeddings, labels, holder):
    count = lax.axis_size("shard")
    block_count = count * OWN
    place = jnp.stack([lax.axis_index("shard"), lax.axis_index("rep")]).astype(jnp.int32)
    listing = holder.reshape(-1)
    labels = pltpu.with_memory_space_constraint(labels.reshape(-1, 128), pltpu.HBM)
    embeddings = pltpu.with_memory_space_constraint(embeddings, pltpu.HBM)
    across = [(s, s + 1) for s in range(1, count - 1, 2)]
    across = across + [(b, a) for a, b in across]
    within = [(s, s ^ 1) for s in range(count)]

    def in_vmem(array):
        return pltpu.with_memory_space_constraint(array, pltpu.VMEM)

    far_out = far_rows(place, listing, embeddings)
    far_in = in_vmem(lax.ppermute(far_out, "shard", across))
    units, chip_out, extra_out, best, stats = own_pairs(
        block_count, place, listing, labels, far_out, embeddings
    )
    chip_in = in_vmem(lax.ppermute(chip_out, "shard", within))
    extra_in = in_vmem(lax.ppermute(extra_out, "shard", within))

    mine, found = pair_call(
        functools.partial(far_kernel, block_count), "far_pairs", 4, (BEST, RETURNED),
        3, PAIR_SCRATCH, (place, listing, stats, best, units, far_in),
    )
    returned, other = pair_call(
        functools.partial(bridge_kernel, block_count), "bridge_pairs", 1, (RETURNED, BEST),
        2, [], (place, stats, found, far_in, chip_in, extra_in),
    )
    back = lax.ppermute(returned, "shard", across)
    mine, other = pair_call(
        functools.partial(chip_kernel, block_count), "chip_pairs", 4, (BEST, BEST),
        3, PAIR_SCRATCH, (place, listing, stats, mine, other, units, chip_in),
    )
    outgoing = finish(block_count, place, mine, other, back)
    groups = [list(range(c * 2 * REPS, (c + 1) * 2 * REPS)) for c in range(count // 2)]
    parts = lax.all_to_all(outgoing, ("shard", "rep"), 0, 0, axis_index_groups=groups)
    return jnp.max(parts, axis=0).reshape(OWN * BLOCK)


def solution(mesh):
    return jax.shard_map(
        shards,
        mesh=mesh,
        in_specs=(P("shard", None), P(), P("shard", None)),
        out_specs=P("shard"),
        check_vma=False,
    )
```

time: 537 us -> 47.3 us (0.09)
  the two profiles are of different devices: /device:TPU:7 before, /device:TPU:3 now
where the time goes in v2:
time: 47.3 us; the launch traced here: 47.7 us
  Pallas kernels  17 us (36%)
  blocking collectives  15.9 us (34%)
  starting transfers between devices  11.7 us (25%)
  waiting for transfers between devices  2.29 us (5%)
  local copies, waits for them, and re-layouts  0.61 us (1%)
    all_to_all x1, blocking collectives, shards(): lax.all_to_all(outgoing, ('shard', 'rep'), 0, 0, axis_index_groups=groups)  15.9 us
    pallas_call x1, Pallas kernels, own_pairs(): pl.pallas_call(functools.partial(own_kernel, block_count), out_shape=(plt...  8.96 us
    ppermute x1, starting transfers between devices, shards(): chip_in = in_vmem(lax.ppermute(chip_out, 'shard', within))  5.59 us
    pallas_call x3, Pallas kernels, pair_call(): pl.pallas_call(kernel, out_shape=outs, in_specs=[SMEM] * scalars + [VMEM]...  5.21 us
    ppermute x1, starting transfers between devices, shards(): far_in = in_vmem(lax.ppermute(far_out, 'shard', across))  4.11 us
    pallas_call x1, Pallas kernels, far_rows(): pl.pallas_call(far_rows_kernel, out_shape=pltpu.VMEM((FAR_ROWS, WIDTH), j...  2.28 us
    ppermute x1, starting transfers between devices, shards(): back = lax.ppermute(returned, 'shard', across)  1.92 us
    ppermute x1, waiting for transfers between devices, shards(): back = lax.ppermute(returned, 'shard', across)  1.26 us
  transfers between devices with their start and end apart: 4, of which 2 were waited for; matrix products, arithmetic and copies ran while one was open for 0% of the time, Pallas kernels for 28%

profile of v2, /device:TPU:3, one launch (start us, length us, event | category | flops | bytes accessed | tf_op | source)
XLA Modules:
  0.0 47.7 jit_solution(7669737883202794467)
XLA Ops:
  0.0 0.1 pad_add_fusion.place
  0.1 0.0 copy-start
  0.1 2.3 %far_rows.1.far = bf16[544,1024]{1,0:T(8,128)(2,1)S(1)} custom-call(s32[2]{0:T(128)S(1)} %pad_add_fusion.place, s32[204]{0:T(256)} %bitcast.4, f32[3072,1024]{1,0:T(8,128)} %emb.3), custom_call_target="tpu_custom_call" | custom-call | bytes 3000000 | tf_op jit(solution)/shard_map/far_rows/pallas_call | solution.py:111
  2.4 4.1 %collective-permute-start = (bf16[544,1024]{1,0:T(8,128)(2,1)S(1)}, bf16[544,1024]{1,0:T(8,128)(2,1)S(1)}, u32[]{:S(2)}, u32[]{:S(2)}) collective-permute-start(bf16[544,1024]{1,0:T(8,128)(2,1)S(1)} %far_rows.1.far), channel_id=1, source_target_pairs={{4,8},{12,16},{20,24},{28,32},{36,40},{44,48},{52,56},{60,64},{68,... | collective-permute-start | bytes 3342344 | tf_op jit(solution)/shard_map/ppermute | solution.py:553
  6.5 0.0 copy-done
  6.5 9.0 %own_pairs.1 = (bf16[3072,1024]{1,0:T(8,128)(2,1)S(1)}, bf16[528,1024]{1,0:T(8,128)(2,1)S(1)}, bf16[512,1024]{1,0:T(8,128)(2,1)S(1)}, f32[12,256]{1,0:T(8,128)S(1)}, s32[8,128]{1,0:T(8,128)S(1)}) custom-call(s32[2]{0:T(128)S(1)} %pad_add_fusion.place, s32[204]{0:T(256)S(1)} %bitcast.5, s32[1536,128]{1,0:T(8,128)} %bitcast.8, ...), custom_call_target="tpu_custom_call" | custom-call | bytes 18000000 | tf_op jit(solution)/shard_map/own_pairs/pallas_call | solution.py:325
  15.5 5.6 %collective-permute-start.1 = (bf16[528,1024]{1,0:T(8,128)(2,1)S(1)}, bf16[528,1024]{1,0:T(8,128)(2,1)S(1)}, u32[]{:S(2)}, u32[]{:S(2)}) collective-permute-start(bf16[528,1024]{1,0:T(8,128)(2,1)S(1)} %get-tuple-element.21), channel_id=1, source_target_pairs={{0,4},{4,0},{8,12},{12,8},{16,20},{20,16},{24,28},{28,24},{32,36},... | collective-permute-start | bytes 3244040 | tf_op jit(solution)/shard_map/ppermute | solution.py:557
  21.0 0.1 collective-permute-start.2
  21.1 0.0 collective-permute-done.far
  21.2 2.7 %far_pairs.1 = (f32[12,256]{1,0:T(8,128)S(1)}, f32[2,256]{1,0:T(2,128)S(1)}) custom-call(s32[2]{0:T(128)S(1)} %pad_add_fusion.place, s32[204]{0:T(256)S(1)} %bitcast.6, s32[8,128]{1,0:T(8,128)S(1)} %get-tuple-element.16.stats, f32[12,256]{1,0:T(8,128)S(1)} %get-tuple-element.17.best, bf16[3072,1024]{1,0:T(8,128)(2,1)S(1)} %get-tuple-element.18.units, ...), custom_call_target="tpu_custom_call" | custom-call | bytes 12000000 | tf_op jit(solution)/shard_map/far_pairs/pallas_call | solution.py:491
  23.9 1.0 %collective-permute-done.2.extra = bf16[512,1024]{1,0:T(8,128)(2,1)S(1)} collective-permute-done((bf16[512,1024]{1,0:T(8,128)(2,1)S(1)}, bf16[512,1024]{1,0:T(8,128)(2,1)S(1)}, u32[]{:S(2)}, u32[]{:S(2)}) %collective-permute-start.2) | collective-permute-done | bytes 1048608 | tf_op jit(solution)/shard_map/ppermute | solution.py:558
  24.9 0.0 collective-permute-done.1.chip
  24.9 0.8 %bridge_pairs.1 = (f32[2,256]{1,0:T(2,128)S(1)}, f32[12,256]{1,0:T(8,128)S(1)}) custom-call(s32[2]{0:T(128)S(1)} %pad_add_fusion.place, s32[8,128]{1,0:T(8,128)S(1)} %get-tuple-element.16.stats, f32[2,256]{1,0:T(2,128)S(1)} %get-tuple-element.20.found, bf16[544,1024]{1,0:T(8,128)(2,1)S(1)} %collective-permute-done.far, ...), custom_call_target="tpu_custom_call" | custom-call | bytes 3000000 | tf_op jit(solution)/shard_map/bridge_pairs/pallas_call | solution.py:491
  25.7 1.9 %collective-permute-start.3 = (f32[2,256]{1,0:T(2,128)S(1)}, f32[2,256]{1,0:T(2,128)S(1)}, u32[]{:S(2)}, u32[]{:S(2)}) collective-permute-start(f32[2,256]{1,0:T(2,128)S(1)} %get-tuple-element.26), channel_id=1, source_target_pairs={{4,8},{12,16},{20,24},{28,32},{36,40},{44,48},{52,56},{60,64},{68,... | collective-permute-start | bytes 6152 | tf_op jit(solution)/shard_map/ppermute | solution.py:568
  27.6 1.7 %chip_pairs.1 = (f32[12,256]{1,0:T(8,128)S(1)}, f32[12,256]{1,0:T(8,128)S(1)}) custom-call(s32[2]{0:T(128)S(1)} %pad_add_fusion.place, s32[204]{0:T(256)S(1)} %bitcast.7, s32[8,128]{1,0:T(8,128)S(1)} %get-tuple-element.16.stats, f32[12,256]{1,0:T(8,128)S(1)} %get-tuple-element.19.mine_in, f32[12,256]{1,0:T(8,128)S(1)} %get-tuple-element.23.other_in, ...), custom_call_target="tpu_custom_call" | custom-call | bytes 12000000 | tf_op jit(solution)/shard_map/chip_pairs/pallas_call | solution.py:491
  29.3 1.3 %collective-permute-done.3.back = f32[2,256]{1,0:T(2,128)S(1)} collective-permute-done((f32[2,256]{1,0:T(2,128)S(1)}, f32[2,256]{1,0:T(2,128)S(1)}, u32[]{:S(2)}, u32[]{:S(2)}) %collective-permute-start.3) | collective-permute-done | bytes 2080 | tf_op jit(solution)/shard_map/ppermute | solution.py:568
  30.6 0.6 %finish.1 = f32[8,12,256]{2,1,0:T(8,128)S(1)} custom-call(s32[2]{0:T(128)S(1)} %pad_add_fusion.place, f32[12,256]{1,0:T(8,128)S(1)} %get-tuple-element.24.mine, f32[12,256]{1,0:T(8,128)S(1)} %get-tuple-element.25.other, f32[2,256]{1,0:T(2,128)S(1)} %collective-permute-done.3.back), custom_call_target="tpu_custom_call" | custom-call | bytes 3000000 | tf_op jit(solution)/shard_map/finish/pallas_call | solution.py:526
  31.2 15.9 %all_to_all.5 = f32[8,12,256]{2,1,0:T(8,128)S(1)} all-to-all(f32[8,12,256]{2,1,0:T(8,128)S(1)} %finish.1), channel_id=1, replica_groups={{0,1,2,3,4,5,6,7},{8,9,10,11,12,13,14,15},{16,17,18,19,20,21,22,23},{24..., dimensions={0} | all-to-all | bytes 196608 | tf_op jit(solution)/shard_map/all_to_all | solution.py:575
  47.1 0.6 %reshape.11 = f32[3072]{0:T(1024)} reshape(f32[12,256]{1,0:T(8,128)S(1)} %reduce_max.9) | data formatting | bytes 24576 | tf_op jit(solution)/shard_map/reshape | solution.py:576
  (1 shorter events, 0.0 us)
Async XLA Ops:
  0.1 6.4 %copy-start = (s32[204,1]{0,1:T(1,128)S(1)}, s32[204,1]{0,1:T(1,128)}, u32[]{:S(2)}) copy-start(s32[204,1]{0,1:T(1,128)} %param.5) | copy-start | bytes 2452
  2.4 18.8 %collective-permute-start = (bf16[544,1024]{1,0:T(8,128)(2,1)S(1)}, bf16[544,1024]{1,0:T(8,128)(2,1)S(1)}, u32[]{:S(2)}, u32[]{:S(2)}) collective-permute-start(bf16[544,1024]{1,0:T(8,128)(2,1)S(1)} %far_rows.1.far), channel_id=1, source_target_pairs={{4,8},{12,16},{20,24},{28,32},{36,40},{44,48},{52,56},{60,64},{68,... | collective-permute-start | bytes 3342344 | tf_op jit(solution)/shard_map/ppermute | solution.py:553
  15.5 9.4 %collective-permute-start.1 = (bf16[528,1024]{1,0:T(8,128)(2,1)S(1)}, bf16[528,1024]{1,0:T(8,128)(2,1)S(1)}, u32[]{:S(2)}, u32[]{:S(2)}) collective-permute-start(bf16[528,1024]{1,0:T(8,128)(2,1)S(1)} %get-tuple-element.21), channel_id=1, source_target_pairs={{0,4},{4,0},{8,12},{12,8},{16,20},{20,16},{24,28},{28,24},{32,36},... | collective-permute-start | bytes 3244040 | tf_op jit(solution)/shard_map/ppermute | solution.py:557
  21.0 3.8 %collective-permute-start.2 = (bf16[512,1024]{1,0:T(8,128)(2,1)S(1)}, bf16[512,1024]{1,0:T(8,128)(2,1)S(1)}, u32[]{:S(2)}, u32[]{:S(2)}) collective-permute-start(bf16[512,1024]{1,0:T(8,128)(2,1)S(1)} %get-tuple-element.22), channel_id=1, source_target_pairs={{0,4},{4,0},{8,12},{12,8},{16,20},{20,16},{24,28},{28,24},{32,36},... | collective-permute-start | bytes 3145736 | tf_op jit(solution)/shard_map/ppermute | solution.py:558
  25.7 4.9 %collective-permute-start.3 = (f32[2,256]{1,0:T(2,128)S(1)}, f32[2,256]{1,0:T(2,128)S(1)}, u32[]{:S(2)}, u32[]{:S(2)}) collective-permute-start(f32[2,256]{1,0:T(2,128)S(1)} %get-tuple-element.26), channel_id=1, source_target_pairs={{4,8},{12,16},{20,24},{28,32},{36,40},{44,48},{52,56},{60,64},{68,... | collective-permute-start | bytes 6152 | tf_op jit(solution)/shard_map/ppermute | solution.py:568

commit v3 on v2

--- a/solution.py
+++ b/solution.py
@@ -15,13 +15,12 @@
 CHIP_SLOTS = 4
 FAR_SLOTS = 2
 TAIL = 16
-FAR_ROWS = FAR_SLOTS * BLOCK + 2 * TAIL
-CHIP_ROWS = 2 * BLOCK + TAIL
-EXTRA_ROWS = 2 * BLOCK
+FAR_ROWS = FAR_SLOTS * BLOCK + TAIL
+CHIP_ROWS = CHIP_SLOTS * BLOCK + TAIL
 WINDOW = OWN + 2 * (SPANS - 1)
 GROUP = 8 * 128 // BLOCK
 CHUNK = 64
-BATCH = 4
+WIDE, NARROW = 8, 4
 FIELDS = 8
 EPS = 1e-6
 VMEM_LIMIT = 20 * 1024 * 1024
@@ -32,8 +31,8 @@
 VMEM = pl.BlockSpec(memory_space=pltpu.VMEM)
 
 
-def cost(us):
-    return pl.CostEstimate(flops=0, bytes_accessed=us * 3_000_000, transcendentals=0)
+def cost(us, flops=0):
+    return pl.CostEstimate(flops=flops, bytes_accessed=us * 3_000_000, transcendentals=0)
 
 
 PARAMS = pltpu.CompilerParams(vmem_limit_bytes=VMEM_LIMIT)
@@ -93,18 +92,21 @@
     local = [far_local(core, far_index(rep, slot)) for slot in range(FAR_SLOTS)]
     listing = pltpu.make_async_copy(holder_hbm, holder, holder_sem)
     listing.start()
-    fetches = [
-        pltpu.make_async_copy(emb.at[rows_of(local[slot])], raw.at[rows_of(slot)], sems.at[slot])
-        for slot in range(FAR_SLOTS)
-    ]
-    for fetch in fetches:
+    fetches = []
+    for slot in range(FAR_SLOTS):
+        for step in range(BLOCK // CHUNK):
+            source = pl.ds(pl.multiple_of(local[slot] * BLOCK + step * CHUNK, CHUNK), CHUNK)
+            part = pl.ds(slot * BLOCK + step * CHUNK, CHUNK)
+            sem = sems.at[len(fetches)]
+            fetches.append((part, pltpu.make_async_copy(emb.at[source], raw.at[part], sem)))
+    for _, fetch in fetches:
         fetch.start()
-    far_out[FAR_SLOTS * BLOCK :, :] = jnp.zeros((2 * TAIL, WIDTH), jnp.bfloat16)
+    far_out[FAR_SLOTS * BLOCK :, :] = jnp.zeros((TAIL, WIDTH), jnp.bfloat16)
     listing.wait()
     far_out[pl.ds(FAR_SLOTS * BLOCK, TAIL), 0:128] = flag_rows(holder, local)
-    for slot in range(FAR_SLOTS):
-        fetches[slot].wait()
-        normalise(raw, slot, far_out, slot)
+    for part, fetch in fetches:
+        fetch.wait()
+        far_out[part, :] = unit_rows(raw[part, :])
 
 
 def far_rows(place, holder, emb):
@@ -116,7 +118,7 @@
         scratch_shapes=[
             pltpu.VMEM((FAR_SLOTS * BLOCK, WIDTH), jnp.float32),
             pltpu.SMEM(holder.shape, jnp.int32),
-            pltpu.SemaphoreType.DMA((FAR_SLOTS,)),
+            pltpu.SemaphoreType.DMA((FAR_SLOTS * BLOCK // CHUNK,)),
             pltpu.SemaphoreType.DMA,
         ],
         compiler_params=PARAMS,
@@ -189,16 +191,18 @@
     return count + active.astype(jnp.int32)
 
 
-def run_tasks(tasks, count, left, right, row_acc, col_acc):
-    for extra in range(BATCH - 1):
+def pad_tasks(tasks, count):
+    for extra in range(WIDE - 1):
         for field in range(FIELDS):
             tasks[(count + extra) * FIELDS + field] = 0
 
-    @pl.loop(0, (count + BATCH - 1) // BATCH)
-    def _(step):
+
+def run_tasks(tasks, count, left, right, row_acc, col_acc):
+
+    def run(first, width):
         found = []
-        for lane in range(BATCH):
-            base = (step * BATCH + lane) * FIELDS
+        for lane in range(width):
+            base = (first + lane) * FIELDS
             task = [tasks[base + field] for field in range(FIELDS)]
             scored = similarity(left[rows_of(task[0]), :], right[rows_of(task[1]), :])
             scored = inside(scored, *task[2:6])
@@ -207,54 +211,80 @@
             row_acc[row_slot] = jnp.maximum(row_acc[row_slot], rows)
             col_acc[col_slot] = jnp.maximum(col_acc[col_slot], cols)
 
-
-def task_scratch(most):
-    return pltpu.SMEM(((most + BATCH) * FIELDS,), jnp.int32)
+    steps = (count + WIDE - NARROW - 1) // WIDE
+
+    @pl.loop(0, steps)
+    def _(step):
+        run(step * WIDE, WIDE)
+
+    @pl.when(count > steps * WIDE)
+    def _():
+        run(steps * WIDE, NARROW)
+
+
+def task_words(most):
+    return (most + WIDE) * FIELDS
+
+
+OWN_TASKS = task_words(OWN * (OWN - 1) // 2)
 
 
 def local_class(rep, turn):
     return (rep, 7 - rep, 8 + rep)[turn]
 
 
-def own_kernel(
+def rows_kernel(
     block_count, place, holder, labels, far, emb,
-    units, chip_out, extra_out, best, stats,
-    raw, tags, table, row_acc, col_acc, tasks, sems, out_sems, tag_sem, table_sem,
+    units, chip_out, best, stats, tasks,
+    raw, tags, table, sems, far_sems, out_sems, tag_sem, table_sem,
 ):
     shard, rep = place[0], place[1]
     core = lax.rem(shard, 2)
-    first_block = shard * OWN
     group = first_group(shard, block_count)
+    sent = [far_local(core, far_index(rep, slot)) for slot in range(FAR_SLOTS)]
+    local = [chip_local(core, chip_index(rep, slot)) for slot in range(CHIP_SLOTS)]
 
     def fetch(block):
         return pltpu.make_async_copy(
             emb.at[rows_of(block)], raw.at[rows_of(block)], sems.at[block]
         )
 
-    rows = pl.ds(pl.multiple_of(group * 8, 8), WINDOW * 2)
-    fetch_tags = pltpu.make_async_copy(labels.at[rows], tags, tag_sem)
+    def reuse(slot):
+        return pltpu.make_async_copy(
+            far.at[rows_of(slot)], units.at[rows_of(sent[slot])], far_sems.at[slot]
+        )
+
+    def push(slot):
+        return pltpu.make_async_copy(
+            units.at[rows_of(local[slot])], chip_out.at[rows_of(slot)], out_sems.at[slot]
+        )
+
+    def is_new(block):
+        return (block != sent[0]) & (block != sent[1])
+
+    window = pl.ds(pl.multiple_of(group * 8, 8), WINDOW * 2)
+    fetch_tags = pltpu.make_async_copy(labels.at[window], tags, tag_sem)
     fetch_tags.start()
 
     @pl.loop(1, OWN + 1)
     def _(m):
-        fetch(chip_local(core, m)).start()
-
-    local = [chip_local(core, chip_index(rep, slot)) for slot in range(CHIP_SLOTS)]
-    chip_out[2 * BLOCK :, :] = jnp.zeros((TAIL, WIDTH), jnp.bfloat16)
-    chip_out[2 * BLOCK :, 0:128] = flag_rows(holder, local)
-    col_acc[...] = jnp.full(col_acc.shape, -1.0, jnp.float32)
-    row_acc[...] = jnp.full(row_acc.shape, -1.0, jnp.float32)
+        block = chip_local(core, m)
+        pl.when(is_new(block))(lambda: fetch(block).start())
+
+    for slot in range(FAR_SLOTS):
+        reuse(slot).start()
+    chip_out[CHIP_SLOTS * BLOCK :, :] = jnp.zeros((TAIL, WIDTH), jnp.bfloat16)
+    chip_out[CHIP_SLOTS * BLOCK :, 0:128] = flag_rows(holder, local)
+    best[...] = jnp.full(best.shape, -1.0, jnp.float32)
     fetch_tags.wait()
     write_stats(tags, table)
     to_scalars = pltpu.make_async_copy(table, stats, table_sem)
     to_scalars.start()
-    to_scalars.wait()
-
-    def label_facts(block):
-        return label_stats(stats, block_count, shard, first_block + block)
+    for slot in range(FAR_SLOTS):
+        reuse(slot).wait()
 
     def diagonal(block):
-        at = (first_block + block - group * GROUP) * 2
+        at = (shard * OWN + block - group * GROUP) * 2
         tag_row = jnp.concatenate([tags[pl.ds(at, 1), :], tags[pl.ds(at + 1, 1), :]], axis=1)
         tag_row = tag_row.astype(jnp.float32)
         rows = lax.broadcasted_iota(jnp.int32, (BLOCK, BLOCK), 0)
@@ -263,91 +293,78 @@
         tag_col = jnp.max(jnp.where(rows == cols, spread, -1.0), axis=1, keepdims=True)
         scored = similarity(units[rows_of(block), :], units[rows_of(block), :])
         keep = (tag_col == tag_row) & (rows != cols)
-        found = fold_cols(jnp.where(keep, scored, -1.0))
-        found = jnp.where(holder[block * SPANS] != REPS, found, -1.0)
-        col_acc[block] = jnp.maximum(col_acc[block], found)
-
-    def push(slot):
-        target = (chip_out, extra_out)[slot // 2]
-        return pltpu.make_async_copy(
-            units.at[rows_of(local[slot])], target.at[rows_of(slot % 2)], out_sems.at[slot]
-        )
-
-    for phase in range(3):
-
-        @pl.loop(4 * phase + 1, 4 * phase + 5)
-        def _(m):
-            block = chip_local(core, m)
+        found = jnp.max(jnp.where(keep, scored, -1.0), axis=0, keepdims=True)
+        best[pl.ds(block, 1), :] = jnp.where(holder[block * SPANS] != REPS, found, -1.0)
+
+    def arrive(m):
+        block = chip_local(core, m)
+
+        @pl.when(is_new(block))
+        def _():
             fetch(block).wait()
             normalise(raw, block, units, block)
-            mine = block == local_class(rep, 0)
-            for turn in range(1, 3):
-                mine = mine | (block == local_class(rep, turn))
-            pl.when(mine)(functools.partial(diagonal, block))
-
-        if phase == 1:
-            for slot in range(CHIP_SLOTS):
-                push(slot).start()
-        low = OWN - 4 - 4 * phase
-        count = jnp.int32(0)
-        for turn in range(3):
-            if turn != phase and turn < 2 - phase:
-                continue
-            block = local_class(rep, turn)
-            b_first, _, b_count, _ = label_facts(block)
-
-            def visit(other, count, block=block, turn=turn, b_first=b_first, b_count=b_count):
-                _, a_last, _, a_start = label_facts(other)
-                listed = holder[other * SPANS + (block - other)] != REPS
-                return put_task(
-                    tasks, count, listed & (a_last == b_first),
-                    block, other, 0, b_count, a_start, BLOCK, turn, other,
-                )
-
-            begin_0 = low if turn >= 2 - phase else 0
-            end_0 = jnp.minimum(block, low + 4) if turn >= 2 - phase else 0
-            end_1 = block if turn == phase else 0
-            begin = jnp.where(core == 0, begin_0, 0)
-            end = jnp.where(core == 0, end_0, end_1)
-            count = lax.fori_loop(begin, end, visit, count)
-        run_tasks(tasks, count, units, units, row_acc, col_acc)
-
-    best[...] = jnp.max(col_acc[...], axis=1)
+
+        mine = block == local_class(rep, 0)
+        for turn in range(1, 3):
+            mine = mine | (block == local_class(rep, turn))
+        pl.when(mine)(lambda: diagonal(block))
+
+    pl.loop(1, 9)(arrive)
+    for slot in range(CHIP_SLOTS):
+        push(slot).start()
+
+    to_scalars.wait()
+
+    def label_facts(block):
+        return label_stats(stats, block_count, shard, shard * OWN + block)
+
+    count = jnp.int32(0)
     for turn in range(3):
-        here = (pl.ds(local_class(rep, turn), 1), slice(None))
-        found = as_lanes(jnp.max(row_acc[turn], axis=1, keepdims=True))
-        best[here] = jnp.maximum(best[here], found)
+        block = local_class(rep, turn)
+        b_first, _, b_count, _ = label_facts(block)
+
+        def visit(other, count, block=block, turn=turn, b_first=b_first, b_count=b_count):
+            _, a_last, _, a_start = label_facts(other)
+            listed = holder[other * SPANS + (block - other)] != REPS
+            return put_task(
+                tasks, count, listed & (a_last == b_first),
+                block, other, 0, b_count, a_start, BLOCK, turn, other,
+            )
+
+        count = lax.fori_loop(0, block, visit, count)
+    pad_tasks(tasks, count)
+    tasks[OWN_TASKS] = count
+
+    pl.loop(9, OWN + 1)(arrive)
     for slot in range(CHIP_SLOTS):
         push(slot).wait()
 
 
-def own_pairs(block_count, place, holder, labels, far, emb):
+def own_rows(block_count, place, holder, labels, far, emb):
     return pl.pallas_call(
-        functools.partial(own_kernel, block_count),
+        functools.partial(rows_kernel, block_count),
         out_shape=(
             pltpu.VMEM((OWN * BLOCK, WIDTH), jnp.bfloat16),
             pltpu.VMEM((CHIP_ROWS, WIDTH), jnp.bfloat16),
-            pltpu.VMEM((EXTRA_ROWS, WIDTH), jnp.bfloat16),
             pltpu.VMEM((OWN, BLOCK), jnp.float32),
             jax.ShapeDtypeStruct((8, 128), jnp.int32),
+            jax.ShapeDtypeStruct((OWN_TASKS + 1,), jnp.int32),
         ),
-        in_specs=[SMEM, SMEM, HBM, ANY, HBM],
-        out_specs=(VMEM, VMEM, VMEM, VMEM, SMEM),
+        in_specs=[SMEM, SMEM, HBM, VMEM, HBM],
+        out_specs=(VMEM, VMEM, VMEM, SMEM, SMEM),
         scratch_shapes=[
             pltpu.VMEM((OWN * BLOCK, WIDTH), jnp.float32),
             pltpu.VMEM((WINDOW * 2, 128), jnp.int32),
             pltpu.VMEM((8, 128), jnp.int32),
-            pltpu.VMEM((3, BLOCK, 128), jnp.float32),
-            pltpu.VMEM((OWN, 8, BLOCK), jnp.float32),
-            task_scratch(3 * 4),
             pltpu.SemaphoreType.DMA((OWN,)),
+            pltpu.SemaphoreType.DMA((FAR_SLOTS,)),
             pltpu.SemaphoreType.DMA((CHIP_SLOTS,)),
             pltpu.SemaphoreType.DMA,
             pltpu.SemaphoreType.DMA,
         ],
         compiler_params=PARAMS,
-        cost_estimate=cost(6),
-        name="own_pairs",
+        cost_estimate=cost(5),
+        name="own_rows",
     )(place, holder, labels, far, emb)
 
 
@@ -397,7 +414,7 @@
 
     def own_tasks(self, tasks, holder, moved_bits):
         count = jnp.int32(0)
-        for which in range(2):
+        for which in moved_bits:
 
             def visit(m, count, which=which):
                 column = self.local(m)
@@ -419,8 +436,9 @@
     col_acc[...] = jnp.full(col_acc.shape, -1.0, jnp.float32)
     row_acc[...] = jnp.full(row_acc.shape, -1.0, jnp.float32)
     tail = far[pl.ds(FAR_SLOTS * BLOCK, TAIL), :]
-    bits = [flag_bits(tail, slot) for slot in range(2)]
+    bits = {slot: flag_bits(tail, slot) for slot in range(2)}
     count = edge.own_tasks(tasks, holder, bits)
+    pad_tasks(tasks, count)
     run_tasks(tasks, count, far, units, row_acc, col_acc)
     mine[...] = jnp.maximum(best[...], jnp.max(col_acc[...], axis=1))
     for which in range(2):
@@ -429,12 +447,14 @@
         )
 
 
-def bridge_kernel(block_count, place, stats, found, far, chip, extra, returned, other):
+def bridge_kernel(
+    block_count, place, stats, found, far, chip, returned, other
+):
     edge = Boundary(True, block_count, place, stats)
     returned[...] = found[...]
     other[...] = jnp.full(other.shape, -1.0, jnp.float32)
     far_bits = flag_bits(far[pl.ds(FAR_SLOTS * BLOCK, TAIL), :], 0)
-    tail = chip[pl.ds(2 * BLOCK, TAIL), :]
+    tail = chip[pl.ds(CHIP_SLOTS * BLOCK, TAIL), :]
     pairs = []
     for slot in range(CHIP_SLOTS):
         bits = flag_bits(tail, slot)
@@ -451,17 +471,28 @@
     def _():
         rows, cols = [], []
         for slot, (active, area) in enumerate(pairs):
-            column = (chip, extra)[slot // 2][rows_of(slot % 2), :]
-            scored = inside(similarity(far[0:BLOCK, :], column), *area)
+            scored = inside(similarity(far[0:BLOCK, :], chip[rows_of(slot), :]), *area)
             scored = jnp.where(active, scored, -1.0)
             rows.append(fold_rows(scored))
             cols.append(fold_cols(scored))
         for slot in range(CHIP_SLOTS):
             block = chip_local(1 - edge.core, chip_index(edge.rep, slot))
-            other[pl.ds(block, 1), :] = jnp.max(cols[slot], axis=0, keepdims=True)
+            here = (pl.ds(block, 1), slice(None))
+            other[here] = jnp.max(cols[slot], axis=0, keepdims=True)
         best = functools.reduce(jnp.maximum, rows)
         best = as_lanes(jnp.max(best, axis=1, keepdims=True))
         returned[0:1, :] = jnp.maximum(returned[0:1, :], best)
+
+
+def own_kernel(place, own_tasks, best, units, mine, row_acc, col_acc):
+    col_acc[...] = jnp.full(col_acc.shape, -1.0, jnp.float32)
+    row_acc[...] = jnp.full(row_acc.shape, -1.0, jnp.float32)
+    run_tasks(own_tasks, own_tasks[OWN_TASKS], units, units, row_acc, col_acc)
+    mine[...] = jnp.maximum(best[...], jnp.max(col_acc[...], axis=1))
+    for turn in range(3):
+        here = (pl.ds(local_class(place[1], turn), 1), slice(None))
+        found = as_lanes(jnp.max(row_acc[turn], axis=1, keepdims=True))
+        mine[here] = jnp.maximum(mine[here], found)
 
 
 def chip_kernel(
@@ -471,9 +502,10 @@
     edge = Boundary(False, block_count, place, stats)
     col_acc[...] = jnp.full(col_acc.shape, -1.0, jnp.float32)
     row_acc[...] = jnp.full(row_acc.shape, -1.0, jnp.float32)
-    tail = chip[pl.ds(2 * BLOCK, TAIL), :]
-    bits = [flag_bits(tail, slot) for slot in range(2)]
+    tail = chip[pl.ds(CHIP_SLOTS * BLOCK, TAIL), :]
+    bits = {slot: flag_bits(tail, slot) for slot in range(2)}
     count = edge.own_tasks(tasks, holder, bits)
+    pad_tasks(tasks, count)
     run_tasks(tasks, count, chip, units, row_acc, col_acc)
     mine[...] = jnp.maximum(mine_in[...], jnp.max(col_acc[...], axis=1))
     other[...] = other_in[...]
@@ -487,7 +519,7 @@
 RETURNED = pltpu.VMEM((2, BLOCK), jnp.float32)
 
 
-def pair_call(kernel, name, us, outs, scalars, scratch, args):
+def pair_call(kernel, name, estimate, outs, scalars, scratch, args):
     return pl.pallas_call(
         kernel,
         out_shape=outs,
@@ -495,15 +527,19 @@
         out_specs=(VMEM,) * len(outs),
         scratch_shapes=scratch,
         compiler_params=PARAMS,
-        cost_estimate=cost(us),
+        cost_estimate=estimate,
         name=name,
     )(*args)
 
 
-PAIR_SCRATCH = [
+OWN_SCRATCH = [
+    pltpu.VMEM((3, BLOCK, 128), jnp.float32),
+    pltpu.VMEM((OWN, 8, BLOCK), jnp.float32),
+]
+EDGE_SCRATCH = [
     pltpu.VMEM((2, BLOCK, 128), jnp.float32),
     pltpu.VMEM((OWN, 8, BLOCK), jnp.float32),
-    task_scratch(2 * OWN),
+    pltpu.SMEM((task_words(2 * OWN),), jnp.int32),
 ]
 
 
@@ -519,13 +555,15 @@
     for target in range(2):
         share = jnp.where(core == target, merged[...], other[...])
         for copy in range(REPS):
-            outgoing[target * REPS + copy] = share
+            at = target * REPS + copy
+            outgoing[at, pl.ds(0, OWN, stride=2), :] = share[:, 0:128]
+            outgoing[at, pl.ds(1, OWN, stride=2), :] = share[:, 128:256]
 
 
 def finish(block_count, place, mine, other, back):
     return pl.pallas_call(
         functools.partial(finish_kernel, block_count),
-        out_shape=jax.ShapeDtypeStruct((2 * REPS, OWN, BLOCK), jnp.float32),
+        out_shape=jax.ShapeDtypeStruct((2 * REPS, OWN * 2, 128), jnp.float32),
         in_specs=[SMEM, VMEM, VMEM, VMEM],
         out_specs=VMEM,
         scratch_shapes=[pltpu.VMEM((OWN, BLOCK), jnp.float32)],
@@ -551,24 +589,26 @@
 
     far_out = far_rows(place, listing, embeddings)
     far_in = in_vmem(lax.ppermute(far_out, "shard", across))
-    units, chip_out, extra_out, best, stats = own_pairs(
+    units, chip_out, best, stats, tasks = own_rows(
         block_count, place, listing, labels, far_out, embeddings
     )
     chip_in = in_vmem(lax.ppermute(chip_out, "shard", within))
-    extra_in = in_vmem(lax.ppermute(extra_out, "shard", within))
-
+
+    (mine,) = pair_call(
+        own_kernel, "own_pairs", cost(3), (BEST,), 2, OWN_SCRATCH, (place, tasks, best, units)
+    )
     mine, found = pair_call(
-        functools.partial(far_kernel, block_count), "far_pairs", 4, (BEST, RETURNED),
-        3, PAIR_SCRATCH, (place, listing, stats, best, units, far_in),
+        functools.partial(far_kernel, block_count), "far_pairs", cost(4, 10**11),
+        (BEST, RETURNED), 3, EDGE_SCRATCH, (place, listing, stats, mine, units, far_in),
     )
     returned, other = pair_call(
-        functools.partial(bridge_kernel, block_count), "bridge_pairs", 1, (RETURNED, BEST),
-        2, [], (place, stats, found, far_in, chip_in, extra_in),
+        functools.partial(bridge_kernel, block_count), "bridge_pairs", cost(1),
+        (RETURNED, BEST), 2, [], (place, stats, found, far_in, chip_in),
     )
     back = lax.ppermute(returned, "shard", across)
     mine, other = pair_call(
-        functools.partial(chip_kernel, block_count), "chip_pairs", 4, (BEST, BEST),
-        3, PAIR_SCRATCH, (place, listing, stats, mine, other, units, chip_in),
+        functools.partial(chip_kernel, block_count), "chip_pairs", cost(4), (BEST, BEST),
+        3, EDGE_SCRATCH, (place, listing, stats, mine, other, units, chip_in),
     )
     outgoing = finish(block_count, place, mine, other, back)
     groups = [list(range(c * 2 * REPS, (c + 1) * 2 * REPS)) for c in range(count // 2)]

time: 47.3 us -> 46.7 us (0.987)
  the two profiles are of different devices: /device:TPU:3 before, /device:TPU:7 now
where the time goes in v3:
time: 46.7 us; the launch traced here: 46.5 us
  blocking collectives  16.9 us (36%)
  Pallas kernels  15.5 us (33%)
  starting transfers between devices  12.5 us (27%)
  waiting for transfers between devices  0.82 us (2%)
  other arithmetic  0.68 us (1%)
    all_to_all x1, blocking collectives, shards(): lax.all_to_all(outgoing, ('shard', 'rep'), 0, 0, axis_index_groups=groups)  16.9 us
    pallas_call x1, Pallas kernels, own_rows(): pl.pallas_call(functools.partial(rows_kernel, block_count), out_shape=(pl...  6.44 us
    pallas_call x4, Pallas kernels, pair_call(): pl.pallas_call(kernel, out_shape=outs, in_specs=[SMEM] * scalars + [VMEM]...  6 us
    ppermute x1, starting transfers between devices, shards(): back = lax.ppermute(returned, 'shard', across)  4.33 us
    ppermute x1, starting transfers between devices, shards(): far_in = in_vmem(lax.ppermute(far_out, 'shard', across))  4.11 us
    ppermute x1, starting transfers between devices, shards(): chip_in = in_vmem(lax.ppermute(chip_out, 'shard', within))  4.06 us
    pallas_call x1, Pallas kernels, far_rows(): pl.pallas_call(far_rows_kernel, out_shape=pltpu.VMEM((FAR_ROWS, WIDTH), j...  2.47 us
  transfers between devices with their start and end apart: 3, of which 1 were waited for; matrix products, arithmetic and copies ran while one was open for 0% of the time, Pallas kernels for 25%

profile of v3, /device:TPU:7, one launch (start us, length us, event | category | flops | bytes accessed | tf_op | source)
XLA Modules:
  0.0 46.5 jit_solution(14637766310199777)
XLA Ops:
  0.0 0.1 pad_add_fusion.place
  0.1 0.0 copy-start
  0.1 2.5 %far_rows.1.far = bf16[528,1024]{1,0:T(8,128)(2,1)S(1)} custom-call(s32[2]{0:T(128)S(1)} %pad_add_fusion.place, s32[204]{0:T(256)} %bitcast.5, f32[3072,1024]{1,0:T(8,128)} %emb.3), custom_call_target="tpu_custom_call" | custom-call | bytes 3000000 | tf_op jit(solution)/shard_map/far_rows/pallas_call | solution.py:113
  2.6 4.1 %collective-permute-start = (bf16[528,1024]{1,0:T(8,128)(2,1)S(1)}, bf16[528,1024]{1,0:T(8,128)(2,1)S(1)}, u32[]{:S(2)}, u32[]{:S(2)}) collective-permute-start(bf16[528,1024]{1,0:T(8,128)(2,1)S(1)} %far_rows.1.far), channel_id=1, source_target_pairs={{4,8},{12,16},{20,24},{28,32},{36,40},{44,48},{52,56},{60,64},{68,... | collective-permute-start | bytes 3244040 | tf_op jit(solution)/shard_map/ppermute | solution.py:591
  6.7 0.0 copy-done
  6.7 6.4 %own_rows.1 = (bf16[3072,1024]{1,0:T(8,128)(2,1)S(1)}, bf16[1040,1024]{1,0:T(8,128)(2,1)S(1)}, f32[12,256]{1,0:T(8,128)S(1)}, s32[8,128]{1,0:T(8,128)S(1)}, s32[593]{0:T(1024)S(1)}) custom-call(s32[2]{0:T(128)S(1)} %pad_add_fusion.place, s32[204]{0:T(256)S(1)} %bitcast.6, s32[1536,128]{1,0:T(8,128)} %bitcast.9, bf16[528,1024]{1,0:T(8,128)(2,1)S(1)} %far_rows.1.far, ...), custom_call_target="tpu_custom_call" | custom-call | bytes 15000000 | tf_op jit(solution)/shard_map/own_rows/pallas_call | solution.py:344
  13.1 4.1 %collective-permute-start.1 = (bf16[1040,1024]{1,0:T(8,128)(2,1)S(1)}, bf16[1040,1024]{1,0:T(8,128)(2,1)S(1)}, u32[]{:S(2)}, u32[]{:S(2)}) collective-permute-start(bf16[1040,1024]{1,0:T(8,128)(2,1)S(1)} %get-tuple-element.22), channel_id=1, source_target_pairs={{0,4},{4,0},{8,12},{12,8},{16,20},{20,16},{24,28},{28,24},{32,36},... | collective-permute-start | bytes 6389768 | tf_op jit(solution)/shard_map/ppermute | solution.py:595
  17.2 1.8 %own_pairs.1.best = f32[12,256]{1,0:T(8,128)S(1)} custom-call(s32[2]{0:T(128)S(1)} %pad_add_fusion.place, s32[593]{0:T(1024)S(1)} %get-tuple-element.17.own_tasks, f32[12,256]{1,0:T(8,128)S(1)} %get-tuple-element.18.best, bf16[3072,1024]{1,0:T(8,128)(2,1)S(1)} %get-tuple-element.19.units), custom_call_target="tpu_custom_call" | custom-call | bytes 9000000 | tf_op jit(solution)/shard_map/own_pairs/pallas_call | solution.py:523
  19.0 0.8 %collective-permute-done.far = bf16[528,1024]{1,0:T(8,128)(2,1)S(1)} collective-permute-done((bf16[528,1024]{1,0:T(8,128)(2,1)S(1)}, bf16[528,1024]{1,0:T(8,128)(2,1)S(1)}, u32[]{:S(2)}, u32[]{:S(2)}) %collective-permute-start) | collective-permute-done | bytes 1081376 | tf_op jit(solution)/shard_map/ppermute | solution.py:591
  19.8 1.7 %far_pairs.1 = (f32[12,256]{1,0:T(8,128)S(1)}, f32[2,256]{1,0:T(2,128)S(1)}) custom-call(s32[2]{0:T(128)S(1)} %pad_add_fusion.place, s32[204]{0:T(256)S(1)} %bitcast.7, s32[8,128]{1,0:T(8,128)S(1)} %get-tuple-element.16.stats, f32[12,256]{1,0:T(8,128)S(1)} %own_pairs.1.best, bf16[3072,1024]{1,0:T(8,128)(2,1)S(1)} %get-tuple-element.19.units, ...), custom_call_target="tpu_custom_call" | custom-call | flops 99999997952 | bytes 12000000 | tf_op jit(solution)/shard_map/far_pairs/pallas_call | solution.py:523
  21.5 0.0 collective-permute-done.1.chip
  21.5 0.8 %bridge_pairs.1 = (f32[2,256]{1,0:T(2,128)S(1)}, f32[12,256]{1,0:T(8,128)S(1)}) custom-call(s32[2]{0:T(128)S(1)} %pad_add_fusion.place, s32[8,128]{1,0:T(8,128)S(1)} %get-tuple-element.16.stats, f32[2,256]{1,0:T(2,128)S(1)} %get-tuple-element.21.found, bf16[528,1024]{1,0:T(8,128)(2,1)S(1)} %collective-permute-done.far, ...), custom_call_target="tpu_custom_call" | custom-call | bytes 3000000 | tf_op jit(solution)/shard_map/bridge_pairs/pallas_call | solution.py:523
  22.3 4.3 %collective-permute-start.2 = (f32[2,256]{1,0:T(2,128)S(1)}, f32[2,256]{1,0:T(2,128)S(1)}, u32[]{:S(2)}, u32[]{:S(2)}) collective-permute-start(f32[2,256]{1,0:T(2,128)S(1)} %get-tuple-element.26), channel_id=1, source_target_pairs={{4,8},{12,16},{20,24},{28,32},{36,40},{44,48},{52,56},{60,64},{68,... | collective-permute-start | bytes 6152 | tf_op jit(solution)/shard_map/ppermute | solution.py:608
  26.6 1.7 %chip_pairs.1 = (f32[12,256]{1,0:T(8,128)S(1)}, f32[12,256]{1,0:T(8,128)S(1)}) custom-call(s32[2]{0:T(128)S(1)} %pad_add_fusion.place, s32[204]{0:T(256)S(1)} %bitcast.8, s32[8,128]{1,0:T(8,128)S(1)} %get-tuple-element.16.stats, f32[12,256]{1,0:T(8,128)S(1)} %get-tuple-element.20.mine_in, f32[12,256]{1,0:T(8,128)S(1)} %get-tuple-element.23.other_in, ...), custom_call_target="tpu_custom_call" | custom-call | bytes 12000000 | tf_op jit(solution)/shard_map/chip_pairs/pallas_call | solution.py:523
  28.4 0.0 collective-permute-done.2.back
  28.4 0.6 %finish.1 = f32[8,24,128]{2,1,0:T(8,128)S(1)} custom-call(s32[2]{0:T(128)S(1)} %pad_add_fusion.place, f32[12,256]{1,0:T(8,128)S(1)} %get-tuple-element.24.mine, f32[12,256]{1,0:T(8,128)S(1)} %get-tuple-element.25.other, f32[2,256]{1,0:T(2,128)S(1)} %collective-permute-done.2.back), custom_call_target="tpu_custom_call" | custom-call | bytes 3000000 | tf_op jit(solution)/shard_map/finish/pallas_call | solution.py:564
  28.9 16.9 %all_to_all.5 = f32[8,24,128]{2,1,0:T(8,128)S(1)} all-to-all(f32[8,24,128]{2,1,0:T(8,128)S(1)} %finish.1), channel_id=1, replica_groups={{0,1,2,3,4,5,6,7},{8,9,10,11,12,13,14,15},{16,17,18,19,20,21,22,23},{24..., dimensions={0} | all-to-all | bytes 196608 | tf_op jit(solution)/shard_map/all_to_all | solution.py:615
  45.9 0.6 %reduce_max.9 = f32[24,128]{1,0:T(8,128)} reduce(f32[8,24,128]{2,1,0:T(8,128)S(1)} %all_to_all.5, f32[]{:T(128)} %constant.10.clone.1), dimensions={0}, to_apply=%region_0.0 | reduce | flops 21504 | bytes 110596 | tf_op jit(solution)/shard_map/reduce_max | solution.py:616
Async XLA Ops:
  0.1 6.6 %copy-start = (s32[204,1]{0,1:T(1,128)S(1)}, s32[204,1]{0,1:T(1,128)}, u32[]{:S(2)}) copy-start(s32[204,1]{0,1:T(1,128)} %param.5) | copy-start | bytes 2452
  2.6 17.2 %collective-permute-start = (bf16[528,1024]{1,0:T(8,128)(2,1)S(1)}, bf16[528,1024]{1,0:T(8,128)(2,1)S(1)}, u32[]{:S(2)}, u32[]{:S(2)}) collective-permute-start(bf16[528,1024]{1,0:T(8,128)(2,1)S(1)} %far_rows.1.far), channel_id=1, source_target_pairs={{4,8},{12,16},{20,24},{28,32},{36,40},{44,48},{52,56},{60,64},{68,... | collective-permute-start | bytes 3244040 | tf_op jit(solution)/shard_map/ppermute | solution.py:591
  13.1 8.3 %collective-permute-start.1 = (bf16[1040,1024]{1,0:T(8,128)(2,1)S(1)}, bf16[1040,1024]{1,0:T(8,128)(2,1)S(1)}, u32[]{:S(2)}, u32[]{:S(2)}) collective-permute-start(bf16[1040,1024]{1,0:T(8,128)(2,1)S(1)} %get-tuple-element.22), channel_id=1, source_target_pairs={{0,4},{4,0},{8,12},{12,8},{16,20},{20,16},{24,28},{28,24},{32,36},... | collective-permute-start | bytes 6389768 | tf_op jit(solution)/shard_map/ppermute | solution.py:595
  22.3 6.1 %collective-permute-start.2 = (f32[2,256]{1,0:T(2,128)S(1)}, f32[2,256]{1,0:T(2,128)S(1)}, u32[]{:S(2)}, u32[]{:S(2)}) collective-permute-start(f32[2,256]{1,0:T(2,128)S(1)} %get-tuple-element.26), channel_id=1, source_target_pairs={{4,8},{12,16},{20,24},{28,32},{36,40},{44,48},{52,56},{60,64},{68,... | collective-permute-start | bytes 6152 | tf_op jit(solution)/shard_map/ppermute | solution.py:608

commit v4 on v3

--- a/solution.py
+++ b/solution.py
@@ -12,7 +12,8 @@
 WIDTH = 1024
 OWN = 12
 REPS = 4
-CHIP_SLOTS = 4
+NEAR = 4
+CHIP_SLOTS = 2 + NEAR - 1
 FAR_SLOTS = 2
 TAIL = 16
 FAR_ROWS = FAR_SLOTS * BLOCK + TAIL
@@ -21,7 +22,7 @@
 GROUP = 8 * 128 // BLOCK
 CHUNK = 64
 WIDE, NARROW = 8, 4
-FIELDS = 8
+FIELDS = 9
 EPS = 1e-6
 VMEM_LIMIT = 20 * 1024 * 1024
 
@@ -66,14 +67,10 @@
     return jnp.where(slot == 0, rep + 1, 8 - rep)
 
 
-CHIP_INDEX = ((3, 4, 1, 2), (2, 7, 1, 3), (5, 6, 1, 2), (1, 8, 2, 3))
-
-
 def chip_index(rep, slot):
-    picked = jnp.int32(CHIP_INDEX[REPS - 1][slot])
-    for other in range(REPS - 1):
-        picked = jnp.where(rep == other, CHIP_INDEX[other][slot], picked)
-    return picked
+    if slot < 2:
+        return far_index(rep, slot)
+    return slot - 1 + (slot - 1 > rep).astype(jnp.int32)
 
 
 def flag_rows(holder, locals_of_slots):
@@ -102,11 +99,11 @@
     for _, fetch in fetches:
         fetch.start()
     far_out[FAR_SLOTS * BLOCK :, :] = jnp.zeros((TAIL, WIDTH), jnp.bfloat16)
-    listing.wait()
-    far_out[pl.ds(FAR_SLOTS * BLOCK, TAIL), 0:128] = flag_rows(holder, local)
     for part, fetch in fetches:
         fetch.wait()
         far_out[part, :] = unit_rows(raw[part, :])
+    listing.wait()
+    far_out[pl.ds(FAR_SLOTS * BLOCK, TAIL), 0:128] = flag_rows(holder, local)
 
 
 def far_rows(place, holder, emb):
@@ -227,6 +224,7 @@
 
 
 OWN_TASKS = task_words(OWN * (OWN - 1) // 2)
+EDGE_TASKS = task_words(2 * OWN)
 
 
 def local_class(rep, turn):
@@ -323,15 +321,21 @@
         block = local_class(rep, turn)
         b_first, _, b_count, _ = label_facts(block)
 
-        def visit(other, count, block=block, turn=turn, b_first=b_first, b_count=b_count):
-            _, a_last, _, a_start = label_facts(other)
+        def shares(state, b_first=b_first):
+            other, _ = state
+            return (other >= 0) & (label_facts(jnp.maximum(other, 0))[1] == b_first)
+
+        def visit(state, block=block, turn=turn, b_count=b_count):
+            other, count = state
             listed = holder[other * SPANS + (block - other)] != REPS
-            return put_task(
-                tasks, count, listed & (a_last == b_first),
-                block, other, 0, b_count, a_start, BLOCK, turn, other,
+            a_start = label_facts(other)[3]
+            count = put_task(
+                tasks, count, listed, block, other, 0, b_count, a_start, BLOCK, turn, other,
+                block - other,
             )
-
-        count = lax.fori_loop(0, block, visit, count)
+            return other - 1, count
+
+        _, count = lax.while_loop(shares, visit, (block - 1, count))
     pad_tasks(tasks, count)
     tasks[OWN_TASKS] = count
 
@@ -377,12 +381,11 @@
 
 
 class Boundary:
-    def __init__(self, far, block_count, place, stats):
-        self.far, self.block_count, self.stats = far, block_count, stats
+    def __init__(self, far, block_count, place):
+        self.far, self.block_count = far, block_count
         self.shard, self.rep = place[0], place[1]
         self.core = lax.rem(self.shard, 2)
         self.side = self.core if far else 1 - self.core
-        self.tie = 1 - self.side
 
     def local(self, m):
         return far_local(self.core, m) if self.far else chip_local(self.core, m)
@@ -390,55 +393,100 @@
     def near(self, which):
         return far_index(self.rep, which) if self.far else chip_index(self.rep, which)
 
-    def pair(self, which, m, moved_bits, column_flag):
+    def start(self, stats, which):
+        first_block = self.shard * OWN
         near = self.near(which)
+        before = self.side == 0
+        block = jnp.where(before, first_block - near, first_block + OWN - 1 + near)
+        facts = label_stats(stats, self.block_count, self.shard, block)
+        present = (block >= 0) & (block < self.block_count)
+        return near, before, present, facts
+
+    def shares(self, stats, moved, m):
+        _, before, _, (m_first, m_last, _, _) = moved
+        c_first, c_last, _, _ = self.column(stats, m)
+        return jnp.where(before, m_last == c_first, c_last == m_first)
+
+    def column(self, stats, m):
         first_block = self.shard * OWN
-        before = self.side == 0
-        moved_block = jnp.where(before, first_block - near, first_block + OWN - 1 + near)
-        column_block = jnp.where(before, first_block + m - 1, first_block + OWN - m)
-        offset = near + m - 1
-        wanted = (m > near) | ((m == near) & (lax.rem(near, 2) == self.tie))
-        wanted = wanted & (offset < SPANS)
-        wanted = wanted & (moved_block >= 0) & (moved_block < self.block_count)
-        offset = jnp.minimum(offset, SPANS - 1)
-        moved_flag = lax.rem(lax.shift_right_logical(moved_bits, offset), 2) == 1
-        listed = jnp.where(before, moved_flag, column_flag(offset))
-        facts = functools.partial(label_stats, self.stats, self.block_count, self.shard)
-        m_first, m_last, m_count, m_start = facts(moved_block)
-        c_first, c_last, c_count, c_start = facts(column_block)
-        shared = jnp.where(before, m_last == c_first, c_last == m_first)
-        return wanted & listed & shared, (
+        block = jnp.where(self.side == 0, first_block + m - 1, first_block + OWN - m)
+        return label_stats(stats, self.block_count, self.shard, block)
+
+    def area(self, stats, moved, m):
+        _, before, _, (_, _, m_count, m_start) = moved
+        _, _, c_count, c_start = self.column(stats, m)
+        return (
             jnp.where(before, m_start, 0), jnp.where(before, BLOCK, m_count),
             jnp.where(before, 0, c_start), jnp.where(before, c_count, BLOCK),
         )
 
-    def own_tasks(self, tasks, holder, moved_bits):
+    def list_tasks(self, tasks, stats, holder):
         count = jnp.int32(0)
-        for which in moved_bits:
-
-            def visit(m, count, which=which):
-                column = self.local(m)
-
-                def flag(offset):
-                    return holder[column * SPANS + offset] != REPS
-
-                active, area = self.pair(which, m, moved_bits[which], flag)
-                return put_task(tasks, count, active, which, column, *area, which, column)
-
-            count = lax.fori_loop(self.near(which), OWN + 1, visit, count)
+        for which in range(2):
+            moved = self.start(stats, which)
+            near, before, present, _ = moved
+            last = jnp.where(present, jnp.minimum(OWN, SPANS - near), 0)
+
+            def shares(state, moved=moved, last=last):
+                m, _ = state
+                return (m <= last) & self.shares(stats, moved, m)
+
+            def visit(state, which=which, moved=moved, near=near, before=before):
+                m, count = state
+                column, offset = self.local(m), near + m - 1
+                listed = before | (holder[column * SPANS + offset] != REPS)
+                area = self.area(stats, moved, m)
+                count = put_task(
+                    tasks, count, listed, which, column, *area, which, column, offset
+                )
+                return m + 1, count
+
+            tie = lax.rem(near, 2) == 1 - self.side
+            first = jnp.where(tie, near, near + 1)
+            _, count = lax.while_loop(shares, visit, (first, count))
+        tasks[EDGE_TASKS] = count
+
+    def keep_listed(self, found, tasks, bits):
+        def visit(index, count):
+            task = [found[index * FIELDS + field] for field in range(FIELDS)]
+            flags = jnp.where(task[0] == 0, bits[0], bits[1])
+            listed = lax.rem(lax.shift_right_logical(flags, task[8]), 2) == 1
+            return put_task(tasks, count, (self.side == 1) | listed, *task)
+
+        count = lax.fori_loop(0, found[EDGE_TASKS], visit, jnp.int32(0))
+        pad_tasks(tasks, count)
         return count
 
 
+def own_kernel(
+    block_count, place, holder, stats, own_tasks, best, units,
+    mine, far_list, chip_list, row_acc, col_acc,
+):
+    col_acc[...] = jnp.full(col_acc.shape, -1.0, jnp.float32)
+    row_acc[...] = jnp.full(row_acc.shape, -1.0, jnp.float32)
+    run_tasks(own_tasks, own_tasks[OWN_TASKS], units, units, row_acc, col_acc)
+    mine[...] = jnp.maximum(best[...], jnp.max(col_acc[...], axis=1))
+    for turn in range(3):
+        here = (pl.ds(local_class(place[1], turn), 1), slice(None))
+        found = as_lanes(jnp.max(row_acc[turn], axis=1, keepdims=True))
+        mine[here] = jnp.maximum(mine[here], found)
+    edge = Boundary(True, block_count, place)
+    edge.list_tasks(far_list, stats, holder)
+    moved = edge.start(stats, 0)
+    bridged = moved[2] & edge.shares(stats, moved, OWN + 1)
+    far_list[EDGE_TASKS + 1] = bridged.astype(jnp.int32)
+    Boundary(False, block_count, place).list_tasks(chip_list, stats, holder)
+
+
 def far_kernel(
-    block_count, place, holder, stats, best, units, far, mine, returned, row_acc, col_acc, tasks
+    block_count, place, far_list, best, units, far, mine, returned, row_acc, col_acc, tasks
 ):
-    edge = Boundary(True, block_count, place, stats)
+    edge = Boundary(True, block_count, place)
     col_acc[...] = jnp.full(col_acc.shape, -1.0, jnp.float32)
     row_acc[...] = jnp.full(row_acc.shape, -1.0, jnp.float32)
     tail = far[pl.ds(FAR_SLOTS * BLOCK, TAIL), :]
-    bits = {slot: flag_bits(tail, slot) for slot in range(2)}
-    count = edge.own_tasks(tasks, holder, bits)
-    pad_tasks(tasks, count)
+    bits = [flag_bits(tail, slot) for slot in range(2)]
+    count = edge.keep_listed(far_list, tasks, bits)
     run_tasks(tasks, count, far, units, row_acc, col_acc)
     mine[...] = jnp.maximum(best[...], jnp.max(col_acc[...], axis=1))
     for which in range(2):
@@ -447,32 +495,26 @@
         )
 
 
-def bridge_kernel(
-    block_count, place, stats, found, far, chip, returned, other
-):
-    edge = Boundary(True, block_count, place, stats)
+def bridge_kernel(block_count, place, far_list, stats, found, far, chip, returned, other):
     returned[...] = found[...]
     other[...] = jnp.full(other.shape, -1.0, jnp.float32)
-    far_bits = flag_bits(far[pl.ds(FAR_SLOTS * BLOCK, TAIL), :], 0)
-    tail = chip[pl.ds(CHIP_SLOTS * BLOCK, TAIL), :]
-    pairs = []
-    for slot in range(CHIP_SLOTS):
-        bits = flag_bits(tail, slot)
-
-        def flag(offset, bits=bits):
-            return lax.rem(lax.shift_right_logical(bits, offset), 2) == 1
-
-        pairs.append(edge.pair(0, OWN + chip_index(edge.rep, slot), far_bits, flag))
-    some = pairs[0][0]
-    for active, _ in pairs[1:]:
-        some = some | active
-
-    @pl.when(some)
+
+    @pl.when(far_list[EDGE_TASKS + 1] > 0)
     def _():
+        edge = Boundary(True, block_count, place)
+        far_bits = flag_bits(far[pl.ds(FAR_SLOTS * BLOCK, TAIL), :], 0)
+        tail = chip[pl.ds(CHIP_SLOTS * BLOCK, TAIL), :]
+        moved = edge.start(stats, 0)
         rows, cols = [], []
-        for slot, (active, area) in enumerate(pairs):
+        for slot in range(CHIP_SLOTS):
+            m = OWN + chip_index(edge.rep, slot)
+            offset, area = moved[0] + m - 1, edge.area(stats, moved, m)
+            active = moved[2] & (offset < SPANS) & edge.shares(stats, moved, m)
+            offset = jnp.minimum(offset, SPANS - 1)
+            bits = jnp.where(edge.side == 0, far_bits, flag_bits(tail, slot))
+            listed = lax.rem(lax.shift_right_logical(bits, offset), 2) == 1
             scored = inside(similarity(far[0:BLOCK, :], chip[rows_of(slot), :]), *area)
-            scored = jnp.where(active, scored, -1.0)
+            scored = jnp.where(active & listed, scored, -1.0)
             rows.append(fold_rows(scored))
             cols.append(fold_cols(scored))
         for slot in range(CHIP_SLOTS):
@@ -484,28 +526,16 @@
         returned[0:1, :] = jnp.maximum(returned[0:1, :], best)
 
 
-def own_kernel(place, own_tasks, best, units, mine, row_acc, col_acc):
-    col_acc[...] = jnp.full(col_acc.shape, -1.0, jnp.float32)
-    row_acc[...] = jnp.full(row_acc.shape, -1.0, jnp.float32)
-    run_tasks(own_tasks, own_tasks[OWN_TASKS], units, units, row_acc, col_acc)
-    mine[...] = jnp.maximum(best[...], jnp.max(col_acc[...], axis=1))
-    for turn in range(3):
-        here = (pl.ds(local_class(place[1], turn), 1), slice(None))
-        found = as_lanes(jnp.max(row_acc[turn], axis=1, keepdims=True))
-        mine[here] = jnp.maximum(mine[here], found)
-
-
 def chip_kernel(
-    block_count, place, holder, stats, mine_in, other_in, units, chip,
+    block_count, place, chip_list, mine_in, other_in, units, chip,
     mine, other, row_acc, col_acc, tasks,
 ):
-    edge = Boundary(False, block_count, place, stats)
+    edge = Boundary(False, block_count, place)
     col_acc[...] = jnp.full(col_acc.shape, -1.0, jnp.float32)
     row_acc[...] = jnp.full(row_acc.shape, -1.0, jnp.float32)
     tail = chip[pl.ds(CHIP_SLOTS * BLOCK, TAIL), :]
-    bits = {slot: flag_bits(tail, slot) for slot in range(2)}
-    count = edge.own_tasks(tasks, holder, bits)
-    pad_tasks(tasks, count)
+    bits = [flag_bits(tail, slot) for slot in range(2)]
+    count = edge.keep_listed(chip_list, tasks, bits)
     run_tasks(tasks, count, chip, units, row_acc, col_acc)
     mine[...] = jnp.maximum(mine_in[...], jnp.max(col_acc[...], axis=1))
     other[...] = other_in[...]
@@ -516,6 +546,7 @@
 
 
 BEST = pltpu.VMEM((OWN, BLOCK), jnp.float32)
+LIST = jax.ShapeDtypeStruct((EDGE_TASKS + 2,), jnp.int32)
 RETURNED = pltpu.VMEM((2, BLOCK), jnp.float32)
 
 
@@ -524,7 +555,7 @@
         kernel,
         out_shape=outs,
         in_specs=[SMEM] * scalars + [VMEM] * (len(args) - scalars),
-        out_specs=(VMEM,) * len(outs),
+        out_specs=tuple(SMEM if out is LIST else VMEM for out in outs),
         scratch_shapes=scratch,
         compiler_params=PARAMS,
         cost_estimate=estimate,
@@ -539,7 +570,7 @@
 EDGE_SCRATCH = [
     pltpu.VMEM((2, BLOCK, 128), jnp.float32),
     pltpu.VMEM((OWN, 8, BLOCK), jnp.float32),
-    pltpu.SMEM((task_words(2 * OWN),), jnp.int32),
+    pltpu.SMEM((EDGE_TASKS,), jnp.int32),
 ]
 
 
@@ -594,21 +625,22 @@
     )
     chip_in = in_vmem(lax.ppermute(chip_out, "shard", within))
 
-    (mine,) = pair_call(
-        own_kernel, "own_pairs", cost(3), (BEST,), 2, OWN_SCRATCH, (place, tasks, best, units)
+    mine, far_list, chip_list = pair_call(
+        functools.partial(own_kernel, block_count), "own_pairs", cost(3), (BEST, LIST, LIST),
+        4, OWN_SCRATCH, (place, listing, stats, tasks, best, units),
     )
     mine, found = pair_call(
         functools.partial(far_kernel, block_count), "far_pairs", cost(4, 10**11),
-        (BEST, RETURNED), 3, EDGE_SCRATCH, (place, listing, stats, mine, units, far_in),
+        (BEST, RETURNED), 2, EDGE_SCRATCH, (place, far_list, mine, units, far_in),
     )
     returned, other = pair_call(
         functools.partial(bridge_kernel, block_count), "bridge_pairs", cost(1),
-        (RETURNED, BEST), 2, [], (place, stats, found, far_in, chip_in),
+        (RETURNED, BEST), 3, [], (place, far_list, stats, found, far_in, chip_in),
     )
     back = lax.ppermute(returned, "shard", across)
     mine, other = pair_call(
         functools.partial(chip_kernel, block_count), "chip_pairs", cost(4), (BEST, BEST),
-        3, EDGE_SCRATCH, (place, listing, stats, mine, other, units, chip_in),
+        2, EDGE_SCRATCH, (place, chip_list, mine, other, units, chip_in),
     )
     outgoing = finish(block_count, place, mine, other, back)
     groups = [list(range(c * 2 * REPS, (c + 1) * 2 * REPS)) for c in range(count // 2)]

time: 46.7 us -> 46.1 us (0.987); the launches traced: 46.5 us -> 46.5 us
  Pallas kernels: 15.5 us -> 24.4 us
  blocking collectives: 16.9 us -> 11.5 us
  starting transfers between devices: 12.5 us -> 9.8 us
  waiting for transfers between devices: 0.82 us -> 0.01 us
    pallas_call x4, Pallas kernels: 6 us -> 14.7 us  [pair_call(): pl.pallas_call(kernel, out_shape=outs, in_specs=[SMEM] * scalars + [VMEM]...]
    all_to_all x1, blocking collectives: 16.9 us -> 11.5 us  [shards(): lax.all_to_all(outgoing, ('shard', 'rep'), 0, 0, axis_index_groups=groups)]
    ppermute x1, starting transfers between devices: 4.33 us -> 1.92 us  [shards(): back = lax.ppermute(returned, 'shard', across)]
    ppermute x1, waiting for transfers between devices: 0.81 us -> 0.01 us  [shards(): far_in = in_vmem(lax.ppermute(far_out, 'shard', across))]
  transfers between devices with their start and end apart: 3 -> 3, of which waited for: 1 -> 0; matrix products, arithmetic and copies ran while one was open for 0% -> 0% of each run, Pallas kernels for 25% -> 42%
where the time goes in v4:
time: 46.1 us; the launch traced here: 46.5 us
  Pallas kernels  24.4 us (53%)
  blocking collectives  11.5 us (25%)
  starting transfers between devices  9.8 us (21%)
  other arithmetic  0.68 us (1%)
    pallas_call x4, Pallas kernels, pair_call(): pl.pallas_call(kernel, out_shape=outs, in_specs=[SMEM] * scalars + [VMEM]...  14.7 us
    all_to_all x1, blocking collectives, shards(): lax.all_to_all(outgoing, ('shard', 'rep'), 0, 0, axis_index_groups=groups)  11.5 us
    pallas_call x1, Pallas kernels, own_rows(): pl.pallas_call(functools.partial(rows_kernel, block_count), out_shape=(pl...  6.67 us
    ppermute x1, starting transfers between devices, shards(): far_in = in_vmem(lax.ppermute(far_out, 'shard', across))  4.11 us
    ppermute x1, starting transfers between devices, shards(): chip_in = in_vmem(lax.ppermute(chip_out, 'shard', within))  3.77 us
    pallas_call x1, Pallas kernels, far_rows(): pl.pallas_call(far_rows_kernel, out_shape=pltpu.VMEM((FAR_ROWS, WIDTH), j...  2.53 us
    ppermute x1, starting transfers between devices, shards(): back = lax.ppermute(returned, 'shard', across)  1.92 us
  transfers between devices with their start and end apart: 3, of which 0 were waited for; matrix products, arithmetic and copies ran while one was open for 0% of the time, Pallas kernels for 42%

profile of v4, /device:TPU:7, one launch (start us, length us, event | category | flops | bytes accessed | tf_op | source)
XLA Modules:
  0.0 46.5 jit_solution(6887475539090824233)
XLA Ops:
  0.0 0.1 pad_add_fusion.place
  0.1 0.0 copy-start
  0.1 2.5 %far_rows.1.far = bf16[528,1024]{1,0:T(8,128)(2,1)S(1)} custom-call(s32[2]{0:T(128)S(1)} %pad_add_fusion.place, s32[204]{0:T(256)} %bitcast.5, f32[3072,1024]{1,0:T(8,128)} %emb.3), custom_call_target="tpu_custom_call" | custom-call | bytes 3000000 | tf_op jit(solution)/shard_map/far_rows/pallas_call | solution.py:110
  2.6 4.1 %collective-permute-start = (bf16[528,1024]{1,0:T(8,128)(2,1)S(1)}, bf16[528,1024]{1,0:T(8,128)(2,1)S(1)}, u32[]{:S(2)}, u32[]{:S(2)}) collective-permute-start(bf16[528,1024]{1,0:T(8,128)(2,1)S(1)} %far_rows.1.far), channel_id=1, source_target_pairs={{4,8},{12,16},{20,24},{28,32},{36,40},{44,48},{52,56},{60,64},{68,... | collective-permute-start | bytes 3244040 | tf_op jit(solution)/shard_map/ppermute | solution.py:622
  6.7 0.0 copy-done
  6.7 6.7 %own_rows.1 = (bf16[3072,1024]{1,0:T(8,128)(2,1)S(1)}, bf16[1296,1024]{1,0:T(8,128)(2,1)S(1)}, f32[12,256]{1,0:T(8,128)S(1)}, s32[8,128]{1,0:T(8,128)S(1)}, s32[667]{0:T(1024)S(1)}) custom-call(s32[2]{0:T(128)S(1)} %pad_add_fusion.place, s32[204]{0:T(256)S(1)} %bitcast.6, s32[1536,128]{1,0:T(8,128)} %bitcast.8, bf16[528,1024]{1,0:T(8,128)(2,1)S(1)} %far_rows.1.far, ...), custom_call_target="tpu_custom_call" | custom-call | bytes 15000000 | tf_op jit(solution)/shard_map/own_rows/pallas_call | solution.py:348
  13.4 3.8 %collective-permute-start.1 = (bf16[1296,1024]{1,0:T(8,128)(2,1)S(1)}, bf16[1296,1024]{1,0:T(8,128)(2,1)S(1)}, u32[]{:S(2)}, u32[]{:S(2)}) collective-permute-start(bf16[1296,1024]{1,0:T(8,128)(2,1)S(1)} %get-tuple-element.28), channel_id=1, source_target_pairs={{0,4},{4,0},{8,12},{12,8},{16,20},{20,16},{24,28},{28,24},{32,36},... | collective-permute-start | bytes 7962632 | tf_op jit(solution)/shard_map/ppermute | solution.py:626
  17.2 5.1 %own_pairs.1 = (f32[12,256]{1,0:T(8,128)S(1)}, s32[290]{0:T(512)S(1)}, s32[290]{0:T(512)S(1)}) custom-call(s32[2]{0:T(128)S(1)} %pad_add_fusion.place, s32[204]{0:T(256)S(1)} %bitcast.7, s32[8,128]{1,0:T(8,128)S(1)} %get-tuple-element.19.stats, s32[667]{0:T(1024)S(1)} %get-tuple-element.20.own_tasks, f32[12,256]{1,0:T(8,128)S(1)} %get-tuple-element.21.best, ...), custom_call_target="tpu_custom_call" | custom-call | bytes 9000000 | tf_op jit(solution)/shard_map/own_pairs/pallas_call | solution.py:554
  22.3 0.0 collective-permute-done.far
  22.4 3.9 %far_pairs.1 = (f32[12,256]{1,0:T(8,128)S(1)}, f32[2,256]{1,0:T(2,128)S(1)}) custom-call(s32[2]{0:T(128)S(1)} %pad_add_fusion.place, s32[290]{0:T(512)S(1)} %get-tuple-element.24.far_list, f32[12,256]{1,0:T(8,128)S(1)} %get-tuple-element.25.best, bf16[3072,1024]{1,0:T(8,128)(2,1)S(1)} %get-tuple-element.22.units, bf16[528,1024]{1,0:T(8,128)(2,1)S(1)} %collective-permute-done.far), custom_call_target="tpu_custom_call" | custom-call | flops 99999997952 | bytes 12000000 | tf_op jit(solution)/shard_map/far_pairs/pallas_call | solution.py:554
  26.2 0.0 collective-permute-done.1.chip
  26.2 1.8 %bridge_pairs.1 = (f32[2,256]{1,0:T(2,128)S(1)}, f32[12,256]{1,0:T(8,128)S(1)}) custom-call(s32[2]{0:T(128)S(1)} %pad_add_fusion.place, s32[290]{0:T(512)S(1)} %get-tuple-element.24.far_list, s32[8,128]{1,0:T(8,128)S(1)} %get-tuple-element.19.stats, f32[2,256]{1,0:T(2,128)S(1)} %get-tuple-element.27.found, bf16[528,1024]{1,0:T(8,128)(2,1)S(1)} %collective-permute-done.far, ...), custom_call_target="tpu_custom_call" | custom-call | bytes 3000000 | tf_op jit(solution)/shard_map/bridge_pairs/pallas_call | solution.py:554
  28.0 1.9 %collective-permute-start.2 = (f32[2,256]{1,0:T(2,128)S(1)}, f32[2,256]{1,0:T(2,128)S(1)}, u32[]{:S(2)}, u32[]{:S(2)}) collective-permute-start(f32[2,256]{1,0:T(2,128)S(1)} %get-tuple-element.32), channel_id=1, source_target_pairs={{4,8},{12,16},{20,24},{28,32},{36,40},{44,48},{52,56},{60,64},{68,... | collective-permute-start | bytes 6152 | tf_op jit(solution)/shard_map/ppermute | solution.py:640
  29.9 3.9 %chip_pairs.1 = (f32[12,256]{1,0:T(8,128)S(1)}, f32[12,256]{1,0:T(8,128)S(1)}) custom-call(s32[2]{0:T(128)S(1)} %pad_add_fusion.place, s32[290]{0:T(512)S(1)} %get-tuple-element.23.chip_list, f32[12,256]{1,0:T(8,128)S(1)} %get-tuple-element.26.mine_in, f32[12,256]{1,0:T(8,128)S(1)} %get-tuple-element.29.other_in, ...), custom_call_target="tpu_custom_call" | custom-call | bytes 12000000 | tf_op jit(solution)/shard_map/chip_pairs/pallas_call | solution.py:554
  33.8 0.0 collective-permute-done.2.back
  33.8 0.6 %finish.1 = f32[8,24,128]{2,1,0:T(8,128)S(1)} custom-call(s32[2]{0:T(128)S(1)} %pad_add_fusion.place, f32[12,256]{1,0:T(8,128)S(1)} %get-tuple-element.30.mine, f32[12,256]{1,0:T(8,128)S(1)} %get-tuple-element.31.other, f32[2,256]{1,0:T(2,128)S(1)} %collective-permute-done.2.back), custom_call_target="tpu_custom_call" | custom-call | bytes 3000000 | tf_op jit(solution)/shard_map/finish/pallas_call | solution.py:595
  34.4 11.5 %all_to_all.5 = f32[8,24,128]{2,1,0:T(8,128)S(1)} all-to-all(f32[8,24,128]{2,1,0:T(8,128)S(1)} %finish.1), channel_id=1, replica_groups={{0,1,2,3,4,5,6,7},{8,9,10,11,12,13,14,15},{16,17,18,19,20,21,22,23},{24..., dimensions={0} | all-to-all | bytes 196608 | tf_op jit(solution)/shard_map/all_to_all | solution.py:647
  45.9 0.6 %reduce_max.9 = f32[24,128]{1,0:T(8,128)} reduce(f32[8,24,128]{2,1,0:T(8,128)S(1)} %all_to_all.5, f32[]{:T(128)} %constant.10.clone.1), dimensions={0}, to_apply=%region_0.0 | reduce | flops 21504 | bytes 110596 | tf_op jit(solution)/shard_map/reduce_max | solution.py:648
Async XLA Ops:
  0.1 6.7 %copy-start = (s32[204,1]{0,1:T(1,128)S(1)}, s32[204,1]{0,1:T(1,128)}, u32[]{:S(2)}) copy-start(s32[204,1]{0,1:T(1,128)} %param.5) | copy-start | bytes 2452
  2.6 19.7 %collective-permute-start = (bf16[528,1024]{1,0:T(8,128)(2,1)S(1)}, bf16[528,1024]{1,0:T(8,128)(2,1)S(1)}, u32[]{:S(2)}, u32[]{:S(2)}) collective-permute-start(bf16[528,1024]{1,0:T(8,128)(2,1)S(1)} %far_rows.1.far), channel_id=1, source_target_pairs={{4,8},{12,16},{20,24},{28,32},{36,40},{44,48},{52,56},{60,64},{68,... | collective-permute-start | bytes 3244040 | tf_op jit(solution)/shard_map/ppermute | solution.py:622
  13.4 12.8 %collective-permute-start.1 = (bf16[1296,1024]{1,0:T(8,128)(2,1)S(1)}, bf16[1296,1024]{1,0:T(8,128)(2,1)S(1)}, u32[]{:S(2)}, u32[]{:S(2)}) collective-permute-start(bf16[1296,1024]{1,0:T(8,128)(2,1)S(1)} %get-tuple-element.28), channel_id=1, source_target_pairs={{0,4},{4,0},{8,12},{12,8},{16,20},{20,16},{24,28},{28,24},{32,36},... | collective-permute-start | bytes 7962632 | tf_op jit(solution)/shard_map/ppermute | solution.py:626
  28.0 5.8 %collective-permute-start.2 = (f32[2,256]{1,0:T(2,128)S(1)}, f32[2,256]{1,0:T(2,128)S(1)}, u32[]{:S(2)}, u32[]{:S(2)}) collective-permute-start(f32[2,256]{1,0:T(2,128)S(1)} %get-tuple-element.32), channel_id=1, source_target_pairs={{4,8},{12,16},{20,24},{28,32},{36,40},{44,48},{52,56},{60,64},{68,... | collective-permute-start | bytes 6152 | tf_op jit(solution)/shard_map/ppermute | solution.py:640

commit v5 on v4

--- a/solution.py
+++ b/solution.py
@@ -12,6 +12,7 @@
 WIDTH = 1024
 OWN = 12
 REPS = 4
+MOVED = 8
 NEAR = 4
 CHIP_SLOTS = 2 + NEAR - 1
 FAR_SLOTS = 2
@@ -20,7 +21,7 @@
 CHIP_ROWS = CHIP_SLOTS * BLOCK + TAIL
 WINDOW = OWN + 2 * (SPANS - 1)
 GROUP = 8 * 128 // BLOCK
-CHUNK = 64
+CHUNK = 128
 WIDE, NARROW = 8, 4
 FIELDS = 9
 EPS = 1e-6
@@ -64,7 +65,7 @@
 
 
 def far_index(rep, slot):
-    return jnp.where(slot == 0, rep + 1, 8 - rep)
+    return jnp.where(slot == 0, rep + 1, MOVED - rep)
 
 
 def chip_index(rep, slot):
@@ -420,8 +421,35 @@
             jnp.where(before, 0, c_start), jnp.where(before, c_count, BLOCK),
         )
 
+    def lean(self, stats):
+        middle = self.shard * OWN + jnp.where(self.side == 0, 0, OWN)
+        facts = functools.partial(label_stats, stats, self.block_count, self.shard)
+        label = facts(middle - 1)[1]
+        ahead = lax.while_loop(
+            lambda n: (n < jnp.minimum(middle, SPANS - 1)) & (facts(middle - 1 - n)[1] == label),
+            lambda n: n + 1,
+            jnp.int32(0),
+        )
+        behind = lax.while_loop(
+            lambda n: (n < jnp.minimum(self.block_count - middle, SPANS - 1))
+            & (facts(middle + n)[0] == label),
+            lambda n: n + 1,
+            jnp.int32(0),
+        )
+        return behind - ahead
+
+    def first_column(self, near, lean):
+        half = lax.shift_right_arithmetic(lean, 1)
+        even = lean - 2 * half == 0
+        behind = near + half + jnp.where(even & (lax.rem(near, 2) == 1), 0, 1)
+        equal = near - half
+        tie = even & (lax.rem(equal + 32, 2) == 1)
+        ahead = equal + jnp.where(tie, 1, 0)
+        return jnp.clip(jnp.where(self.side == 0, behind, ahead), 1, MOVED + 1)
+
     def list_tasks(self, tasks, stats, holder):
         count = jnp.int32(0)
+        lean = self.lean(stats)
         for which in range(2):
             moved = self.start(stats, which)
             near, before, present, _ = moved
@@ -441,8 +469,7 @@
                 )
                 return m + 1, count
 
-            tie = lax.rem(near, 2) == 1 - self.side
-            first = jnp.where(tie, near, near + 1)
+            first = self.first_column(near, lean)
             _, count = lax.while_loop(shares, visit, (first, count))
         tasks[EDGE_TASKS] = count
 
@@ -495,8 +522,8 @@
         )
 
 
-def bridge_kernel(block_count, place, far_list, stats, found, far, chip, returned, other):
-    returned[...] = found[...]
+def bridge_kernel(block_count, place, far_list, stats, found_in, far, chip, returned, other):
+    returned[...] = found_in[...]
     other[...] = jnp.full(other.shape, -1.0, jnp.float32)
 
     @pl.when(far_list[EDGE_TASKS + 1] > 0)
@@ -506,7 +533,8 @@
         tail = chip[pl.ds(CHIP_SLOTS * BLOCK, TAIL), :]
         moved = edge.start(stats, 0)
         rows, cols = [], []
-        for slot in range(CHIP_SLOTS):
+        slots = (0, 2, 3, 4)
+        for slot in slots:
             m = OWN + chip_index(edge.rep, slot)
             offset, area = moved[0] + m - 1, edge.area(stats, moved, m)
             active = moved[2] & (offset < SPANS) & edge.shares(stats, moved, m)
@@ -517,10 +545,9 @@
             scored = jnp.where(active & listed, scored, -1.0)
             rows.append(fold_rows(scored))
             cols.append(fold_cols(scored))
-        for slot in range(CHIP_SLOTS):
+        for slot, found in zip(slots, cols):
             block = chip_local(1 - edge.core, chip_index(edge.rep, slot))
-            here = (pl.ds(block, 1), slice(None))
-            other[here] = jnp.max(cols[slot], axis=0, keepdims=True)
+            other[pl.ds(block, 1), :] = jnp.max(found, axis=0, keepdims=True)
         best = functools.reduce(jnp.maximum, rows)
         best = as_lanes(jnp.max(best, axis=1, keepdims=True))
         returned[0:1, :] = jnp.maximum(returned[0:1, :], best)

time: 46.1 us -> 45 us (0.976); the launches traced: 46.5 us -> 45 us
  Pallas kernels: 24.4 us -> 20.7 us
  blocking collectives: 11.5 us -> 13.5 us
    pallas_call x4, Pallas kernels: 14.7 us -> 11.2 us  [pair_call(): pl.pallas_call(kernel, out_shape=outs, in_specs=[SMEM] * scalars + [VMEM]...]
    all_to_all x1, blocking collectives: 11.5 us -> 13.5 us  [shards(): lax.all_to_all(outgoing, ('shard', 'rep'), 0, 0, axis_index_groups=groups)]
  transfers between devices with their start and end apart: 3 -> 3, of which waited for: 0 -> 1; matrix products, arithmetic and copies ran while one was open for 0% -> 0% of each run, Pallas kernels for 42% -> 38%
where the time goes in v5:
time: 45 us
  Pallas kernels  20.7 us (46%)
  blocking collectives  13.5 us (30%)
  starting transfers between devices  9.77 us (22%)
  other arithmetic  0.68 us (2%)
    all_to_all x1, blocking collectives, shards(): lax.all_to_all(outgoing, ('shard', 'rep'), 0, 0, axis_index_groups=groups)  13.5 us
    pallas_call x4, Pallas kernels, pair_call(): pl.pallas_call(kernel, out_shape=outs, in_specs=[SMEM] * scalars + [VMEM]...  11.2 us
    pallas_call x1, Pallas kernels, own_rows(): pl.pallas_call(functools.partial(rows_kernel, block_count), out_shape=(pl...  6.68 us
    ppermute x1, starting transfers between devices, shards(): far_in = in_vmem(lax.ppermute(far_out, 'shard', across))  4.11 us
    ppermute x1, starting transfers between devices, shards(): chip_in = in_vmem(lax.ppermute(chip_out, 'shard', within))  3.74 us
    pallas_call x1, Pallas kernels, far_rows(): pl.pallas_call(far_rows_kernel, out_shape=pltpu.VMEM((FAR_ROWS, WIDTH), j...  2.29 us
    ppermute x1, starting transfers between devices, shards(): back = lax.ppermute(returned, 'shard', across)  1.92 us
  transfers between devices with their start and end apart: 3, of which 1 were waited for; matrix products, arithmetic and copies ran while one was open for 0% of the time, Pallas kernels for 38%

profile of v5, /device:TPU:7, one launch (start us, length us, event | category | flops | bytes accessed | tf_op | source)
XLA Modules:
  0.0 45.0 jit_solution(2043621193682134312)
XLA Ops:
  0.0 0.1 pad_add_fusion.place
  0.1 0.0 copy-start
  0.1 2.3 %far_rows.1.far = bf16[528,1024]{1,0:T(8,128)(2,1)S(1)} custom-call(s32[2]{0:T(128)S(1)} %pad_add_fusion.place, s32[204]{0:T(256)} %bitcast.5, f32[3072,1024]{1,0:T(8,128)} %emb.3), custom_call_target="tpu_custom_call" | custom-call | bytes 3000000 | tf_op jit(solution)/shard_map/far_rows/pallas_call | solution.py:111
  2.4 4.1 %collective-permute-start = (bf16[528,1024]{1,0:T(8,128)(2,1)S(1)}, bf16[528,1024]{1,0:T(8,128)(2,1)S(1)}, u32[]{:S(2)}, u32[]{:S(2)}) collective-permute-start(bf16[528,1024]{1,0:T(8,128)(2,1)S(1)} %far_rows.1.far), channel_id=1, source_target_pairs={{4,8},{12,16},{20,24},{28,32},{36,40},{44,48},{52,56},{60,64},{68,... | collective-permute-start | bytes 3244040 | tf_op jit(solution)/shard_map/ppermute | solution.py:649
  6.5 0.0 copy-done
  6.5 6.7 %own_rows.1 = (bf16[3072,1024]{1,0:T(8,128)(2,1)S(1)}, bf16[1296,1024]{1,0:T(8,128)(2,1)S(1)}, f32[12,256]{1,0:T(8,128)S(1)}, s32[8,128]{1,0:T(8,128)S(1)}, s32[667]{0:T(1024)S(1)}) custom-call(s32[2]{0:T(128)S(1)} %pad_add_fusion.place, s32[204]{0:T(256)S(1)} %bitcast.6, s32[1536,128]{1,0:T(8,128)} %bitcast.8, bf16[528,1024]{1,0:T(8,128)(2,1)S(1)} %far_rows.1.far, ...), custom_call_target="tpu_custom_call" | custom-call | bytes 15000000 | tf_op jit(solution)/shard_map/own_rows/pallas_call | solution.py:349
  13.2 3.7 %collective-permute-start.1 = (bf16[1296,1024]{1,0:T(8,128)(2,1)S(1)}, bf16[1296,1024]{1,0:T(8,128)(2,1)S(1)}, u32[]{:S(2)}, u32[]{:S(2)}) collective-permute-start(bf16[1296,1024]{1,0:T(8,128)(2,1)S(1)} %get-tuple-element.28), channel_id=1, source_target_pairs={{0,4},{4,0},{8,12},{12,8},{16,20},{20,16},{24,28},{28,24},{32,36},... | collective-permute-start | bytes 7962632 | tf_op jit(solution)/shard_map/ppermute | solution.py:653
  16.9 5.8 %own_pairs.1 = (f32[12,256]{1,0:T(8,128)S(1)}, s32[290]{0:T(512)S(1)}, s32[290]{0:T(512)S(1)}) custom-call(s32[2]{0:T(128)S(1)} %pad_add_fusion.place, s32[204]{0:T(256)S(1)} %bitcast.7, s32[8,128]{1,0:T(8,128)S(1)} %get-tuple-element.19.stats, s32[667]{0:T(1024)S(1)} %get-tuple-element.20.own_tasks, f32[12,256]{1,0:T(8,128)S(1)} %get-tuple-element.21.best, ...), custom_call_target="tpu_custom_call" | custom-call | bytes 9000000 | tf_op jit(solution)/shard_map/own_pairs/pallas_call | solution.py:581
  22.8 0.0 collective-permute-done.far
  22.8 1.9 %far_pairs.1 = (f32[12,256]{1,0:T(8,128)S(1)}, f32[2,256]{1,0:T(2,128)S(1)}) custom-call(s32[2]{0:T(128)S(1)} %pad_add_fusion.place, s32[290]{0:T(512)S(1)} %get-tuple-element.24.far_list, f32[12,256]{1,0:T(8,128)S(1)} %get-tuple-element.25.best, bf16[3072,1024]{1,0:T(8,128)(2,1)S(1)} %get-tuple-element.22.units, bf16[528,1024]{1,0:T(8,128)(2,1)S(1)} %collective-permute-done.far), custom_call_target="tpu_custom_call" | custom-call | flops 99999997952 | bytes 12000000 | tf_op jit(solution)/shard_map/far_pairs/pallas_call | solution.py:581
  24.7 0.0 collective-permute-done.1.chip
  24.7 0.6 %bridge_pairs.1 = (f32[2,256]{1,0:T(2,128)S(1)}, f32[12,256]{1,0:T(8,128)S(1)}) custom-call(s32[2]{0:T(128)S(1)} %pad_add_fusion.place, s32[290]{0:T(512)S(1)} %get-tuple-element.24.far_list, s32[8,128]{1,0:T(8,128)S(1)} %get-tuple-element.19.stats, f32[2,256]{1,0:T(2,128)S(1)} %get-tuple-element.27.found_in, ...), custom_call_target="tpu_custom_call" | custom-call | bytes 3000000 | tf_op jit(solution)/shard_map/bridge_pairs/pallas_call | solution.py:581
  25.3 1.9 %collective-permute-start.2 = (f32[2,256]{1,0:T(2,128)S(1)}, f32[2,256]{1,0:T(2,128)S(1)}, u32[]{:S(2)}, u32[]{:S(2)}) collective-permute-start(f32[2,256]{1,0:T(2,128)S(1)} %get-tuple-element.32), channel_id=1, source_target_pairs={{4,8},{12,16},{20,24},{28,32},{36,40},{44,48},{52,56},{60,64},{68,... | collective-permute-start | bytes 6152 | tf_op jit(solution)/shard_map/ppermute | solution.py:667
  27.3 2.8 %chip_pairs.1 = (f32[12,256]{1,0:T(8,128)S(1)}, f32[12,256]{1,0:T(8,128)S(1)}) custom-call(s32[2]{0:T(128)S(1)} %pad_add_fusion.place, s32[290]{0:T(512)S(1)} %get-tuple-element.23.chip_list, f32[12,256]{1,0:T(8,128)S(1)} %get-tuple-element.26.mine_in, f32[12,256]{1,0:T(8,128)S(1)} %get-tuple-element.29.other_in, ...), custom_call_target="tpu_custom_call" | custom-call | bytes 12000000 | tf_op jit(solution)/shard_map/chip_pairs/pallas_call | solution.py:581
  30.1 0.1 collective-permute-done.2.back
  30.2 0.6 %finish.1 = f32[8,24,128]{2,1,0:T(8,128)S(1)} custom-call(s32[2]{0:T(128)S(1)} %pad_add_fusion.place, f32[12,256]{1,0:T(8,128)S(1)} %get-tuple-element.30.mine, f32[12,256]{1,0:T(8,128)S(1)} %get-tuple-element.31.other, f32[2,256]{1,0:T(2,128)S(1)} %collective-permute-done.2.back), custom_call_target="tpu_custom_call" | custom-call | bytes 3000000 | tf_op jit(solution)/shard_map/finish/pallas_call | solution.py:622
  30.8 13.5 %all_to_all.5 = f32[8,24,128]{2,1,0:T(8,128)S(1)} all-to-all(f32[8,24,128]{2,1,0:T(8,128)S(1)} %finish.1), channel_id=1, replica_groups={{0,1,2,3,4,5,6,7},{8,9,10,11,12,13,14,15},{16,17,18,19,20,21,22,23},{24..., dimensions={0} | all-to-all | bytes 196608 | tf_op jit(solution)/shard_map/all_to_all | solution.py:674
  44.3 0.6 %reduce_max.9 = f32[24,128]{1,0:T(8,128)} reduce(f32[8,24,128]{2,1,0:T(8,128)S(1)} %all_to_all.5, f32[]{:T(128)} %constant.10.clone.1), dimensions={0}, to_apply=%region_0.0 | reduce | flops 21504 | bytes 110596 | tf_op jit(solution)/shard_map/reduce_max | solution.py:675
Async XLA Ops:
  0.1 6.4 %copy-start = (s32[204,1]{0,1:T(1,128)S(1)}, s32[204,1]{0,1:T(1,128)}, u32[]{:S(2)}) copy-start(s32[204,1]{0,1:T(1,128)} %param.5) | copy-start | bytes 2452
  2.4 20.4 %collective-permute-start = (bf16[528,1024]{1,0:T(8,128)(2,1)S(1)}, bf16[528,1024]{1,0:T(8,128)(2,1)S(1)}, u32[]{:S(2)}, u32[]{:S(2)}) collective-permute-start(bf16[528,1024]{1,0:T(8,128)(2,1)S(1)} %far_rows.1.far), channel_id=1, source_target_pairs={{4,8},{12,16},{20,24},{28,32},{36,40},{44,48},{52,56},{60,64},{68,... | collective-permute-start | bytes 3244040 | tf_op jit(solution)/shard_map/ppermute | solution.py:649
  13.2 11.5 %collective-permute-start.1 = (bf16[1296,1024]{1,0:T(8,128)(2,1)S(1)}, bf16[1296,1024]{1,0:T(8,128)(2,1)S(1)}, u32[]{:S(2)}, u32[]{:S(2)}) collective-permute-start(bf16[1296,1024]{1,0:T(8,128)(2,1)S(1)} %get-tuple-element.28), channel_id=1, source_target_pairs={{0,4},{4,0},{8,12},{12,8},{16,20},{20,16},{24,28},{28,24},{32,36},... | collective-permute-start | bytes 7962632 | tf_op jit(solution)/shard_map/ppermute | solution.py:653
  25.3 4.9 %collective-permute-start.2 = (f32[2,256]{1,0:T(2,128)S(1)}, f32[2,256]{1,0:T(2,128)S(1)}, u32[]{:S(2)}, u32[]{:S(2)}) collective-permute-start(f32[2,256]{1,0:T(2,128)S(1)} %get-tuple-element.32), channel_id=1, source_target_pairs={{4,8},{12,16},{20,24},{28,32},{36,40},{44,48},{52,56},{60,64},{68,... | collective-permute-start | bytes 6152 | tf_op jit(solution)/shard_map/ppermute | solution.py:667

commit v6 on v5

--- a/solution.py
+++ b/solution.py
@@ -234,8 +234,8 @@
 
 def rows_kernel(
     block_count, place, holder, labels, far, emb,
-    units, chip_out, best, stats, tasks,
-    raw, tags, table, sems, far_sems, out_sems, tag_sem, table_sem,
+    units, chip_out, best, stats,
+    raw, tags, sems, tag_sem,
 ):
     shard, rep = place[0], place[1]
     core = lax.rem(shard, 2)
@@ -248,16 +248,6 @@
             emb.at[rows_of(block)], raw.at[rows_of(block)], sems.at[block]
         )
 
-    def reuse(slot):
-        return pltpu.make_async_copy(
-            far.at[rows_of(slot)], units.at[rows_of(sent[slot])], far_sems.at[slot]
-        )
-
-    def push(slot):
-        return pltpu.make_async_copy(
-            units.at[rows_of(local[slot])], chip_out.at[rows_of(slot)], out_sems.at[slot]
-        )
-
     def is_new(block):
         return (block != sent[0]) & (block != sent[1])
 
@@ -265,22 +255,19 @@
     fetch_tags = pltpu.make_async_copy(labels.at[window], tags, tag_sem)
     fetch_tags.start()
 
-    @pl.loop(1, OWN + 1)
-    def _(m):
+    def request(m):
         block = chip_local(core, m)
         pl.when(is_new(block))(lambda: fetch(block).start())
 
-    for slot in range(FAR_SLOTS):
-        reuse(slot).start()
+    pl.loop(1, 5)(request)
     chip_out[CHIP_SLOTS * BLOCK :, :] = jnp.zeros((TAIL, WIDTH), jnp.bfloat16)
     chip_out[CHIP_SLOTS * BLOCK :, 0:128] = flag_rows(holder, local)
     best[...] = jnp.full(best.shape, -1.0, jnp.float32)
+    for slot in range(FAR_SLOTS):
+        units[rows_of(sent[slot]), :] = far[rows_of(slot), :]
     fetch_tags.wait()
-    write_stats(tags, table)
-    to_scalars = pltpu.make_async_copy(table, stats, table_sem)
-    to_scalars.start()
-    for slot in range(FAR_SLOTS):
-        reuse(slot).wait()
+    write_stats(tags, stats)
+    pl.loop(5, OWN + 1)(request)
 
     def diagonal(block):
         at = (shard * OWN + block - group * GROUP) * 2
@@ -308,41 +295,17 @@
             mine = mine | (block == local_class(rep, turn))
         pl.when(mine)(lambda: diagonal(block))
 
-    pl.loop(1, 9)(arrive)
-    for slot in range(CHIP_SLOTS):
-        push(slot).start()
-
-    to_scalars.wait()
-
-    def label_facts(block):
-        return label_stats(stats, block_count, shard, shard * OWN + block)
-
-    count = jnp.int32(0)
-    for turn in range(3):
-        block = local_class(rep, turn)
-        b_first, _, b_count, _ = label_facts(block)
-
-        def shares(state, b_first=b_first):
-            other, _ = state
-            return (other >= 0) & (label_facts(jnp.maximum(other, 0))[1] == b_first)
-
-        def visit(state, block=block, turn=turn, b_count=b_count):
-            other, count = state
-            listed = holder[other * SPANS + (block - other)] != REPS
-            a_start = label_facts(other)[3]
-            count = put_task(
-                tasks, count, listed, block, other, 0, b_count, a_start, BLOCK, turn, other,
-                block - other,
-            )
-            return other - 1, count
-
-        _, count = lax.while_loop(shares, visit, (block - 1, count))
-    pad_tasks(tasks, count)
-    tasks[OWN_TASKS] = count
-
-    pl.loop(9, OWN + 1)(arrive)
-    for slot in range(CHIP_SLOTS):
-        push(slot).wait()
+    def arrive_and_send(m):
+        arrive(m)
+        block = chip_local(core, m)
+        for slot in range(CHIP_SLOTS):
+
+            @pl.when(block == local[slot])
+            def _(slot=slot):
+                chip_out[rows_of(slot), :] = units[rows_of(block), :]
+
+    pl.loop(1, MOVED + 1)(arrive_and_send)
+    pl.loop(MOVED + 1, OWN + 1)(arrive)
 
 
 def own_rows(block_count, place, holder, labels, far, emb):
@@ -352,19 +315,14 @@
             pltpu.VMEM((OWN * BLOCK, WIDTH), jnp.bfloat16),
             pltpu.VMEM((CHIP_ROWS, WIDTH), jnp.bfloat16),
             pltpu.VMEM((OWN, BLOCK), jnp.float32),
-            jax.ShapeDtypeStruct((8, 128), jnp.int32),
-            jax.ShapeDtypeStruct((OWN_TASKS + 1,), jnp.int32),
+            pltpu.VMEM((8, 128), jnp.int32),
         ),
         in_specs=[SMEM, SMEM, HBM, VMEM, HBM],
-        out_specs=(VMEM, VMEM, VMEM, SMEM, SMEM),
+        out_specs=(VMEM, VMEM, VMEM, VMEM),
         scratch_shapes=[
             pltpu.VMEM((OWN * BLOCK, WIDTH), jnp.float32),
             pltpu.VMEM((WINDOW * 2, 128), jnp.int32),
-            pltpu.VMEM((8, 128), jnp.int32),
             pltpu.SemaphoreType.DMA((OWN,)),
-            pltpu.SemaphoreType.DMA((FAR_SLOTS,)),
-            pltpu.SemaphoreType.DMA((CHIP_SLOTS,)),
-            pltpu.SemaphoreType.DMA,
             pltpu.SemaphoreType.DMA,
         ],
         compiler_params=PARAMS,
@@ -379,6 +337,10 @@
     weight = lax.shift_left(jnp.int32(1), jnp.minimum(lane, SPANS)).astype(jnp.float32)
     weight = jnp.where((row == slot) & (lane < SPANS), weight, 0.0)
     return jnp.sum(tail[:, 0:128].astype(jnp.float32) * weight).astype(jnp.int32)
+
+
+def has_bit(bits, offset):
+    return lax.rem(lax.shift_right_logical(bits, offset), 2) == 1
 
 
 class Boundary:
@@ -447,7 +409,7 @@
         ahead = equal + jnp.where(tie, 1, 0)
         return jnp.clip(jnp.where(self.side == 0, behind, ahead), 1, MOVED + 1)
 
-    def list_tasks(self, tasks, stats, holder):
+    def list_tasks(self, tasks, stats, holder, bits=None):
         count = jnp.int32(0)
         lean = self.lean(stats)
         for which in range(2):
@@ -462,7 +424,9 @@
             def visit(state, which=which, moved=moved, near=near, before=before):
                 m, count = state
                 column, offset = self.local(m), near + m - 1
-                listed = before | (holder[column * SPANS + offset] != REPS)
+                moved_flag = True if bits is None else has_bit(bits[which], offset)
+                column_flag = holder[column * SPANS + offset] != REPS
+                listed = (before & moved_flag) | (jnp.logical_not(before) & column_flag)
                 area = self.area(stats, moved, m)
                 count = put_task(
                     tasks, count, listed, which, column, *area, which, column, offset
@@ -471,13 +435,12 @@
 
             first = self.first_column(near, lean)
             _, count = lax.while_loop(shares, visit, (first, count))
-        tasks[EDGE_TASKS] = count
+        return count
 
     def keep_listed(self, found, tasks, bits):
         def visit(index, count):
             task = [found[index * FIELDS + field] for field in range(FIELDS)]
-            flags = jnp.where(task[0] == 0, bits[0], bits[1])
-            listed = lax.rem(lax.shift_right_logical(flags, task[8]), 2) == 1
+            listed = has_bit(jnp.where(task[0] == 0, bits[0], bits[1]), task[8])
             return put_task(tasks, count, (self.side == 1) | listed, *task)
 
         count = lax.fori_loop(0, found[EDGE_TASKS], visit, jnp.int32(0))
@@ -486,23 +449,47 @@
 
 
 def own_kernel(
-    block_count, place, holder, stats, own_tasks, best, units,
-    mine, far_list, chip_list, row_acc, col_acc,
+    block_count, place, holder, stats, best, units, mine, far_list, row_acc, col_acc, tasks
 ):
     col_acc[...] = jnp.full(col_acc.shape, -1.0, jnp.float32)
     row_acc[...] = jnp.full(row_acc.shape, -1.0, jnp.float32)
-    run_tasks(own_tasks, own_tasks[OWN_TASKS], units, units, row_acc, col_acc)
+    shard, rep = place[0], place[1]
+
+    def label_facts(block):
+        return label_stats(stats, block_count, shard, shard * OWN + block)
+
+    count = jnp.int32(0)
+    for turn in range(3):
+        block = local_class(rep, turn)
+        b_first, _, b_count, _ = label_facts(block)
+
+        def shares(state, b_first=b_first):
+            other, _ = state
+            return (other >= 0) & (label_facts(jnp.maximum(other, 0))[1] == b_first)
+
+        def visit(state, block=block, turn=turn, b_count=b_count):
+            other, count = state
+            listed = holder[other * SPANS + (block - other)] != REPS
+            a_start = label_facts(other)[3]
+            count = put_task(
+                tasks, count, listed, block, other, 0, b_count, a_start, BLOCK, turn, other,
+                block - other,
+            )
+            return other - 1, count
+
+        _, count = lax.while_loop(shares, visit, (block - 1, count))
+    pad_tasks(tasks, count)
+    run_tasks(tasks, count, units, units, row_acc, col_acc)
     mine[...] = jnp.maximum(best[...], jnp.max(col_acc[...], axis=1))
     for turn in range(3):
         here = (pl.ds(local_class(place[1], turn), 1), slice(None))
         found = as_lanes(jnp.max(row_acc[turn], axis=1, keepdims=True))
         mine[here] = jnp.maximum(mine[here], found)
     edge = Boundary(True, block_count, place)
-    edge.list_tasks(far_list, stats, holder)
+    far_list[EDGE_TASKS] = edge.list_tasks(far_list, stats, holder)
     moved = edge.start(stats, 0)
     bridged = moved[2] & edge.shares(stats, moved, OWN + 1)
     far_list[EDGE_TASKS + 1] = bridged.astype(jnp.int32)
-    Boundary(False, block_count, place).list_tasks(chip_list, stats, holder)
 
 
 def far_kernel(
@@ -540,7 +527,7 @@
             active = moved[2] & (offset < SPANS) & edge.shares(stats, moved, m)
             offset = jnp.minimum(offset, SPANS - 1)
             bits = jnp.where(edge.side == 0, far_bits, flag_bits(tail, slot))
-            listed = lax.rem(lax.shift_right_logical(bits, offset), 2) == 1
+            listed = has_bit(bits, offset)
             scored = inside(similarity(far[0:BLOCK, :], chip[rows_of(slot), :]), *area)
             scored = jnp.where(active & listed, scored, -1.0)
             rows.append(fold_rows(scored))
@@ -554,7 +541,7 @@
 
 
 def chip_kernel(
-    block_count, place, chip_list, mine_in, other_in, units, chip,
+    block_count, place, holder, stats, mine_in, other_in, units, chip,
     mine, other, row_acc, col_acc, tasks,
 ):
     edge = Boundary(False, block_count, place)
@@ -562,7 +549,8 @@
     row_acc[...] = jnp.full(row_acc.shape, -1.0, jnp.float32)
     tail = chip[pl.ds(CHIP_SLOTS * BLOCK, TAIL), :]
     bits = [flag_bits(tail, slot) for slot in range(2)]
-    count = edge.keep_listed(chip_list, tasks, bits)
+    count = edge.list_tasks(tasks, stats, holder, bits)
+    pad_tasks(tasks, count)
     run_tasks(tasks, count, chip, units, row_acc, col_acc)
     mine[...] = jnp.maximum(mine_in[...], jnp.max(col_acc[...], axis=1))
     other[...] = other_in[...]
@@ -593,6 +581,7 @@
 OWN_SCRATCH = [
     pltpu.VMEM((3, BLOCK, 128), jnp.float32),
     pltpu.VMEM((OWN, 8, BLOCK), jnp.float32),
+    pltpu.SMEM((OWN_TASKS,), jnp.int32),
 ]
 EDGE_SCRATCH = [
     pltpu.VMEM((2, BLOCK, 128), jnp.float32),
@@ -647,14 +636,14 @@
 
     far_out = far_rows(place, listing, embeddings)
     far_in = in_vmem(lax.ppermute(far_out, "shard", across))
-    units, chip_out, best, stats, tasks = own_rows(
+    units, chip_out, best, stats = own_rows(
         block_count, place, listing, labels, far_out, embeddings
     )
     chip_in = in_vmem(lax.ppermute(chip_out, "shard", within))
 
-    mine, far_list, chip_list = pair_call(
-        functools.partial(own_kernel, block_count), "own_pairs", cost(3), (BEST, LIST, LIST),
-        4, OWN_SCRATCH, (place, listing, stats, tasks, best, units),
+    mine, far_list = pair_call(
+        functools.partial(own_kernel, block_count), "own_pairs", cost(3), (BEST, LIST),
+        3, OWN_SCRATCH, (place, listing, stats, best, units),
     )
     mine, found = pair_call(
         functools.partial(far_kernel, block_count), "far_pairs", cost(4, 10**11),
@@ -667,7 +656,7 @@
     back = lax.ppermute(returned, "shard", across)
     mine, other = pair_call(
         functools.partial(chip_kernel, block_count), "chip_pairs", cost(4), (BEST, BEST),
-        2, EDGE_SCRATCH, (place, chip_list, mine, other, units, chip_in),
+        3, EDGE_SCRATCH, (place, listing, stats, mine, other, units, chip_in),
     )
     outgoing = finish(block_count, place, mine, other, back)
     groups = [list(range(c * 2 * REPS, (c + 1) * 2 * REPS)) for c in range(count // 2)]

time: 45 us -> 45 us (level)
  blocking collectives: 13.5 us -> 11.5 us
  waiting for transfers between devices: 0.14 us -> 0.86 us
  Pallas kernels: 20.7 us -> 21.3 us
    all_to_all x1, blocking collectives: 13.5 us -> 11.5 us  [shards(): lax.all_to_all(outgoing, ('shard', 'rep'), 0, 0, axis_index_groups=groups)]
    pallas_call x4, Pallas kernels: 11.2 us -> 12.9 us  [pair_call(): pl.pallas_call(kernel, out_shape=outs, in_specs=[SMEM] * scalars + [VMEM]...]
    pallas_call x1, Pallas kernels: 6.68 us -> 5.5 us  [own_rows(): pl.pallas_call(functools.partial(rows_kernel, block_count), out_shape=(pl...]
    ppermute x1, waiting for transfers between devices: 0.14 us -> 0.85 us  [shards(): back = lax.ppermute(returned, 'shard', across)]
where the time goes in v6:
time: 45 us; the launch traced here: 44.5 us
  Pallas kernels  21.3 us (47%)
  blocking collectives  11.5 us (26%)
  starting transfers between devices  10.1 us (22%)
  waiting for transfers between devices  0.86 us (2%)
  other arithmetic  0.68 us (2%)
    pallas_call x4, Pallas kernels, pair_call(): pl.pallas_call(kernel, out_shape=outs, in_specs=[SMEM] * scalars + [VMEM]...  12.9 us
    all_to_all x1, blocking collectives, shards(): lax.all_to_all(outgoing, ('shard', 'rep'), 0, 0, axis_index_groups=groups)  11.5 us
    pallas_call x1, Pallas kernels, own_rows(): pl.pallas_call(functools.partial(rows_kernel, block_count), out_shape=(pl...  5.5 us
    ppermute x1, starting transfers between devices, shards(): far_in = in_vmem(lax.ppermute(far_out, 'shard', across))  4.11 us
    ppermute x1, starting transfers between devices, shards(): chip_in = in_vmem(lax.ppermute(chip_out, 'shard', within))  4.09 us
    pallas_call x1, Pallas kernels, far_rows(): pl.pallas_call(far_rows_kernel, out_shape=pltpu.VMEM((FAR_ROWS, WIDTH), j...  2.29 us
    ppermute x1, starting transfers between devices, shards(): back = lax.ppermute(returned, 'shard', across)  1.92 us
  transfers between devices with their start and end apart: 3, of which 1 were waited for; matrix products, arithmetic and copies ran while one was open for 0% of the time, Pallas kernels for 38%

profile of v6, /device:TPU:7, one launch (start us, length us, event | category | flops | bytes accessed | tf_op | source)
XLA Modules:
  0.0 44.5 jit_solution(16738688380390980184)
XLA Ops:
  0.0 0.1 pad_add_fusion.place
  0.1 0.0 copy-start
  0.1 2.3 %far_rows.1.far = bf16[528,1024]{1,0:T(8,128)(2,1)S(1)} custom-call(s32[2]{0:T(128)S(1)} %pad_add_fusion.place, s32[204]{0:T(256)} %bitcast.5, f32[3072,1024]{1,0:T(8,128)} %emb.3), custom_call_target="tpu_custom_call" | custom-call | bytes 3000000 | tf_op jit(solution)/shard_map/far_rows/pallas_call | solution.py:111
  2.4 4.1 %collective-permute-start = (bf16[528,1024]{1,0:T(8,128)(2,1)S(1)}, bf16[528,1024]{1,0:T(8,128)(2,1)S(1)}, u32[]{:S(2)}, u32[]{:S(2)}) collective-permute-start(bf16[528,1024]{1,0:T(8,128)(2,1)S(1)} %far_rows.1.far), channel_id=1, source_target_pairs={{4,8},{12,16},{20,24},{28,32},{36,40},{44,48},{52,56},{60,64},{68,... | collective-permute-start | bytes 3244040 | tf_op jit(solution)/shard_map/ppermute | solution.py:638
  6.5 0.0 copy-done
  6.5 5.5 %own_rows.1 = (bf16[3072,1024]{1,0:T(8,128)(2,1)S(1)}, bf16[1296,1024]{1,0:T(8,128)(2,1)S(1)}, f32[12,256]{1,0:T(8,128)S(1)}, s32[8,128]{1,0:T(8,128)S(1)}) custom-call(s32[2]{0:T(128)S(1)} %pad_add_fusion.place, s32[204]{0:T(256)S(1)} %bitcast.6, s32[1536,128]{1,0:T(8,128)} %bitcast.9, bf16[528,1024]{1,0:T(8,128)(2,1)S(1)} %far_rows.1.far, f32[3072,1024]{1,0:T(8,128)} %emb.3), custom_call_target="tpu_custom_call" | custom-call | bytes 15000000 | tf_op jit(solution)/shard_map/own_rows/pallas_call | solution.py:312
  12.0 4.1 %collective-permute-start.1 = (bf16[1296,1024]{1,0:T(8,128)(2,1)S(1)}, bf16[1296,1024]{1,0:T(8,128)(2,1)S(1)}, u32[]{:S(2)}, u32[]{:S(2)}) collective-permute-start(bf16[1296,1024]{1,0:T(8,128)(2,1)S(1)} %get-tuple-element.24), channel_id=1, source_target_pairs={{0,4},{4,0},{8,12},{12,8},{16,20},{20,16},{24,28},{28,24},{32,36},... | collective-permute-start | bytes 7962632 | tf_op jit(solution)/shard_map/ppermute | solution.py:642
  16.1 6.1 %own_pairs.1 = (f32[12,256]{1,0:T(8,128)S(1)}, s32[290]{0:T(512)S(1)}) custom-call(s32[2]{0:T(128)S(1)} %pad_add_fusion.place, s32[204]{0:T(256)S(1)} %bitcast.7, s32[8,128]{1,0:T(8,128)S(1)} %get-tuple-element.17.stats, f32[12,256]{1,0:T(8,128)S(1)} %get-tuple-element.18.best, bf16[3072,1024]{1,0:T(8,128)(2,1)S(1)} %get-tuple-element.19.units), custom_call_target="tpu_custom_call" | custom-call | bytes 9000000 | tf_op jit(solution)/shard_map/own_pairs/pallas_call | solution.py:569
  22.2 0.0 collective-permute-done.far
  22.2 2.8 %far_pairs.1 = (f32[12,256]{1,0:T(8,128)S(1)}, f32[2,256]{1,0:T(2,128)S(1)}) custom-call(s32[2]{0:T(128)S(1)} %pad_add_fusion.place, s32[290]{0:T(512)S(1)} %get-tuple-element.20.far_list, f32[12,256]{1,0:T(8,128)S(1)} %get-tuple-element.21.best, bf16[3072,1024]{1,0:T(8,128)(2,1)S(1)} %get-tuple-element.19.units, bf16[528,1024]{1,0:T(8,128)(2,1)S(1)} %collective-permute-done.far), custom_call_target="tpu_custom_call" | custom-call | flops 99999997952 | bytes 12000000 | tf_op jit(solution)/shard_map/far_pairs/pallas_call | solution.py:569
  25.0 0.0 collective-permute-done.1.chip
  25.0 1.6 %bridge_pairs.1 = (f32[2,256]{1,0:T(2,128)S(1)}, f32[12,256]{1,0:T(8,128)S(1)}) custom-call(s32[2]{0:T(128)S(1)} %pad_add_fusion.place, s32[290]{0:T(512)S(1)} %get-tuple-element.20.far_list, s32[8,128]{1,0:T(8,128)S(1)} %get-tuple-element.17.stats, f32[2,256]{1,0:T(2,128)S(1)} %get-tuple-element.23.found_in, ...), custom_call_target="tpu_custom_call" | custom-call | bytes 3000000 | tf_op jit(solution)/shard_map/bridge_pairs/pallas_call | solution.py:569
  26.6 1.9 %collective-permute-start.2 = (f32[2,256]{1,0:T(2,128)S(1)}, f32[2,256]{1,0:T(2,128)S(1)}, u32[]{:S(2)}, u32[]{:S(2)}) collective-permute-start(f32[2,256]{1,0:T(2,128)S(1)} %get-tuple-element.28), channel_id=1, source_target_pairs={{4,8},{12,16},{20,24},{28,32},{36,40},{44,48},{52,56},{60,64},{68,... | collective-permute-start | bytes 6152 | tf_op jit(solution)/shard_map/ppermute | solution.py:656
  28.5 2.4 %chip_pairs.1 = (f32[12,256]{1,0:T(8,128)S(1)}, f32[12,256]{1,0:T(8,128)S(1)}) custom-call(s32[2]{0:T(128)S(1)} %pad_add_fusion.place, s32[204]{0:T(256)S(1)} %bitcast.8, s32[8,128]{1,0:T(8,128)S(1)} %get-tuple-element.17.stats, f32[12,256]{1,0:T(8,128)S(1)} %get-tuple-element.22.mine_in, f32[12,256]{1,0:T(8,128)S(1)} %get-tuple-element.25.other_in, ...), custom_call_target="tpu_custom_call" | custom-call | bytes 12000000 | tf_op jit(solution)/shard_map/chip_pairs/pallas_call | solution.py:569
  31.0 0.8 %collective-permute-done.2.back = f32[2,256]{1,0:T(2,128)S(1)} collective-permute-done((f32[2,256]{1,0:T(2,128)S(1)}, f32[2,256]{1,0:T(2,128)S(1)}, u32[]{:S(2)}, u32[]{:S(2)}) %collective-permute-start.2) | collective-permute-done | bytes 2080 | tf_op jit(solution)/shard_map/ppermute | solution.py:656
  31.8 0.6 %finish.1 = f32[8,24,128]{2,1,0:T(8,128)S(1)} custom-call(s32[2]{0:T(128)S(1)} %pad_add_fusion.place, f32[12,256]{1,0:T(8,128)S(1)} %get-tuple-element.26.mine, f32[12,256]{1,0:T(8,128)S(1)} %get-tuple-element.27.other, f32[2,256]{1,0:T(2,128)S(1)} %collective-permute-done.2.back), custom_call_target="tpu_custom_call" | custom-call | bytes 3000000 | tf_op jit(solution)/shard_map/finish/pallas_call | solution.py:611
  32.4 11.5 %all_to_all.5 = f32[8,24,128]{2,1,0:T(8,128)S(1)} all-to-all(f32[8,24,128]{2,1,0:T(8,128)S(1)} %finish.1), channel_id=1, replica_groups={{0,1,2,3,4,5,6,7},{8,9,10,11,12,13,14,15},{16,17,18,19,20,21,22,23},{24..., dimensions={0} | all-to-all | bytes 196608 | tf_op jit(solution)/shard_map/all_to_all | solution.py:663
  43.9 0.6 %reduce_max.9 = f32[24,128]{1,0:T(8,128)} reduce(f32[8,24,128]{2,1,0:T(8,128)S(1)} %all_to_all.5, f32[]{:T(128)} %constant.10.clone.1), dimensions={0}, to_apply=%region_0.0 | reduce | flops 21504 | bytes 110596 | tf_op jit(solution)/shard_map/reduce_max | solution.py:664
Async XLA Ops:
  0.1 6.4 %copy-start = (s32[204,1]{0,1:T(1,128)S(1)}, s32[204,1]{0,1:T(1,128)}, u32[]{:S(2)}) copy-start(s32[204,1]{0,1:T(1,128)} %param.5) | copy-start | bytes 2452
  2.4 19.8 %collective-permute-start = (bf16[528,1024]{1,0:T(8,128)(2,1)S(1)}, bf16[528,1024]{1,0:T(8,128)(2,1)S(1)}, u32[]{:S(2)}, u32[]{:S(2)}) collective-permute-start(bf16[528,1024]{1,0:T(8,128)(2,1)S(1)} %far_rows.1.far), channel_id=1, source_target_pairs={{4,8},{12,16},{20,24},{28,32},{36,40},{44,48},{52,56},{60,64},{68,... | collective-permute-start | bytes 3244040 | tf_op jit(solution)/shard_map/ppermute | solution.py:638
  12.0 13.0 %collective-permute-start.1 = (bf16[1296,1024]{1,0:T(8,128)(2,1)S(1)}, bf16[1296,1024]{1,0:T(8,128)(2,1)S(1)}, u32[]{:S(2)}, u32[]{:S(2)}) collective-permute-start(bf16[1296,1024]{1,0:T(8,128)(2,1)S(1)} %get-tuple-element.24), channel_id=1, source_target_pairs={{0,4},{4,0},{8,12},{12,8},{16,20},{20,16},{24,28},{28,24},{32,36},... | collective-permute-start | bytes 7962632 | tf_op jit(solution)/shard_map/ppermute | solution.py:642
  26.6 5.2 %collective-permute-start.2 = (f32[2,256]{1,0:T(2,128)S(1)}, f32[2,256]{1,0:T(2,128)S(1)}, u32[]{:S(2)}, u32[]{:S(2)}) collective-permute-start(f32[2,256]{1,0:T(2,128)S(1)} %get-tuple-element.28), channel_id=1, source_target_pairs={{4,8},{12,16},{20,24},{28,32},{36,40},{44,48},{52,56},{60,64},{68,... | collective-permute-start | bytes 6152 | tf_op jit(solution)/shard_map/ppermute | solution.py:656

commit v7 on v6

--- a/solution.py
+++ b/solution.py
@@ -13,6 +13,7 @@
 OWN = 12
 REPS = 4
 MOVED = 8
+ROW = 16
 NEAR = 4
 CHIP_SLOTS = 2 + NEAR - 1
 FAR_SLOTS = 2
@@ -509,8 +510,31 @@
         )
 
 
-def bridge_kernel(block_count, place, far_list, stats, found_in, far, chip, returned, other):
+def pairs_chip_early(shard):
+    return lax.rem(shard, ROW) == 0
+
+
+def compare_chip(edge, holder, stats, units, chip, mine, other, row_acc, col_acc, tasks):
+    col_acc[...] = jnp.full(col_acc.shape, -1.0, jnp.float32)
+    row_acc[...] = jnp.full(row_acc.shape, -1.0, jnp.float32)
+    tail = chip[pl.ds(CHIP_SLOTS * BLOCK, TAIL), :]
+    bits = [flag_bits(tail, slot) for slot in range(2)]
+    count = edge.list_tasks(tasks, stats, holder, bits)
+    pad_tasks(tasks, count)
+    run_tasks(tasks, count, chip, units, row_acc, col_acc)
+    mine[...] = jnp.maximum(mine[...], jnp.max(col_acc[...], axis=1))
+    for which in range(2):
+        here = (pl.ds(chip_local(1 - edge.core, edge.near(which)), 1), slice(None))
+        found = as_lanes(jnp.max(row_acc[which], axis=1, keepdims=True))
+        other[here] = jnp.maximum(other[here], found)
+
+
+def bridge_kernel(
+    block_count, place, holder, far_list, stats, found_in, mine_in, units, far, chip,
+    returned, mine, other, row_acc, col_acc, tasks,
+):
     returned[...] = found_in[...]
+    mine[...] = mine_in[...]
     other[...] = jnp.full(other.shape, -1.0, jnp.float32)
 
     @pl.when(far_list[EDGE_TASKS + 1] > 0)
@@ -539,25 +563,23 @@
         best = as_lanes(jnp.max(best, axis=1, keepdims=True))
         returned[0:1, :] = jnp.maximum(returned[0:1, :], best)
 
+    @pl.when(pairs_chip_early(place[0]))
+    def _():
+        edge = Boundary(False, block_count, place)
+        compare_chip(edge, holder, stats, units, chip, mine, other, row_acc, col_acc, tasks)
+
 
 def chip_kernel(
     block_count, place, holder, stats, mine_in, other_in, units, chip,
     mine, other, row_acc, col_acc, tasks,
 ):
-    edge = Boundary(False, block_count, place)
-    col_acc[...] = jnp.full(col_acc.shape, -1.0, jnp.float32)
-    row_acc[...] = jnp.full(row_acc.shape, -1.0, jnp.float32)
-    tail = chip[pl.ds(CHIP_SLOTS * BLOCK, TAIL), :]
-    bits = [flag_bits(tail, slot) for slot in range(2)]
-    count = edge.list_tasks(tasks, stats, holder, bits)
-    pad_tasks(tasks, count)
-    run_tasks(tasks, count, chip, units, row_acc, col_acc)
-    mine[...] = jnp.maximum(mine_in[...], jnp.max(col_acc[...], axis=1))
+    mine[...] = mine_in[...]
     other[...] = other_in[...]
-    for which in range(2):
-        here = (pl.ds(chip_local(1 - edge.core, edge.near(which)), 1), slice(None))
-        found = as_lanes(jnp.max(row_acc[which], axis=1, keepdims=True))
-        other[here] = jnp.maximum(other[here], found)
+
+    @pl.when(jnp.logical_not(pairs_chip_early(place[0])))
+    def _():
+        edge = Boundary(False, block_count, place)
+        compare_chip(edge, holder, stats, units, chip, mine, other, row_acc, col_acc, tasks)
 
 
 BEST = pltpu.VMEM((OWN, BLOCK), jnp.float32)
@@ -649,9 +671,10 @@
         functools.partial(far_kernel, block_count), "far_pairs", cost(4, 10**11),
         (BEST, RETURNED), 2, EDGE_SCRATCH, (place, far_list, mine, units, far_in),
     )
-    returned, other = pair_call(
+    returned, mine, other = pair_call(
         functools.partial(bridge_kernel, block_count), "bridge_pairs", cost(1),
-        (RETURNED, BEST), 3, [], (place, far_list, stats, found, far_in, chip_in),
+        (RETURNED, BEST, BEST), 4, EDGE_SCRATCH,
+        (place, listing, far_list, stats, found, mine, units, far_in, chip_in),
     )
     back = lax.ppermute(returned, "shard", across)
     mine, other = pair_call(

time: 45 us -> 44.7 us (level); the launches traced: 44.5 us -> 44.8 us
  Pallas kernels: 21.3 us -> 16.5 us
  blocking collectives: 11.5 us -> 14.6 us
  starting transfers between devices: 10.1 us -> 12.5 us
    pallas_call x4, Pallas kernels: 12.9 us -> 8.1 us  [pair_call(): pl.pallas_call(kernel, out_shape=outs, in_specs=[SMEM] * scalars + [VMEM]...]
    all_to_all x1, blocking collectives: 11.5 us -> 14.6 us  [shards(): lax.all_to_all(outgoing, ('shard', 'rep'), 0, 0, axis_index_groups=groups)]
    ppermute x1, starting transfers between devices: 1.92 us -> 4.26 us  [shards(): back = lax.ppermute(returned, 'shard', across)]
    ppermute x1, waiting for transfers between devices: 0.85 us -> 0.01 us  [shards(): back = lax.ppermute(returned, 'shard', across)]
    ppermute x1, waiting for transfers between devices: 0.01 us -> 0.47 us  [shards(): far_in = in_vmem(lax.ppermute(far_out, 'shard', across))]
  transfers between devices with their start and end apart: 3 -> 3, of which waited for: 1 -> 1; matrix products, arithmetic and copies ran while one was open for 0% -> 0% of each run, Pallas kernels for 38% -> 29%
where the time goes in v7:
time: 44.7 us; the launch traced here: 44.8 us
  Pallas kernels  16.5 us (37%)
  blocking collectives  14.6 us (33%)
  starting transfers between devices  12.5 us (28%)
  other arithmetic  0.68 us (2%)
  waiting for transfers between devices  0.47 us (1%)
    all_to_all x1, blocking collectives, shards(): lax.all_to_all(outgoing, ('shard', 'rep'), 0, 0, axis_index_groups=groups)  14.6 us
    pallas_call x4, Pallas kernels, pair_call(): pl.pallas_call(kernel, out_shape=outs, in_specs=[SMEM] * scalars + [VMEM]...  8.1 us
    pallas_call x1, Pallas kernels, own_rows(): pl.pallas_call(functools.partial(rows_kernel, block_count), out_shape=(pl...  5.5 us
    ppermute x1, starting transfers between devices, shards(): back = lax.ppermute(returned, 'shard', across)  4.26 us
    ppermute x1, starting transfers between devices, shards(): far_in = in_vmem(lax.ppermute(far_out, 'shard', across))  4.11 us
    ppermute x1, starting transfers between devices, shards(): chip_in = in_vmem(lax.ppermute(chip_out, 'shard', within))  4.09 us
    pallas_call x1, Pallas kernels, far_rows(): pl.pallas_call(far_rows_kernel, out_shape=pltpu.VMEM((FAR_ROWS, WIDTH), j...  2.29 us
  transfers between devices with their start and end apart: 3, of which 1 were waited for; matrix products, arithmetic and copies ran while one was open for 0% of the time, Pallas kernels for 29%

profile of v7, /device:TPU:7, one launch (start us, length us, event | category | flops | bytes accessed | tf_op | source)
XLA Modules:
  0.0 44.8 jit_solution(16452530977543363876)
XLA Ops:
  0.0 0.1 pad_add_fusion.place
  0.1 0.0 copy-start
  0.1 2.3 %far_rows.1.far = bf16[528,1024]{1,0:T(8,128)(2,1)S(1)} custom-call(s32[2]{0:T(128)S(1)} %pad_add_fusion.place, s32[204]{0:T(256)} %bitcast.5, f32[3072,1024]{1,0:T(8,128)} %emb.3), custom_call_target="tpu_custom_call" | custom-call | bytes 3000000 | tf_op jit(solution)/shard_map/far_rows/pallas_call | solution.py:112
  2.4 4.1 %collective-permute-start = (bf16[528,1024]{1,0:T(8,128)(2,1)S(1)}, bf16[528,1024]{1,0:T(8,128)(2,1)S(1)}, u32[]{:S(2)}, u32[]{:S(2)}) collective-permute-start(bf16[528,1024]{1,0:T(8,128)(2,1)S(1)} %far_rows.1.far), channel_id=1, source_target_pairs={{4,8},{12,16},{20,24},{28,32},{36,40},{44,48},{52,56},{60,64},{68,... | collective-permute-start | bytes 3244040 | tf_op jit(solution)/shard_map/ppermute | solution.py:660
  6.5 0.0 copy-done
  6.5 5.5 %own_rows.1 = (bf16[3072,1024]{1,0:T(8,128)(2,1)S(1)}, bf16[1296,1024]{1,0:T(8,128)(2,1)S(1)}, f32[12,256]{1,0:T(8,128)S(1)}, s32[8,128]{1,0:T(8,128)S(1)}) custom-call(s32[2]{0:T(128)S(1)} %pad_add_fusion.place, s32[204]{0:T(256)S(1)} %bitcast.6, s32[1536,128]{1,0:T(8,128)} %bitcast.10, bf16[528,1024]{1,0:T(8,128)(2,1)S(1)} %far_rows.1.far, f32[3072,1024]{1,0:T(8,128)} %emb.3), custom_call_target="tpu_custom_call" | custom-call | bytes 15000000 | tf_op jit(solution)/shard_map/own_rows/pallas_call | solution.py:313
  12.0 4.1 %collective-permute-start.1 = (bf16[1296,1024]{1,0:T(8,128)(2,1)S(1)}, bf16[1296,1024]{1,0:T(8,128)(2,1)S(1)}, u32[]{:S(2)}, u32[]{:S(2)}) collective-permute-start(bf16[1296,1024]{1,0:T(8,128)(2,1)S(1)} %get-tuple-element.25), channel_id=1, source_target_pairs={{0,4},{4,0},{8,12},{12,8},{16,20},{20,16},{24,28},{28,24},{32,36},... | collective-permute-start | bytes 7962632 | tf_op jit(solution)/shard_map/ppermute | solution.py:664
  16.1 3.0 %own_pairs.1 = (f32[12,256]{1,0:T(8,128)S(1)}, s32[290]{0:T(512)S(1)}) custom-call(s32[2]{0:T(128)S(1)} %pad_add_fusion.place, s32[204]{0:T(256)S(1)} %bitcast.7, s32[8,128]{1,0:T(8,128)S(1)} %get-tuple-element.18.stats, f32[12,256]{1,0:T(8,128)S(1)} %get-tuple-element.19.best, bf16[3072,1024]{1,0:T(8,128)(2,1)S(1)} %get-tuple-element.20.units), custom_call_target="tpu_custom_call" | custom-call | bytes 9000000 | tf_op jit(solution)/shard_map/own_pairs/pallas_call | solution.py:591
  19.1 0.5 %collective-permute-done.far = bf16[528,1024]{1,0:T(8,128)(2,1)S(1)} collective-permute-done((bf16[528,1024]{1,0:T(8,128)(2,1)S(1)}, bf16[528,1024]{1,0:T(8,128)(2,1)S(1)}, u32[]{:S(2)}, u32[]{:S(2)}) %collective-permute-start) | collective-permute-done | bytes 1081376 | tf_op jit(solution)/shard_map/ppermute | solution.py:660
  19.6 1.9 %far_pairs.1 = (f32[12,256]{1,0:T(8,128)S(1)}, f32[2,256]{1,0:T(2,128)S(1)}) custom-call(s32[2]{0:T(128)S(1)} %pad_add_fusion.place, s32[290]{0:T(512)S(1)} %get-tuple-element.21.far_list, f32[12,256]{1,0:T(8,128)S(1)} %get-tuple-element.22.best, bf16[3072,1024]{1,0:T(8,128)(2,1)S(1)} %get-tuple-element.20.units, bf16[528,1024]{1,0:T(8,128)(2,1)S(1)} %collective-permute-done.far), custom_call_target="tpu_custom_call" | custom-call | flops 99999997952 | bytes 12000000 | tf_op jit(solution)/shard_map/far_pairs/pallas_call | solution.py:591
  21.5 0.0 collective-permute-done.1.chip
  21.5 0.7 %bridge_pairs.1 = (f32[2,256]{1,0:T(2,128)S(1)}, f32[12,256]{1,0:T(8,128)S(1)}, f32[12,256]{1,0:T(8,128)S(1)}) custom-call(s32[2]{0:T(128)S(1)} %pad_add_fusion.place, s32[204]{0:T(256)S(1)} %bitcast.8, s32[290]{0:T(512)S(1)} %get-tuple-element.21.far_list, s32[8,128]{1,0:T(8,128)S(1)} %get-tuple-element.18.stats, f32[2,256]{1,0:T(2,128)S(1)} %get-tuple-element.23.found_in, ...), custom_call_target="tpu_custom_call" | custom-call | bytes 3000000 | tf_op jit(solution)/shard_map/bridge_pairs/pallas_call | solution.py:591
  22.2 4.3 %collective-permute-start.2 = (f32[2,256]{1,0:T(2,128)S(1)}, f32[2,256]{1,0:T(2,128)S(1)}, u32[]{:S(2)}, u32[]{:S(2)}) collective-permute-start(f32[2,256]{1,0:T(2,128)S(1)} %get-tuple-element.30), channel_id=1, source_target_pairs={{4,8},{12,16},{20,24},{28,32},{36,40},{44,48},{52,56},{60,64},{68,... | collective-permute-start | bytes 6152 | tf_op jit(solution)/shard_map/ppermute | solution.py:679
  26.5 2.5 %chip_pairs.1 = (f32[12,256]{1,0:T(8,128)S(1)}, f32[12,256]{1,0:T(8,128)S(1)}) custom-call(s32[2]{0:T(128)S(1)} %pad_add_fusion.place, s32[204]{0:T(256)S(1)} %bitcast.9, s32[8,128]{1,0:T(8,128)S(1)} %get-tuple-element.18.stats, f32[12,256]{1,0:T(8,128)S(1)} %get-tuple-element.26.mine_in, f32[12,256]{1,0:T(8,128)S(1)} %get-tuple-element.27.other_in, ...), custom_call_target="tpu_custom_call" | custom-call | bytes 12000000 | tf_op jit(solution)/shard_map/chip_pairs/pallas_call | solution.py:591
  29.0 0.0 collective-permute-done.2.back
  29.0 0.6 %finish.1 = f32[8,24,128]{2,1,0:T(8,128)S(1)} custom-call(s32[2]{0:T(128)S(1)} %pad_add_fusion.place, f32[12,256]{1,0:T(8,128)S(1)} %get-tuple-element.28.mine, f32[12,256]{1,0:T(8,128)S(1)} %get-tuple-element.29.other, f32[2,256]{1,0:T(2,128)S(1)} %collective-permute-done.2.back), custom_call_target="tpu_custom_call" | custom-call | bytes 3000000 | tf_op jit(solution)/shard_map/finish/pallas_call | solution.py:633
  29.6 14.6 %all_to_all.5 = f32[8,24,128]{2,1,0:T(8,128)S(1)} all-to-all(f32[8,24,128]{2,1,0:T(8,128)S(1)} %finish.1), channel_id=1, replica_groups={{0,1,2,3,4,5,6,7},{8,9,10,11,12,13,14,15},{16,17,18,19,20,21,22,23},{24..., dimensions={0} | all-to-all | bytes 196608 | tf_op jit(solution)/shard_map/all_to_all | solution.py:686
  44.1 0.6 %reduce_max.9 = f32[24,128]{1,0:T(8,128)} reduce(f32[8,24,128]{2,1,0:T(8,128)S(1)} %all_to_all.5, f32[]{:T(128)} %constant.10.clone.1), dimensions={0}, to_apply=%region_0.0 | reduce | flops 21504 | bytes 110596 | tf_op jit(solution)/shard_map/reduce_max | solution.py:687
Async XLA Ops:
  0.1 6.4 %copy-start = (s32[204,1]{0,1:T(1,128)S(1)}, s32[204,1]{0,1:T(1,128)}, u32[]{:S(2)}) copy-start(s32[204,1]{0,1:T(1,128)} %param.5) | copy-start | bytes 2452
  2.4 17.2 %collective-permute-start = (bf16[528,1024]{1,0:T(8,128)(2,1)S(1)}, bf16[528,1024]{1,0:T(8,128)(2,1)S(1)}, u32[]{:S(2)}, u32[]{:S(2)}) collective-permute-start(bf16[528,1024]{1,0:T(8,128)(2,1)S(1)} %far_rows.1.far), channel_id=1, source_target_pairs={{4,8},{12,16},{20,24},{28,32},{36,40},{44,48},{52,56},{60,64},{68,... | collective-permute-start | bytes 3244040 | tf_op jit(solution)/shard_map/ppermute | solution.py:660
  12.0 9.5 %collective-permute-start.1 = (bf16[1296,1024]{1,0:T(8,128)(2,1)S(1)}, bf16[1296,1024]{1,0:T(8,128)(2,1)S(1)}, u32[]{:S(2)}, u32[]{:S(2)}) collective-permute-start(bf16[1296,1024]{1,0:T(8,128)(2,1)S(1)} %get-tuple-element.25), channel_id=1, source_target_pairs={{0,4},{4,0},{8,12},{12,8},{16,20},{20,16},{24,28},{28,24},{32,36},... | collective-permute-start | bytes 7962632 | tf_op jit(solution)/shard_map/ppermute | solution.py:664
  22.2 6.8 %collective-permute-start.2 = (f32[2,256]{1,0:T(2,128)S(1)}, f32[2,256]{1,0:T(2,128)S(1)}, u32[]{:S(2)}, u32[]{:S(2)}) collective-permute-start(f32[2,256]{1,0:T(2,128)S(1)} %get-tuple-element.30), channel_id=1, source_target_pairs={{4,8},{12,16},{20,24},{28,32},{36,40},{44,48},{52,56},{60,64},{68,... | collective-permute-start | bytes 6152 | tf_op jit(solution)/shard_map/ppermute | solution.py:679

commit v8 on v6

--- a/solution.py
+++ b/solution.py
@@ -495,18 +495,23 @@
 def far_kernel(
     block_count, place, far_list, best, units, far, mine, returned, row_acc, col_acc, tasks
 ):
-    edge = Boundary(True, block_count, place)
-    col_acc[...] = jnp.full(col_acc.shape, -1.0, jnp.float32)
-    row_acc[...] = jnp.full(row_acc.shape, -1.0, jnp.float32)
-    tail = far[pl.ds(FAR_SLOTS * BLOCK, TAIL), :]
-    bits = [flag_bits(tail, slot) for slot in range(2)]
-    count = edge.keep_listed(far_list, tasks, bits)
-    run_tasks(tasks, count, far, units, row_acc, col_acc)
-    mine[...] = jnp.maximum(best[...], jnp.max(col_acc[...], axis=1))
-    for which in range(2):
-        returned[which : which + 1, :] = as_lanes(
-            jnp.max(row_acc[which], axis=1, keepdims=True)
-        )
+    mine[...] = best[...]
+    returned[...] = jnp.full(returned.shape, -1.0, jnp.float32)
+
+    @pl.when(far_list[EDGE_TASKS] > 0)
+    def _():
+        edge = Boundary(True, block_count, place)
+        col_acc[...] = jnp.full(col_acc.shape, -1.0, jnp.float32)
+        row_acc[...] = jnp.full(row_acc.shape, -1.0, jnp.float32)
+        tail = far[pl.ds(FAR_SLOTS * BLOCK, TAIL), :]
+        bits = [flag_bits(tail, slot) for slot in range(2)]
+        count = edge.keep_listed(far_list, tasks, bits)
+        run_tasks(tasks, count, far, units, row_acc, col_acc)
+        mine[...] = jnp.maximum(best[...], jnp.max(col_acc[...], axis=1))
+        for which in range(2):
+            returned[which : which + 1, :] = as_lanes(
+                jnp.max(row_acc[which], axis=1, keepdims=True)
+            )
 
 
 def bridge_kernel(block_count, place, far_list, stats, found_in, far, chip, returned, other):
@@ -661,7 +666,8 @@
     outgoing = finish(block_count, place, mine, other, back)
     groups = [list(range(c * 2 * REPS, (c + 1) * 2 * REPS)) for c in range(count // 2)]
     parts = lax.all_to_all(outgoing, ("shard", "rep"), 0, 0, axis_index_groups=groups)
-    return jnp.max(parts, axis=0).reshape(OWN * BLOCK)
+    best = functools.reduce(jnp.maximum, [parts[i] for i in range(2 * REPS)])
+    return best.reshape(OWN * BLOCK)
 
 
 def solution(mesh):

time: 45 us -> 44.9 us (level)
  Pallas kernels: 21.3 us -> 18.4 us
  blocking collectives: 11.5 us -> 14.3 us
  waiting for transfers between devices: 0.86 us -> 0.01 us
  starting transfers between devices: 10.1 us -> 10.9 us
    pallas_call x4, Pallas kernels: 12.9 us -> 10 us  [pair_call(): pl.pallas_call(kernel, out_shape=outs, in_specs=[SMEM] * scalars + [VMEM]...]
    all_to_all x1, blocking collectives: 11.5 us -> 14.3 us  [shards(): lax.all_to_all(outgoing, ('shard', 'rep'), 0, 0, axis_index_groups=groups)]
    ppermute x1, waiting for transfers between devices: 0.85 us -> 0.01 us  [shards(): back = lax.ppermute(returned, 'shard', across)]
    ppermute x1, starting transfers between devices: 1.92 us -> 2.72 us  [shards(): back = lax.ppermute(returned, 'shard', across)]
    reduce_max x1 -> x0, other arithmetic: 0.61 us -> none  [shards(): return jnp.max(parts, axis=0).reshape(OWN * BLOCK)]
    max x0 -> x1, other arithmetic: none -> 0.61 us  [shards(): best = functools.reduce(jnp.maximum, [parts[i] for i in range(2 * REPS)])]
  transfers between devices with their start and end apart: 3 -> 3, of which waited for: 1 -> 0; matrix products, arithmetic and copies ran while one was open for 0% -> 0% of each run, Pallas kernels for 38% -> 34%
where the time goes in v8:
time: 44.9 us; the launch traced here: 44.4 us
  Pallas kernels  18.4 us (41%)
  blocking collectives  14.3 us (32%)
  starting transfers between devices  10.9 us (24%)
  other arithmetic  0.68 us (2%)
    all_to_all x1, blocking collectives, shards(): lax.all_to_all(outgoing, ('shard', 'rep'), 0, 0, axis_index_groups=groups)  14.3 us
    pallas_call x4, Pallas kernels, pair_call(): pl.pallas_call(kernel, out_shape=outs, in_specs=[SMEM] * scalars + [VMEM]...  10 us
    pallas_call x1, Pallas kernels, own_rows(): pl.pallas_call(functools.partial(rows_kernel, block_count), out_shape=(pl...  5.5 us
    ppermute x1, starting transfers between devices, shards(): far_in = in_vmem(lax.ppermute(far_out, 'shard', across))  4.11 us
    ppermute x1, starting transfers between devices, shards(): chip_in = in_vmem(lax.ppermute(chip_out, 'shard', within))  4.09 us
    ppermute x1, starting transfers between devices, shards(): back = lax.ppermute(returned, 'shard', across)  2.72 us
    pallas_call x1, Pallas kernels, far_rows(): pl.pallas_call(far_rows_kernel, out_shape=pltpu.VMEM((FAR_ROWS, WIDTH), j...  2.29 us
  transfers between devices with their start and end apart: 3, of which 0 were waited for; matrix products, arithmetic and copies ran while one was open for 0% of the time, Pallas kernels for 34%

profile of v8, /device:TPU:7, one launch (start us, length us, event | category | flops | bytes accessed | tf_op | source)
XLA Modules:
  0.0 44.4 jit_solution(2269185607479986431)
XLA Ops:
  0.0 0.1 pad_add_fusion.place
  0.1 0.0 copy-start
  0.1 2.3 %far_rows.1.far = bf16[528,1024]{1,0:T(8,128)(2,1)S(1)} custom-call(s32[2]{0:T(128)S(1)} %pad_add_fusion.place, s32[204]{0:T(256)} %bitcast.6, f32[3072,1024]{1,0:T(8,128)} %emb.3), custom_call_target="tpu_custom_call" | custom-call | bytes 3000000 | tf_op jit(solution)/shard_map/far_rows/pallas_call | solution.py:111
  2.4 4.1 %collective-permute-start = (bf16[528,1024]{1,0:T(8,128)(2,1)S(1)}, bf16[528,1024]{1,0:T(8,128)(2,1)S(1)}, u32[]{:S(2)}, u32[]{:S(2)}) collective-permute-start(bf16[528,1024]{1,0:T(8,128)(2,1)S(1)} %far_rows.1.far), channel_id=1, source_target_pairs={{4,8},{12,16},{20,24},{28,32},{36,40},{44,48},{52,56},{60,64},{68,... | collective-permute-start | bytes 3244040 | tf_op jit(solution)/shard_map/ppermute | solution.py:643
  6.5 0.0 copy-done
  6.5 5.5 %own_rows.1 = (bf16[3072,1024]{1,0:T(8,128)(2,1)S(1)}, bf16[1296,1024]{1,0:T(8,128)(2,1)S(1)}, f32[12,256]{1,0:T(8,128)S(1)}, s32[8,128]{1,0:T(8,128)S(1)}) custom-call(s32[2]{0:T(128)S(1)} %pad_add_fusion.place, s32[204]{0:T(256)S(1)} %bitcast.7, s32[1536,128]{1,0:T(8,128)} %bitcast.10, bf16[528,1024]{1,0:T(8,128)(2,1)S(1)} %far_rows.1.far, f32[3072,1024]{1,0:T(8,128)} %emb.3), custom_call_target="tpu_custom_call" | custom-call | bytes 15000000 | tf_op jit(solution)/shard_map/own_rows/pallas_call | solution.py:312
  12.0 4.1 %collective-permute-start.1 = (bf16[1296,1024]{1,0:T(8,128)(2,1)S(1)}, bf16[1296,1024]{1,0:T(8,128)(2,1)S(1)}, u32[]{:S(2)}, u32[]{:S(2)}) collective-permute-start(bf16[1296,1024]{1,0:T(8,128)(2,1)S(1)} %get-tuple-element.24), channel_id=1, source_target_pairs={{0,4},{4,0},{8,12},{12,8},{16,20},{20,16},{24,28},{28,24},{32,36},... | collective-permute-start | bytes 7962632 | tf_op jit(solution)/shard_map/ppermute | solution.py:647
  16.1 5.1 %own_pairs.1 = (f32[12,256]{1,0:T(8,128)S(1)}, s32[290]{0:T(512)S(1)}) custom-call(s32[2]{0:T(128)S(1)} %pad_add_fusion.place, s32[204]{0:T(256)S(1)} %bitcast.8, s32[8,128]{1,0:T(8,128)S(1)} %get-tuple-element.17.stats, f32[12,256]{1,0:T(8,128)S(1)} %get-tuple-element.18.best, bf16[3072,1024]{1,0:T(8,128)(2,1)S(1)} %get-tuple-element.19.units), custom_call_target="tpu_custom_call" | custom-call | bytes 9000000 | tf_op jit(solution)/shard_map/own_pairs/pallas_call | solution.py:574
  21.3 0.0 collective-permute-done.far
  21.3 1.9 %far_pairs.1 = (f32[12,256]{1,0:T(8,128)S(1)}, f32[2,256]{1,0:T(2,128)S(1)}) custom-call(s32[2]{0:T(128)S(1)} %pad_add_fusion.place, s32[290]{0:T(512)S(1)} %get-tuple-element.20.far_list, f32[12,256]{1,0:T(8,128)S(1)} %get-tuple-element.21.best, bf16[3072,1024]{1,0:T(8,128)(2,1)S(1)} %get-tuple-element.19.units, bf16[528,1024]{1,0:T(8,128)(2,1)S(1)} %collective-permute-done.far), custom_call_target="tpu_custom_call" | custom-call | flops 99999997952 | bytes 12000000 | tf_op jit(solution)/shard_map/far_pairs/pallas_call | solution.py:574
  23.2 0.0 collective-permute-done.1.chip
  23.2 0.6 %bridge_pairs.1 = (f32[2,256]{1,0:T(2,128)S(1)}, f32[12,256]{1,0:T(8,128)S(1)}) custom-call(s32[2]{0:T(128)S(1)} %pad_add_fusion.place, s32[290]{0:T(512)S(1)} %get-tuple-element.20.far_list, s32[8,128]{1,0:T(8,128)S(1)} %get-tuple-element.17.stats, f32[2,256]{1,0:T(2,128)S(1)} %get-tuple-element.23.found_in, ...), custom_call_target="tpu_custom_call" | custom-call | bytes 3000000 | tf_op jit(solution)/shard_map/bridge_pairs/pallas_call | solution.py:574
  23.9 2.7 %collective-permute-start.2 = (f32[2,256]{1,0:T(2,128)S(1)}, f32[2,256]{1,0:T(2,128)S(1)}, u32[]{:S(2)}, u32[]{:S(2)}) collective-permute-start(f32[2,256]{1,0:T(2,128)S(1)} %get-tuple-element.28), channel_id=1, source_target_pairs={{4,8},{12,16},{20,24},{28,32},{36,40},{44,48},{52,56},{60,64},{68,... | collective-permute-start | bytes 6152 | tf_op jit(solution)/shard_map/ppermute | solution.py:661
  26.6 2.3 %chip_pairs.1 = (f32[12,256]{1,0:T(8,128)S(1)}, f32[12,256]{1,0:T(8,128)S(1)}) custom-call(s32[2]{0:T(128)S(1)} %pad_add_fusion.place, s32[204]{0:T(256)S(1)} %bitcast.9, s32[8,128]{1,0:T(8,128)S(1)} %get-tuple-element.17.stats, f32[12,256]{1,0:T(8,128)S(1)} %get-tuple-element.22.mine_in, f32[12,256]{1,0:T(8,128)S(1)} %get-tuple-element.25.other_in, ...), custom_call_target="tpu_custom_call" | custom-call | bytes 12000000 | tf_op jit(solution)/shard_map/chip_pairs/pallas_call | solution.py:574
  28.9 0.0 collective-permute-done.2.back
  28.9 0.6 %finish.1 = f32[8,24,128]{2,1,0:T(8,128)S(1)} custom-call(s32[2]{0:T(128)S(1)} %pad_add_fusion.place, f32[12,256]{1,0:T(8,128)S(1)} %get-tuple-element.26.mine, f32[12,256]{1,0:T(8,128)S(1)} %get-tuple-element.27.other, f32[2,256]{1,0:T(2,128)S(1)} %collective-permute-done.2.back), custom_call_target="tpu_custom_call" | custom-call | bytes 3000000 | tf_op jit(solution)/shard_map/finish/pallas_call | solution.py:616
  29.5 14.3 %all_to_all.5 = f32[8,24,128]{2,1,0:T(8,128)S(1)} all-to-all(f32[8,24,128]{2,1,0:T(8,128)S(1)} %finish.1), channel_id=1, replica_groups={{0,1,2,3,4,5,6,7},{8,9,10,11,12,13,14,15},{16,17,18,19,20,21,22,23},{24..., dimensions={0} | all-to-all | bytes 196608 | tf_op jit(solution)/shard_map/all_to_all | solution.py:668
  43.8 0.6 %fusion = f32[3072]{0:T(1024)} fusion(f32[8,24,128]{2,1,0:T(8,128)S(1)} %all_to_all.5), kind=kLoop, calls=%fused_computation.1 | loop fusion | flops 21504 | bytes 110592 | tf_op jit(solution)/shard_map/max | solution.py:669
Async XLA Ops:
  0.1 6.4 %copy-start = (s32[204,1]{0,1:T(1,128)S(1)}, s32[204,1]{0,1:T(1,128)}, u32[]{:S(2)}) copy-start(s32[204,1]{0,1:T(1,128)} %param.5) | copy-start | bytes 2452
  2.4 18.9 %collective-permute-start = (bf16[528,1024]{1,0:T(8,128)(2,1)S(1)}, bf16[528,1024]{1,0:T(8,128)(2,1)S(1)}, u32[]{:S(2)}, u32[]{:S(2)}) collective-permute-start(bf16[528,1024]{1,0:T(8,128)(2,1)S(1)} %far_rows.1.far), channel_id=1, source_target_pairs={{4,8},{12,16},{20,24},{28,32},{36,40},{44,48},{52,56},{60,64},{68,... | collective-permute-start | bytes 3244040 | tf_op jit(solution)/shard_map/ppermute | solution.py:643
  12.0 11.2 %collective-permute-start.1 = (bf16[1296,1024]{1,0:T(8,128)(2,1)S(1)}, bf16[1296,1024]{1,0:T(8,128)(2,1)S(1)}, u32[]{:S(2)}, u32[]{:S(2)}) collective-permute-start(bf16[1296,1024]{1,0:T(8,128)(2,1)S(1)} %get-tuple-element.24), channel_id=1, source_target_pairs={{0,4},{4,0},{8,12},{12,8},{16,20},{20,16},{24,28},{28,24},{32,36},... | collective-permute-start | bytes 7962632 | tf_op jit(solution)/shard_map/ppermute | solution.py:647
  23.9 5.1 %collective-permute-start.2 = (f32[2,256]{1,0:T(2,128)S(1)}, f32[2,256]{1,0:T(2,128)S(1)}, u32[]{:S(2)}, u32[]{:S(2)}) collective-permute-start(f32[2,256]{1,0:T(2,128)S(1)} %get-tuple-element.28), channel_id=1, source_target_pairs={{4,8},{12,16},{20,24},{28,32},{36,40},{44,48},{52,56},{60,64},{68,... | collective-permute-start | bytes 6152 | tf_op jit(solution)/shard_map/ppermute | solution.py:661

commit v9 on v6

--- a/solution.py
+++ b/solution.py
@@ -449,7 +449,8 @@
 
 
 def own_kernel(
-    block_count, place, holder, stats, best, units, mine, far_list, row_acc, col_acc, tasks
+    block_count, place, holder, stats, best, units, mine, far_list, chip_list,
+    row_acc, col_acc, tasks,
 ):
     col_acc[...] = jnp.full(col_acc.shape, -1.0, jnp.float32)
     row_acc[...] = jnp.full(row_acc.shape, -1.0, jnp.float32)
@@ -487,6 +488,8 @@
         mine[here] = jnp.maximum(mine[here], found)
     edge = Boundary(True, block_count, place)
     far_list[EDGE_TASKS] = edge.list_tasks(far_list, stats, holder)
+    near = Boundary(False, block_count, place)
+    chip_list[EDGE_TASKS] = near.list_tasks(chip_list, stats, holder)
     moved = edge.start(stats, 0)
     bridged = moved[2] & edge.shares(stats, moved, OWN + 1)
     far_list[EDGE_TASKS + 1] = bridged.astype(jnp.int32)
@@ -541,7 +544,7 @@
 
 
 def chip_kernel(
-    block_count, place, holder, stats, mine_in, other_in, units, chip,
+    block_count, place, chip_list, mine_in, other_in, units, chip,
     mine, other, row_acc, col_acc, tasks,
 ):
     edge = Boundary(False, block_count, place)
@@ -549,8 +552,7 @@
     row_acc[...] = jnp.full(row_acc.shape, -1.0, jnp.float32)
     tail = chip[pl.ds(CHIP_SLOTS * BLOCK, TAIL), :]
     bits = [flag_bits(tail, slot) for slot in range(2)]
-    count = edge.list_tasks(tasks, stats, holder, bits)
-    pad_tasks(tasks, count)
+    count = edge.keep_listed(chip_list, tasks, bits)
     run_tasks(tasks, count, chip, units, row_acc, col_acc)
     mine[...] = jnp.maximum(mine_in[...], jnp.max(col_acc[...], axis=1))
     other[...] = other_in[...]
@@ -641,8 +643,8 @@
     )
     chip_in = in_vmem(lax.ppermute(chip_out, "shard", within))
 
-    mine, far_list = pair_call(
-        functools.partial(own_kernel, block_count), "own_pairs", cost(3), (BEST, LIST),
+    mine, far_list, chip_list = pair_call(
+        functools.partial(own_kernel, block_count), "own_pairs", cost(3), (BEST, LIST, LIST),
         3, OWN_SCRATCH, (place, listing, stats, best, units),
     )
     mine, found = pair_call(
@@ -656,7 +658,7 @@
     back = lax.ppermute(returned, "shard", across)
     mine, other = pair_call(
         functools.partial(chip_kernel, block_count), "chip_pairs", cost(4), (BEST, BEST),
-        3, EDGE_SCRATCH, (place, listing, stats, mine, other, units, chip_in),
+        2, EDGE_SCRATCH, (place, chip_list, mine, other, units, chip_in),
     )
     outgoing = finish(block_count, place, mine, other, back)
     groups = [list(range(c * 2 * REPS, (c + 1) * 2 * REPS)) for c in range(count // 2)]

time: 45 us -> 44.8 us (level); the launches traced: 44.5 us -> 45 us
  Pallas kernels: 21.3 us -> 14.9 us
  blocking collectives: 11.5 us -> 16.3 us
  starting transfers between devices: 10.1 us -> 12.4 us
    pallas_call x4, Pallas kernels: 12.9 us -> 6.51 us  [pair_call(): pl.pallas_call(kernel, out_shape=outs, in_specs=[SMEM] * scalars + [VMEM]...]
    all_to_all x1, blocking collectives: 11.5 us -> 16.3 us  [shards(): lax.all_to_all(outgoing, ('shard', 'rep'), 0, 0, axis_index_groups=groups)]
    ppermute x1, starting transfers between devices: 1.92 us -> 4.19 us  [shards(): back = lax.ppermute(returned, 'shard', across)]
    ppermute x1, waiting for transfers between devices: 0.85 us -> 0.01 us  [shards(): back = lax.ppermute(returned, 'shard', across)]
  transfers between devices with their start and end apart: 3 -> 3, of which waited for: 1 -> 2; matrix products, arithmetic and copies ran while one was open for 0% -> 0% of each run, Pallas kernels for 38% -> 25%
where the time goes in v9:
time: 44.8 us; the launch traced here: 45 us
  blocking collectives  16.3 us (36%)
  Pallas kernels  14.9 us (33%)
  starting transfers between devices  12.4 us (28%)
  other arithmetic  0.68 us (2%)
  waiting for transfers between devices  0.63 us (1%)
    all_to_all x1, blocking collectives, shards(): lax.all_to_all(outgoing, ('shard', 'rep'), 0, 0, axis_index_groups=groups)  16.3 us
    pallas_call x4, Pallas kernels, pair_call(): pl.pallas_call(kernel, out_shape=outs, in_specs=[SMEM] * scalars + [VMEM]...  6.51 us
    pallas_call x1, Pallas kernels, own_rows(): pl.pallas_call(functools.partial(rows_kernel, block_count), out_shape=(pl...  5.5 us
    ppermute x1, starting transfers between devices, shards(): back = lax.ppermute(returned, 'shard', across)  4.19 us
    ppermute x1, starting transfers between devices, shards(): far_in = in_vmem(lax.ppermute(far_out, 'shard', across))  4.11 us
    ppermute x1, starting transfers between devices, shards(): chip_in = in_vmem(lax.ppermute(chip_out, 'shard', within))  4.09 us
    pallas_call x1, Pallas kernels, far_rows(): pl.pallas_call(far_rows_kernel, out_shape=pltpu.VMEM((FAR_ROWS, WIDTH), j...  2.29 us
  transfers between devices with their start and end apart: 3, of which 2 were waited for; matrix products, arithmetic and copies ran while one was open for 0% of the time, Pallas kernels for 25%

profile of v9, /device:TPU:7, one launch (start us, length us, event | category | flops | bytes accessed | tf_op | source)
XLA Modules:
  0.0 45.0 jit_solution(14554941319948689556)
XLA Ops:
  0.0 0.1 pad_add_fusion.place
  0.1 0.0 copy-start
  0.1 2.3 %far_rows.1.far = bf16[528,1024]{1,0:T(8,128)(2,1)S(1)} custom-call(s32[2]{0:T(128)S(1)} %pad_add_fusion.place, s32[204]{0:T(256)} %bitcast.5, f32[3072,1024]{1,0:T(8,128)} %emb.3), custom_call_target="tpu_custom_call" | custom-call | bytes 3000000 | tf_op jit(solution)/shard_map/far_rows/pallas_call | solution.py:111
  2.4 4.1 %collective-permute-start = (bf16[528,1024]{1,0:T(8,128)(2,1)S(1)}, bf16[528,1024]{1,0:T(8,128)(2,1)S(1)}, u32[]{:S(2)}, u32[]{:S(2)}) collective-permute-start(bf16[528,1024]{1,0:T(8,128)(2,1)S(1)} %far_rows.1.far), channel_id=1, source_target_pairs={{4,8},{12,16},{20,24},{28,32},{36,40},{44,48},{52,56},{60,64},{68,... | collective-permute-start | bytes 3244040 | tf_op jit(solution)/shard_map/ppermute | solution.py:640
  6.5 0.0 copy-done
  6.5 5.5 %own_rows.1 = (bf16[3072,1024]{1,0:T(8,128)(2,1)S(1)}, bf16[1296,1024]{1,0:T(8,128)(2,1)S(1)}, f32[12,256]{1,0:T(8,128)S(1)}, s32[8,128]{1,0:T(8,128)S(1)}) custom-call(s32[2]{0:T(128)S(1)} %pad_add_fusion.place, s32[204]{0:T(256)S(1)} %bitcast.6, s32[1536,128]{1,0:T(8,128)} %bitcast.8, bf16[528,1024]{1,0:T(8,128)(2,1)S(1)} %far_rows.1.far, f32[3072,1024]{1,0:T(8,128)} %emb.3), custom_call_target="tpu_custom_call" | custom-call | bytes 15000000 | tf_op jit(solution)/shard_map/own_rows/pallas_call | solution.py:312
  12.0 4.1 %collective-permute-start.1 = (bf16[1296,1024]{1,0:T(8,128)(2,1)S(1)}, bf16[1296,1024]{1,0:T(8,128)(2,1)S(1)}, u32[]{:S(2)}, u32[]{:S(2)}) collective-permute-start(bf16[1296,1024]{1,0:T(8,128)(2,1)S(1)} %get-tuple-element.26), channel_id=1, source_target_pairs={{0,4},{4,0},{8,12},{12,8},{16,20},{20,16},{24,28},{28,24},{32,36},... | collective-permute-start | bytes 7962632 | tf_op jit(solution)/shard_map/ppermute | solution.py:644
  16.1 3.1 %own_pairs.1 = (f32[12,256]{1,0:T(8,128)S(1)}, s32[290]{0:T(512)S(1)}, s32[290]{0:T(512)S(1)}) custom-call(s32[2]{0:T(128)S(1)} %pad_add_fusion.place, s32[204]{0:T(256)S(1)} %bitcast.7, s32[8,128]{1,0:T(8,128)S(1)} %get-tuple-element.18.stats, f32[12,256]{1,0:T(8,128)S(1)} %get-tuple-element.19.best, bf16[3072,1024]{1,0:T(8,128)(2,1)S(1)} %get-tuple-element.20.units), custom_call_target="tpu_custom_call" | custom-call | bytes 9000000 | tf_op jit(solution)/shard_map/own_pairs/pallas_call | solution.py:571
  19.2 0.4 collective-permute-done.far
  19.6 0.9 %far_pairs.1 = (f32[12,256]{1,0:T(8,128)S(1)}, f32[2,256]{1,0:T(2,128)S(1)}) custom-call(s32[2]{0:T(128)S(1)} %pad_add_fusion.place, s32[290]{0:T(512)S(1)} %get-tuple-element.22.far_list, f32[12,256]{1,0:T(8,128)S(1)} %get-tuple-element.23.best, bf16[3072,1024]{1,0:T(8,128)(2,1)S(1)} %get-tuple-element.20.units, bf16[528,1024]{1,0:T(8,128)(2,1)S(1)} %collective-permute-done.far), custom_call_target="tpu_custom_call" | custom-call | flops 99999997952 | bytes 12000000 | tf_op jit(solution)/shard_map/far_pairs/pallas_call | solution.py:571
  20.5 0.2 collective-permute-done.1.chip
  20.7 0.6 %bridge_pairs.1 = (f32[2,256]{1,0:T(2,128)S(1)}, f32[12,256]{1,0:T(8,128)S(1)}) custom-call(s32[2]{0:T(128)S(1)} %pad_add_fusion.place, s32[290]{0:T(512)S(1)} %get-tuple-element.22.far_list, s32[8,128]{1,0:T(8,128)S(1)} %get-tuple-element.18.stats, f32[2,256]{1,0:T(2,128)S(1)} %get-tuple-element.25.found_in, ...), custom_call_target="tpu_custom_call" | custom-call | bytes 3000000 | tf_op jit(solution)/shard_map/bridge_pairs/pallas_call | solution.py:571
  21.3 4.2 %collective-permute-start.2 = (f32[2,256]{1,0:T(2,128)S(1)}, f32[2,256]{1,0:T(2,128)S(1)}, u32[]{:S(2)}, u32[]{:S(2)}) collective-permute-start(f32[2,256]{1,0:T(2,128)S(1)} %get-tuple-element.30), channel_id=1, source_target_pairs={{4,8},{12,16},{20,24},{28,32},{36,40},{44,48},{52,56},{60,64},{68,... | collective-permute-start | bytes 6152 | tf_op jit(solution)/shard_map/ppermute | solution.py:658
  25.5 1.9 %chip_pairs.1 = (f32[12,256]{1,0:T(8,128)S(1)}, f32[12,256]{1,0:T(8,128)S(1)}) custom-call(s32[2]{0:T(128)S(1)} %pad_add_fusion.place, s32[290]{0:T(512)S(1)} %get-tuple-element.21.chip_list, f32[12,256]{1,0:T(8,128)S(1)} %get-tuple-element.24.mine_in, f32[12,256]{1,0:T(8,128)S(1)} %get-tuple-element.27.other_in, ...), custom_call_target="tpu_custom_call" | custom-call | bytes 12000000 | tf_op jit(solution)/shard_map/chip_pairs/pallas_call | solution.py:571
  27.5 0.0 collective-permute-done.2.back
  27.5 0.6 %finish.1 = f32[8,24,128]{2,1,0:T(8,128)S(1)} custom-call(s32[2]{0:T(128)S(1)} %pad_add_fusion.place, f32[12,256]{1,0:T(8,128)S(1)} %get-tuple-element.28.mine, f32[12,256]{1,0:T(8,128)S(1)} %get-tuple-element.29.other, f32[2,256]{1,0:T(2,128)S(1)} %collective-permute-done.2.back), custom_call_target="tpu_custom_call" | custom-call | bytes 3000000 | tf_op jit(solution)/shard_map/finish/pallas_call | solution.py:613
  28.1 16.3 %all_to_all.5 = f32[8,24,128]{2,1,0:T(8,128)S(1)} all-to-all(f32[8,24,128]{2,1,0:T(8,128)S(1)} %finish.1), channel_id=1, replica_groups={{0,1,2,3,4,5,6,7},{8,9,10,11,12,13,14,15},{16,17,18,19,20,21,22,23},{24..., dimensions={0} | all-to-all | bytes 196608 | tf_op jit(solution)/shard_map/all_to_all | solution.py:665
  44.4 0.6 %reduce_max.9 = f32[24,128]{1,0:T(8,128)} reduce(f32[8,24,128]{2,1,0:T(8,128)S(1)} %all_to_all.5, f32[]{:T(128)} %constant.10.clone.1), dimensions={0}, to_apply=%region_0.0 | reduce | flops 21504 | bytes 110596 | tf_op jit(solution)/shard_map/reduce_max | solution.py:666
Async XLA Ops:
  0.1 6.4 %copy-start = (s32[204,1]{0,1:T(1,128)S(1)}, s32[204,1]{0,1:T(1,128)}, u32[]{:S(2)}) copy-start(s32[204,1]{0,1:T(1,128)} %param.5) | copy-start | bytes 2452
  2.4 17.2 %collective-permute-start = (bf16[528,1024]{1,0:T(8,128)(2,1)S(1)}, bf16[528,1024]{1,0:T(8,128)(2,1)S(1)}, u32[]{:S(2)}, u32[]{:S(2)}) collective-permute-start(bf16[528,1024]{1,0:T(8,128)(2,1)S(1)} %far_rows.1.far), channel_id=1, source_target_pairs={{4,8},{12,16},{20,24},{28,32},{36,40},{44,48},{52,56},{60,64},{68,... | collective-permute-start | bytes 3244040 | tf_op jit(solution)/shard_map/ppermute | solution.py:640
  12.0 8.7 %collective-permute-start.1 = (bf16[1296,1024]{1,0:T(8,128)(2,1)S(1)}, bf16[1296,1024]{1,0:T(8,128)(2,1)S(1)}, u32[]{:S(2)}, u32[]{:S(2)}) collective-permute-start(bf16[1296,1024]{1,0:T(8,128)(2,1)S(1)} %get-tuple-element.26), channel_id=1, source_target_pairs={{0,4},{4,0},{8,12},{12,8},{16,20},{20,16},{24,28},{28,24},{32,36},... | collective-permute-start | bytes 7962632 | tf_op jit(solution)/shard_map/ppermute | solution.py:644
  21.3 6.1 %collective-permute-start.2 = (f32[2,256]{1,0:T(2,128)S(1)}, f32[2,256]{1,0:T(2,128)S(1)}, u32[]{:S(2)}, u32[]{:S(2)}) collective-permute-start(f32[2,256]{1,0:T(2,128)S(1)} %get-tuple-element.30), channel_id=1, source_target_pairs={{4,8},{12,16},{20,24},{28,32},{36,40},{44,48},{52,56},{60,64},{68,... | collective-permute-start | bytes 6152 | tf_op jit(solution)/shard_map/ppermute | solution.py:658
